TPU v7x, 32 devices: a whole 2x2x4 slice. The times are simulated.
32 devices in a mesh: tile: 8 (over y, x, core), lev: 4 (over z).
Axes of the slice: x: 2, y: 2, z: 4, core: 2. Of those that a mesh axis runs over, the one named last changes fastest.
Arguments:
- tracers: float32 [8, 8, 8, 72, 128], P('tile', None, None, 'lev'), may hold values from -6 to 6
- courant_first: float32 [8, 8, 8, 72], P('tile', None, None, 'lev'), may hold values from -0.9 to 0.9
- courant_second: float32 [8, 8, 8, 72], P('tile', None, None, 'lev'), may hold values from -0.9 to 0.9
- weights: float32 [8, 8, 8, 72, 72], P('tile', 'lev'), may hold values from 0.05 to 1
- frame_flip: int32 [8, 2], P('tile'), may hold values from 0 to 1
Outputs:
- transported: float32 [8, 8, 8, 72, 128], P('tile', None, None, 'lev')
All inputs are finite; a program needn't handle non-finite values.
Results may differ from a plain program's by a relative error of at most 0.0003.
Values sent between devices are 32-bit elements; how exact they have to be, the bound alone decides.
No kernel may reach another device: no remote copies, remote signals or barrier semaphores. Data moves between devices by JAX's collectives and lax.ppermute only.
A program may use at most 64 MiB of HBM per device.

v0:
```python
import jax
import jax.numpy as jnp
from jax import lax
from jax.sharding import PartitionSpec as P

SUBSTEPS = 3


def passed_along(value, axis, steps):
    count = lax.axis_size(axis)
    pairs = [(source, (source + steps) % count) for source in range(count)]
    return lax.ppermute(value, axis, pairs)


def ppm_update(extended, courant, along):
    length = extended.shape[along] - 6

    def window(values, offset, amount):
        return lax.slice_in_dim(values, offset, offset + amount, axis=along)

    interfaces = (
        7.0 * (window(extended, 1, length + 3) + window(extended, 2, length + 3))
        - (window(extended, 0, length + 3) + window(extended, 3, length + 3))
    ) / 12.0
    low_edge = window(interfaces, 0, length + 2)
    high_edge = window(interfaces, 1, length + 2)
    centre = window(extended, 2, length + 2)
    gradient = high_edge - low_edge
    curvature = 6.0 * centre - 3.0 * (low_edge + high_edge)
    upward = courant * (
        window(high_edge, 0, length + 1)
        - 0.5
        * courant
        * (
            window(gradient, 0, length + 1)
            - (1.0 - courant * (2.0 / 3.0)) * window(curvature, 0, length + 1)
        )
    )
    downward = courant * (
        window(low_edge, 1, length + 1)
        - 0.5
        * courant
        * (
            window(gradient, 1, length + 1)
            + (1.0 + courant * (2.0 / 3.0)) * window(curvature, 1, length + 1)
        )
    )
    fluxes = jnp.where(courant >= 0.0, upward, downward)
    return window(centre, 1, length) - (window(fluxes, 1, length) - window(fluxes, 0, length))


def to_frame(blocks, flip_flags):
    first_flag = (flip_flags[:, 0] == 1)[:, None, None, None, None]
    second_flag = (flip_flags[:, 1] == 1)[:, None, None, None, None]
    turned = jnp.where(first_flag, blocks[:, ::-1], blocks)
    return jnp.where(second_flag, turned[:, :, ::-1], turned)


def mixing_matrix(weights):
    totals = jnp.sum(weights, axis=-1, keepdims=True)
    identity = jnp.eye(weights.shape[-1], dtype=jnp.float32)
    return 0.6 * identity + 0.4 * (weights / totals)


def on_device(tracers, courant_first, courant_second, weights, frame_flip):
    stride = max(2, lax.axis_size("tile") // 8)
    extent = tracers.shape[1]
    fields = to_frame(tracers, frame_flip)
    first_faces = courant_first[..., None]
    second_faces = courant_second[..., None]

    def swap_columns(low_columns, high_columns):
        from_low, low_faces = passed_along(
            (high_columns, second_faces[:, :, extent - 1 :]), "tile", 1
        )
        from_high = passed_along(low_columns, "tile", -1)
        return (from_low, low_faces, from_high)

    def sweep_second(values, margins):
        from_low, low_faces, from_high = margins
        extended = jnp.concatenate([from_low, values, from_high], axis=2)
        courant = jnp.concatenate([low_faces, second_faces], axis=2)
        return ppm_update(extended, courant, 2)

    for substep in range(SUBSTEPS):
        swap_from_low, swap_low_faces = passed_along(
            (fields[:, extent - 3 :], first_faces[:, extent - 1 :]), "tile", stride
        )
        swap_from_high = passed_along(fields[:, :3], "tile", -stride)
        sweep_extended = jnp.concatenate([swap_from_low, fields, swap_from_high], axis=1)
        sweep_courant = jnp.concatenate([swap_low_faces, first_faces], axis=1)
        fields = ppm_update(sweep_extended, sweep_courant, 1)
        fields = sweep_second(fields, swap_columns(fields[:, :, :3], fields[:, :, extent - 3 :]))
    advected = to_frame(fields, frame_flip)
    mixing = mixing_matrix(weights)
    columns = lax.all_to_all(advected, "lev", split_axis=1, concat_axis=3, tiled=True)
    mixed = jnp.einsum("txykl,txylq->txykq", mixing, columns, precision=lax.Precision.HIGHEST)
    result = lax.all_to_all(mixed, "lev", split_axis=3, concat_axis=1, tiled=True)
    return result


def solution(mesh):
    in_specs = (
        P("tile", None, None, "lev", None),
        P("tile", None, None, "lev"),
        P("tile", None, None, "lev"),
        P("tile", "lev", None, None, None),
        P("tile", None),
    )
    out_specs = P("tile", None, None, "lev", None)
    return jax.shard_map(
        on_device, mesh=mesh, in_specs=in_specs, out_specs=out_specs, check_vma=False
    )
```

profile of v0, /device:TPU:0, one launch (start us, length us, event | category | flops | bytes accessed | tf_op | source)
XLA Modules:
  0.0 132.6 jit_solution(12249083645208609947)
XLA Ops:
  0.0 0.7 slice.412
  0.7 2.9 %collective-permute-start = (f32[1,1,8,18,1]{3,2,4,1,0:T(8,128)S(1)}, f32[1,1,8,18,1]{3,2,4,1,0:T(8,128)S(1)}, u32[]{:S(2)}, u32[]{:S(2)}) collective-permute-start(f32[1,1,8,18,1]{3,2,4,1,0:T(8,128)S(1)} %slice.412), channel_id=1, source_target_pairs={{0,8},{4,12},{8,16},{12,20},{16,24},{20,28},{24,0},{28,4},{1,9},{5... | collective-permute-start | bytes 1736 | tf_op jit(solution)/shard_map/ppermute | solution.py:12
  3.6 1.3 fusion.100
  5.6 1.5 %reverse_select_fusion.1 = f32[1,8,8,18,128]{4,2,3,0,1:T(8,128)S(1)} fusion(f32[1,8,8,18,128]{4,2,3,0,1:T(8,128)} %bitcast.31, pred[]{:T(512)} %bitcast.2), kind=kLoop, calls=%fused_computation.65 | loop fusion | flops 147456 | bytes 1179649 | tf_op jit(solution)/shard_map/jit(_where)/select_n | solution.py:55
  7.1 0.3 rev.13
  8.2 1.5 %collective-permute-start.1 = (f32[1,3,8,18,128]{4,2,3,0,1:T(8,128)S(1)}, f32[1,3,8,18,128]{4,2,3,0,1:T(8,128)S(1)}, u32[]{:S(2)}, u32[]{:S(2)}) collective-permute-start(f32[1,3,8,18,128]{4,2,3,0,1:T(8,128)S(1)} %get-tuple-element.27), channel_id=1, source_target_pairs={{0,8},{4,12},{8,16},{12,20},{16,24},{20,28},{24,0},{28,4},{1,9},{5... | collective-permute-start | bytes 663560 | tf_op jit(solution)/shard_map/ppermute | solution.py:12
  9.7 1.4 %collective-permute-start.2 = (f32[1,3,8,18,128]{4,2,3,0,1:T(8,128)S(1)}, f32[1,3,8,18,128]{4,2,3,0,1:T(8,128)S(1)}, u32[]{:S(2)}, u32[]{:S(2)}) collective-permute-start(f32[1,3,8,18,128]{4,2,3,0,1:T(8,128)S(1)} %get-tuple-element.28), channel_id=1, source_target_pairs={{0,24},{4,28},{8,0},{12,4},{16,8},{20,12},{24,16},{28,20},{1,25},{... | collective-permute-start | bytes 663560 | tf_op jit(solution)/shard_map/ppermute | solution.py:12
  11.3 0.1 copy.68
  11.4 0.1 copy.69
  11.6 0.1 copy.70
  11.7 0.2 copy.66
  11.9 0.1 copy.67
  12.0 7.4 %collective-permute-done.3 = f32[1,8,1,18,1]{3,1,4,2,0:T(8,128)S(1)} collective-permute-done((f32[1,8,1,18,1]{3,1,4,2,0:T(8,128)S(1)}, f32[1,8,1,18,1]{3,1,4,2,0:T(8,128)S(1)}, u32[]{:S(2)}, u32[]{:S(2)}) %collective-permute-start.3) | collective-permute-done | bytes 608 | tf_op jit(solution)/shard_map/ppermute | solution.py:12
  19.4 0.1 copy.76
  19.5 0.1 copy.77
  19.6 0.1 copy.78
  19.8 1.0 collective-permute-done.2
  20.9 0.2 fusion.47
  21.1 0.1 slice_subtract_fusion.5
  21.2 1.1 fusion.73
  22.6 2.6 %collective-permute-start.5 = (f32[1,8,3,18,128]{4,2,3,0,1:T(4,128)S(1)}, f32[1,8,3,18,128]{4,2,3,0,1:T(4,128)S(1)}, u32[]{:S(2)}, u32[]{:S(2)}) collective-permute-start(f32[1,8,3,18,128]{4,2,3,0,1:T(4,128)S(1)} %get-tuple-element.26), channel_id=1, source_target_pairs={{0,28},{4,0},{8,4},{12,8},{16,12},{20,16},{24,20},{28,24},{1,29},{... | collective-permute-start | bytes 663560 | tf_op jit(solution)/shard_map/ppermute | solution.py:12
  25.3 0.2 copy.73
  25.4 0.1 copy.75
  25.6 6.4 %collective-permute-done.4 = f32[1,8,3,18,128]{4,2,3,0,1:T(4,128)S(1)} collective-permute-done((f32[1,8,3,18,128]{4,2,3,0,1:T(4,128)S(1)}, f32[1,8,3,18,128]{4,2,3,0,1:T(4,128)S(1)}, u32[]{:S(2)}, u32[]{:S(2)}) %collective-permute-start.4) | collective-permute-done | bytes 221216 | tf_op jit(solution)/shard_map/ppermute | solution.py:12
  32.0 0.2 pad_maximum_fusion
  32.2 0.5 fusion.38
  32.7 0.3 slice_subtract_fusion.2
  33.1 2.1 %fusion.30 = f32[1,8,9,18,128]{4,2,3,0,1:T(8,128)S(1)} fusion(f32[1,8,10,18,128]{4,2,3,0,1:T(8,128)S(1)} %get-tuple-element.10, f32[1,8,10,18,128]{4,2,3,0,1:T(8,128)S(1)} %get-tuple-element.9, f32[1,8,11,18,128]{4,2,3,0,1:T(8,128)S(1)} %fusion.38, f32[8,9,18]{1,2,0:T(8,128)S(1)} %copy.78, f32[8,9,18]{1,2,0:T(8,128)S(1)} %copy.77, f32[8,9,18]{1,2,0:T(8,128)S(1)} %copy.76, ...), kind=kLoop, calls=%fused_computation.40 | loop fusion | flops 1824768 | bytes 4003344 | tf_op jit(solution)/shard_map/jit(_where)/select_n | solution.py:48
  35.2 0.1 fusion.82
  35.4 2.9 %collective-permute-start.7 = (f32[1,3,8,18,128]{4,2,3,0,1:T(8,128)S(1)}, f32[1,3,8,18,128]{4,2,3,0,1:T(8,128)S(1)}, u32[]{:S(2)}, u32[]{:S(2)}) collective-permute-start(f32[1,3,8,18,128]{4,2,3,0,1:T(8,128)S(1)} %get-tuple-element.24), channel_id=1, source_target_pairs={{0,24},{4,28},{8,0},{12,4},{16,8},{20,12},{24,16},{28,20},{1,25},{... | collective-permute-start | bytes 663560 | tf_op jit(solution)/shard_map/ppermute | solution.py:12
  38.3 6.3 %collective-permute-done.6 = f32[1,3,8,18,128]{4,2,3,0,1:T(8,128)S(1)} collective-permute-done((f32[1,3,8,18,128]{4,2,3,0,1:T(8,128)S(1)}, f32[1,3,8,18,128]{4,2,3,0,1:T(8,128)S(1)}, u32[]{:S(2)}, u32[]{:S(2)}) %collective-permute-start.6) | collective-permute-done | bytes 221216 | tf_op jit(solution)/shard_map/ppermute | solution.py:12
  44.6 3.5 %collective-permute-done.7 = f32[1,3,8,18,128]{4,2,3,0,1:T(8,128)S(1)} collective-permute-done((f32[1,3,8,18,128]{4,2,3,0,1:T(8,128)S(1)}, f32[1,3,8,18,128]{4,2,3,0,1:T(8,128)S(1)}, u32[]{:S(2)}, u32[]{:S(2)}) %collective-permute-start.7) | collective-permute-done | bytes 221216 | tf_op jit(solution)/shard_map/ppermute | solution.py:12
  48.2 0.2 fusion.44
  48.3 0.1 slice_subtract_fusion.4
  48.5 1.1 fusion.64
  49.7 0.1 fusion.96
  49.9 2.6 %collective-permute-start.9 = (f32[1,8,3,18,128]{4,2,3,0,1:T(4,128)S(1)}, f32[1,8,3,18,128]{4,2,3,0,1:T(4,128)S(1)}, u32[]{:S(2)}, u32[]{:S(2)}) collective-permute-start(f32[1,8,3,18,128]{4,2,3,0,1:T(4,128)S(1)} %get-tuple-element.22), channel_id=1, source_target_pairs={{0,28},{4,0},{8,4},{12,8},{16,12},{20,16},{24,20},{28,24},{1,29},{... | collective-permute-start | bytes 663560 | tf_op jit(solution)/shard_map/ppermute | solution.py:12
  52.5 7.2 %collective-permute-done.8 = f32[1,8,3,18,128]{4,2,3,0,1:T(4,128)S(1)} collective-permute-done((f32[1,8,3,18,128]{4,2,3,0,1:T(4,128)S(1)}, f32[1,8,3,18,128]{4,2,3,0,1:T(4,128)S(1)}, u32[]{:S(2)}, u32[]{:S(2)}) %collective-permute-start.8) | collective-permute-done | bytes 221216 | tf_op jit(solution)/shard_map/ppermute | solution.py:12
  59.7 0.2 pad_maximum_fusion.1
  59.9 0.5 fusion.25
  60.4 0.3 slice_subtract_fusion.1
  60.7 2.1 %fusion.17 = f32[1,8,9,18,128]{4,2,3,0,1:T(8,128)S(1)} fusion(f32[1,8,10,18,128]{4,2,3,0,1:T(8,128)S(1)} %get-tuple-element.8, f32[1,8,10,18,128]{4,2,3,0,1:T(8,128)S(1)} %get-tuple-element.7, f32[1,8,11,18,128]{4,2,3,0,1:T(8,128)S(1)} %fusion.25, f32[8,9,18]{1,2,0:T(8,128)S(1)} %copy.78, f32[8,9,18]{1,2,0:T(8,128)S(1)} %copy.77, f32[8,9,18]{1,2,0:T(8,128)S(1)} %copy.76, ...), kind=kLoop, calls=%fused_computation.23 | loop fusion | flops 1824768 | bytes 4003344 | tf_op jit(solution)/shard_map/jit(_where)/select_n | solution.py:48
  63.0 2.9 %collective-permute-start.11 = (f32[1,3,8,18,128]{4,2,3,0,1:T(8,128)S(1)}, f32[1,3,8,18,128]{4,2,3,0,1:T(8,128)S(1)}, u32[]{:S(2)}, u32[]{:S(2)}) collective-permute-start(f32[1,3,8,18,128]{4,2,3,0,1:T(8,128)S(1)} %get-tuple-element.20), channel_id=1, source_target_pairs={{0,24},{4,28},{8,0},{12,4},{16,8},{20,12},{24,16},{28,20},{1,25},{... | collective-permute-start | bytes 663560 | tf_op jit(solution)/shard_map/ppermute | solution.py:12
  66.0 6.3 %collective-permute-done.10 = f32[1,3,8,18,128]{4,2,3,0,1:T(8,128)S(1)} collective-permute-done((f32[1,3,8,18,128]{4,2,3,0,1:T(8,128)S(1)}, f32[1,3,8,18,128]{4,2,3,0,1:T(8,128)S(1)}, u32[]{:S(2)}, u32[]{:S(2)}) %collective-permute-start.10) | collective-permute-done | bytes 221216 | tf_op jit(solution)/shard_map/ppermute | solution.py:12
  72.3 3.2 %collective-permute-done.11 = f32[1,3,8,18,128]{4,2,3,0,1:T(8,128)S(1)} collective-permute-done((f32[1,3,8,18,128]{4,2,3,0,1:T(8,128)S(1)}, f32[1,3,8,18,128]{4,2,3,0,1:T(8,128)S(1)}, u32[]{:S(2)}, u32[]{:S(2)}) %collective-permute-start.11) | collective-permute-done | bytes 221216 | tf_op jit(solution)/shard_map/ppermute | solution.py:12
  75.6 0.2 fusion.41
  75.7 0.1 slice_subtract_fusion.3
  75.9 1.1 fusion.55
  77.3 2.6 %collective-permute-start.13 = (f32[1,8,3,18,128]{4,2,3,0,1:T(4,128)S(1)}, f32[1,8,3,18,128]{4,2,3,0,1:T(4,128)S(1)}, u32[]{:S(2)}, u32[]{:S(2)}) collective-permute-start(f32[1,8,3,18,128]{4,2,3,0,1:T(4,128)S(1)} %get-tuple-element.18), channel_id=1, source_target_pairs={{0,28},{4,0},{8,4},{12,8},{16,12},{20,16},{24,20},{28,24},{1,29},{... | collective-permute-start | bytes 663560 | tf_op jit(solution)/shard_map/ppermute | solution.py:12
  79.9 7.3 %collective-permute-done.12 = f32[1,8,3,18,128]{4,2,3,0,1:T(4,128)S(1)} collective-permute-done((f32[1,8,3,18,128]{4,2,3,0,1:T(4,128)S(1)}, f32[1,8,3,18,128]{4,2,3,0,1:T(4,128)S(1)}, u32[]{:S(2)}, u32[]{:S(2)}) %collective-permute-start.12) | collective-permute-done | bytes 221216 | tf_op jit(solution)/shard_map/ppermute | solution.py:12
  87.2 0.2 pad_maximum_fusion.2
  87.4 0.5 fusion.12
  87.9 0.3 slice_subtract_fusion
  88.3 2.1 %fusion.4 = f32[1,8,9,18,128]{4,2,3,0,1:T(8,128)S(1)} fusion(f32[1,8,10,18,128]{4,2,3,0,1:T(8,128)S(1)} %get-tuple-element.6, f32[1,8,10,18,128]{4,2,3,0,1:T(8,128)S(1)} %get-tuple-element.5, f32[1,8,11,18,128]{4,2,3,0,1:T(8,128)S(1)} %fusion.12, f32[8,9,18]{1,2,0:T(8,128)S(1)} %copy.78, f32[8,9,18]{1,2,0:T(8,128)S(1)} %copy.77, f32[8,9,18]{1,2,0:T(8,128)S(1)} %copy.76, ...), kind=kLoop, calls=%fused_computation.6 | loop fusion | flops 1824768 | bytes 4003344 | tf_op jit(solution)/shard_map/jit(_where)/select_n | solution.py:48
  90.4 0.1 fusion.78
  90.6 0.3 rev.15
  90.8 0.9 broadcast_select_fusion
  91.7 4.7 %all-to-all-start = ((f32[1,8,8,18,128]{4,2,3,0,1:T(8,128)}), f32[1,8,8,18,128]{4,2,3,0,1:T(8,128)S(1)}, u32[]{:S(2)}, u32[]{:S(2)}) async-start(f32[1,8,8,18,128]{4,2,3,0,1:T(8,128)} %broadcast_select_fusion), calls=%async_computation | async-start | bytes 1179648 | tf_op jit(solution)/shard_map/all_to_all | solution.py:96
  96.4 0.3 reduce_sum.9
  96.8 15.7 %all-to-all-done = f32[1,8,8,18,128]{4,2,3,0,1:T(8,128)S(1)} async-done(((f32[1,8,8,18,128]{4,2,3,0,1:T(8,128)}), f32[1,8,8,18,128]{4,2,3,0,1:T(8,128)S(1)}, u32[]{:S(2)}, u32[]{:S(2)}) %all-to-all-start) | async-done | bytes 589856 | tf_op jit(solution)/shard_map/all_to_all | solution.py:96
  112.5 1.2 convolution_bitcast_fusion
  113.8 0.1 copy.81
  113.9 17.8 %all_to_all.33 = f32[1,2,8,72,128]{4,2,1,0,3:T(8,128)S(1)} all-to-all(f32[1,2,8,72,128]{4,2,1,0,3:T(8,128)S(1)} %copy.81), channel_id=1, replica_groups=mesh['tile'=8,'lev'=4] {'lev'}, dimensions={3} | all-to-all | bytes 1179648 | tf_op jit(solution)/shard_map/all_to_all | solution.py:98
  131.7 0.9 copy.83
  (44 shorter events, 1.4 us)
Async XLA Ops:
  0.7 10.5 %collective-permute-start = (f32[1,1,8,18,1]{3,2,4,1,0:T(8,128)S(1)}, f32[1,1,8,18,1]{3,2,4,1,0:T(8,128)S(1)}, u32[]{:S(2)}, u32[]{:S(2)}) collective-permute-start(f32[1,1,8,18,1]{3,2,4,1,0:T(8,128)S(1)} %slice.412), channel_id=1, source_target_pairs={{0,8},{4,12},{8,16},{12,20},{16,24},{20,28},{24,0},{28,4},{1,9},{5... | collective-permute-start | bytes 1736 | tf_op jit(solution)/shard_map/ppermute | solution.py:12
  5.6 2.4 %copy-start = (f32[1,8,8,18,128]{4,2,3,1,0:T(8,128)S(1)}, f32[1,8,8,18,128]{4,2,3,1,0:T(8,128)}, u32[]{:S(2)}) copy-start(f32[1,8,8,18,128]{4,2,3,1,0:T(8,128)} %param.5) | copy-start | bytes 1769476
  8.0 3.1 %copy-start.3 = (f32[1,8,8,18]{3,2,1,0:T(8,128)S(1)}, f32[1,8,8,18]{3,2,1,0:T(8,128)}, u32[]{:S(2)}) copy-start(f32[1,8,8,18]{3,2,1,0:T(8,128)} %param.7) | copy-start | bytes 13828
  8.0 3.2 %copy-start.2 = (f32[1,8,8,18]{3,2,1,0:T(8,128)S(1)}, f32[1,8,8,18]{3,2,1,0:T(8,128)}, u32[]{:S(2)}) copy-start(f32[1,8,8,18]{3,2,1,0:T(8,128)} %param.6) | copy-start | bytes 13828
  8.2 11.6 %collective-permute-start.1 = (f32[1,3,8,18,128]{4,2,3,0,1:T(8,128)S(1)}, f32[1,3,8,18,128]{4,2,3,0,1:T(8,128)S(1)}, u32[]{:S(2)}, u32[]{:S(2)}) collective-permute-start(f32[1,3,8,18,128]{4,2,3,0,1:T(8,128)S(1)} %get-tuple-element.27), channel_id=1, source_target_pairs={{0,8},{4,12},{8,16},{12,20},{16,24},{20,28},{24,0},{28,4},{1,9},{5... | collective-permute-start | bytes 663560 | tf_op jit(solution)/shard_map/ppermute | solution.py:12
  9.7 11.1 %collective-permute-start.2 = (f32[1,3,8,18,128]{4,2,3,0,1:T(8,128)S(1)}, f32[1,3,8,18,128]{4,2,3,0,1:T(8,128)S(1)}, u32[]{:S(2)}, u32[]{:S(2)}) collective-permute-start(f32[1,3,8,18,128]{4,2,3,0,1:T(8,128)S(1)} %get-tuple-element.28), channel_id=1, source_target_pairs={{0,24},{4,28},{8,0},{12,4},{16,8},{20,12},{24,16},{28,20},{1,25},{... | collective-permute-start | bytes 663560 | tf_op jit(solution)/shard_map/ppermute | solution.py:12
  11.1 8.2 %collective-permute-start.3 = (f32[1,8,1,18,1]{3,1,4,2,0:T(8,128)S(1)}, f32[1,8,1,18,1]{3,1,4,2,0:T(8,128)S(1)}, u32[]{:S(2)}, u32[]{:S(2)}) collective-permute-start(f32[1,8,1,18,1]{3,1,4,2,0:T(8,128)S(1)} %bitcast.49), channel_id=1, source_target_pairs={{0,4},{4,8},{8,12},{12,16},{16,20},{20,24},{24,28},{28,0},{1,5},{5... | collective-permute-start | bytes 1736 | tf_op jit(solution)/shard_map/ppermute | solution.py:12
  22.6 9.5 %collective-permute-start.4 = (f32[1,8,3,18,128]{4,2,3,0,1:T(4,128)S(1)}, f32[1,8,3,18,128]{4,2,3,0,1:T(4,128)S(1)}, u32[]{:S(2)}, u32[]{:S(2)}) collective-permute-start(f32[1,8,3,18,128]{4,2,3,0,1:T(4,128)S(1)} %get-tuple-element.25), channel_id=1, source_target_pairs={{0,4},{4,8},{8,12},{12,16},{16,20},{20,24},{24,28},{28,0},{1,5},{5... | collective-permute-start | bytes 663560 | tf_op jit(solution)/shard_map/ppermute | solution.py:12
  22.6 9.4 %collective-permute-start.5 = (f32[1,8,3,18,128]{4,2,3,0,1:T(4,128)S(1)}, f32[1,8,3,18,128]{4,2,3,0,1:T(4,128)S(1)}, u32[]{:S(2)}, u32[]{:S(2)}) collective-permute-start(f32[1,8,3,18,128]{4,2,3,0,1:T(4,128)S(1)} %get-tuple-element.26), channel_id=1, source_target_pairs={{0,28},{4,0},{8,4},{12,8},{16,12},{20,16},{24,20},{28,24},{1,29},{... | collective-permute-start | bytes 663560 | tf_op jit(solution)/shard_map/ppermute | solution.py:12
  35.4 9.2 %collective-permute-start.6 = (f32[1,3,8,18,128]{4,2,3,0,1:T(8,128)S(1)}, f32[1,3,8,18,128]{4,2,3,0,1:T(8,128)S(1)}, u32[]{:S(2)}, u32[]{:S(2)}) collective-permute-start(f32[1,3,8,18,128]{4,2,3,0,1:T(8,128)S(1)} %get-tuple-element.23), channel_id=1, source_target_pairs={{0,8},{4,12},{8,16},{12,20},{16,24},{20,28},{24,0},{28,4},{1,9},{5... | collective-permute-start | bytes 663560 | tf_op jit(solution)/shard_map/ppermute | solution.py:12
  35.4 12.7 %collective-permute-start.7 = (f32[1,3,8,18,128]{4,2,3,0,1:T(8,128)S(1)}, f32[1,3,8,18,128]{4,2,3,0,1:T(8,128)S(1)}, u32[]{:S(2)}, u32[]{:S(2)}) collective-permute-start(f32[1,3,8,18,128]{4,2,3,0,1:T(8,128)S(1)} %get-tuple-element.24), channel_id=1, source_target_pairs={{0,24},{4,28},{8,0},{12,4},{16,8},{20,12},{24,16},{28,20},{1,25},{... | collective-permute-start | bytes 663560 | tf_op jit(solution)/shard_map/ppermute | solution.py:12
  49.8 9.9 %collective-permute-start.8 = (f32[1,8,3,18,128]{4,2,3,0,1:T(4,128)S(1)}, f32[1,8,3,18,128]{4,2,3,0,1:T(4,128)S(1)}, u32[]{:S(2)}, u32[]{:S(2)}) collective-permute-start(f32[1,8,3,18,128]{4,2,3,0,1:T(4,128)S(1)} %get-tuple-element.21), channel_id=1, source_target_pairs={{0,4},{4,8},{8,12},{12,16},{16,20},{20,24},{24,28},{28,0},{1,5},{5... | collective-permute-start | bytes 663560 | tf_op jit(solution)/shard_map/ppermute | solution.py:12
  49.9 9.8 %collective-permute-start.9 = (f32[1,8,3,18,128]{4,2,3,0,1:T(4,128)S(1)}, f32[1,8,3,18,128]{4,2,3,0,1:T(4,128)S(1)}, u32[]{:S(2)}, u32[]{:S(2)}) collective-permute-start(f32[1,8,3,18,128]{4,2,3,0,1:T(4,128)S(1)} %get-tuple-element.22), channel_id=1, source_target_pairs={{0,28},{4,0},{8,4},{12,8},{16,12},{20,16},{24,20},{28,24},{1,29},{... | collective-permute-start | bytes 663560 | tf_op jit(solution)/shard_map/ppermute | solution.py:12
  63.0 9.3 %collective-permute-start.10 = (f32[1,3,8,18,128]{4,2,3,0,1:T(8,128)S(1)}, f32[1,3,8,18,128]{4,2,3,0,1:T(8,128)S(1)}, u32[]{:S(2)}, u32[]{:S(2)}) collective-permute-start(f32[1,3,8,18,128]{4,2,3,0,1:T(8,128)S(1)} %get-tuple-element.19), channel_id=1, source_target_pairs={{0,8},{4,12},{8,16},{12,20},{16,24},{20,28},{24,0},{28,4},{1,9},{5... | collective-permute-start | bytes 663560 | tf_op jit(solution)/shard_map/ppermute | solution.py:12
  63.0 12.5 %collective-permute-start.11 = (f32[1,3,8,18,128]{4,2,3,0,1:T(8,128)S(1)}, f32[1,3,8,18,128]{4,2,3,0,1:T(8,128)S(1)}, u32[]{:S(2)}, u32[]{:S(2)}) collective-permute-start(f32[1,3,8,18,128]{4,2,3,0,1:T(8,128)S(1)} %get-tuple-element.20), channel_id=1, source_target_pairs={{0,24},{4,28},{8,0},{12,4},{16,8},{20,12},{24,16},{28,20},{1,25},{... | collective-permute-start | bytes 663560 | tf_op jit(solution)/shard_map/ppermute | solution.py:12
  77.2 10.0 %collective-permute-start.12 = (f32[1,8,3,18,128]{4,2,3,0,1:T(4,128)S(1)}, f32[1,8,3,18,128]{4,2,3,0,1:T(4,128)S(1)}, u32[]{:S(2)}, u32[]{:S(2)}) collective-permute-start(f32[1,8,3,18,128]{4,2,3,0,1:T(4,128)S(1)} %get-tuple-element.17), channel_id=1, source_target_pairs={{0,4},{4,8},{8,12},{12,16},{16,20},{20,24},{24,28},{28,0},{1,5},{5... | collective-permute-start | bytes 663560 | tf_op jit(solution)/shard_map/ppermute | solution.py:12
  77.3 9.9 %collective-permute-start.13 = (f32[1,8,3,18,128]{4,2,3,0,1:T(4,128)S(1)}, f32[1,8,3,18,128]{4,2,3,0,1:T(4,128)S(1)}, u32[]{:S(2)}, u32[]{:S(2)}) collective-permute-start(f32[1,8,3,18,128]{4,2,3,0,1:T(4,128)S(1)} %get-tuple-element.18), channel_id=1, source_target_pairs={{0,28},{4,0},{8,4},{12,8},{16,12},{20,16},{24,20},{28,24},{1,29},{... | collective-permute-start | bytes 663560 | tf_op jit(solution)/shard_map/ppermute | solution.py:12
  90.8 5.6 %copy-start.1 = (f32[1,2,8,72,72]{4,3,2,1,0:T(8,128)S(1)}, f32[1,2,8,72,72]{4,3,2,1,0:T(8,128)}, u32[]{:S(2)}) copy-start(f32[1,2,8,72,72]{4,3,2,1,0:T(8,128)} %param.8) | copy-start | bytes 995332
  91.7 20.8 %all-to-all-start = ((f32[1,8,8,18,128]{4,2,3,0,1:T(8,128)}), f32[1,8,8,18,128]{4,2,3,0,1:T(8,128)S(1)}, u32[]{:S(2)}, u32[]{:S(2)}) async-start(f32[1,8,8,18,128]{4,2,3,0,1:T(8,128)} %broadcast_select_fusion), calls=%async_computation | async-start | bytes 1179648 | tf_op jit(solution)/shard_map/all_to_all | solution.py:96
where the time goes:
time: 133 us
  waiting for transfers between devices  64.3 us (48%)
  starting transfers between devices  24.7 us (19%)
  blocking collectives  17.8 us (13%)
  other arithmetic  17.4 us (13%)
  local copies, waits for them, and re-layouts  5.39 us (4%)
  between operations  1.74 us (1%)
    ppermute x14, waiting for transfers between devices, passed_along(): return lax.ppermute(value, axis, pairs)  48.6 us
    ppermute x14, starting transfers between devices, passed_along(): return lax.ppermute(value, axis, pairs)  20 us
    all_to_all x1, blocking collectives, on_device(): lax.all_to_all(mixed, 'lev', split_axis=3, concat_axis=1, tiled=True)  17.8 us
    all_to_all x1, waiting for transfers between devices, on_device(): lax.all_to_all(advected, 'lev', split_axis=1, concat_axis=3, tiled=True)  15.7 us
    select_n x6, other arithmetic, ppm_update(): fluxes = jnp.where(courant >= 0.0, upward, downward)  9.72 us
    all_to_all x1, starting transfers between devices, on_device(): lax.all_to_all(advected, 'lev', split_axis=1, concat_axis=3, tiled=True)  4.7 us
  transfers between devices with their start and end apart: 15, of which 10 were waited for; matrix products, arithmetic and copies ran while one was open for 4% of the time, Pallas kernels for 0%

commit v1 on v0

--- a/solution.py
+++ b/solution.py
@@ -1,9 +1,16 @@
+import functools
+
 import jax
 import jax.numpy as jnp
 from jax import lax
+from jax.experimental import pallas as pl
+from jax.experimental.pallas import tpu as pltpu
 from jax.sharding import PartitionSpec as P
 
 SUBSTEPS = 3
+SUBLANES = 8
+LANES = 128
+VMEM_LIMIT = 40 * 1024 * 1024
 
 
 def passed_along(value, axis, steps):
@@ -62,41 +69,389 @@
     return 0.6 * identity + 0.4 * (weights / totals)
 
 
-def on_device(tracers, courant_first, courant_second, weights, frame_flip):
-    stride = max(2, lax.axis_size("tile") // 8)
+def tile_stride(tiles):
+    return max(2, tiles // 8)
+
+
+def by_halos(tracers, courant_first, courant_second, weights, frame_flip):
+    stride = tile_stride(lax.axis_size("tile"))
     extent = tracers.shape[1]
     fields = to_frame(tracers, frame_flip)
     first_faces = courant_first[..., None]
     second_faces = courant_second[..., None]
-
-    def swap_columns(low_columns, high_columns):
-        from_low, low_faces = passed_along(
-            (high_columns, second_faces[:, :, extent - 1 :]), "tile", 1
-        )
-        from_high = passed_along(low_columns, "tile", -1)
-        return (from_low, low_faces, from_high)
-
-    def sweep_second(values, margins):
-        from_low, low_faces, from_high = margins
-        extended = jnp.concatenate([from_low, values, from_high], axis=2)
-        courant = jnp.concatenate([low_faces, second_faces], axis=2)
-        return ppm_update(extended, courant, 2)
-
     for substep in range(SUBSTEPS):
-        swap_from_low, swap_low_faces = passed_along(
-            (fields[:, extent - 3 :], first_faces[:, extent - 1 :]), "tile", stride
-        )
-        swap_from_high = passed_along(fields[:, :3], "tile", -stride)
-        sweep_extended = jnp.concatenate([swap_from_low, fields, swap_from_high], axis=1)
-        sweep_courant = jnp.concatenate([swap_low_faces, first_faces], axis=1)
-        fields = ppm_update(sweep_extended, sweep_courant, 1)
-        fields = sweep_second(fields, swap_columns(fields[:, :, :3], fields[:, :, extent - 3 :]))
+        for along, faces, steps in ((1, first_faces, stride), (2, second_faces, 1)):
+            size = fields.shape[along]
+            high_cells = lax.slice_in_dim(fields, size - 3, size, axis=along)
+            low_cells = lax.slice_in_dim(fields, 0, 3, axis=along)
+            high_face = lax.slice_in_dim(faces, size - 1, size, axis=along)
+            from_low, low_face = passed_along((high_cells, high_face), "tile", steps)
+            from_high = passed_along(low_cells, "tile", -steps)
+            fields = ppm_update(
+                jnp.concatenate([from_low, fields, from_high], axis=along),
+                jnp.concatenate([low_face, faces], axis=along),
+                along,
+            )
     advected = to_frame(fields, frame_flip)
     mixing = mixing_matrix(weights)
     columns = lax.all_to_all(advected, "lev", split_axis=1, concat_axis=3, tiled=True)
     mixed = jnp.einsum("txykl,txylq->txykq", mixing, columns, precision=lax.Precision.HIGHEST)
-    result = lax.all_to_all(mixed, "lev", split_axis=3, concat_axis=1, tiled=True)
-    return result
+    return lax.all_to_all(mixed, "lev", split_axis=3, concat_axis=1, tiled=True)
+
+
+class Plan:
+    def __init__(self, side, levels, tracers, tiles, layers):
+        self.side, self.levels, self.tracers = side, levels, tracers
+        self.tiles, self.layers = tiles, layers
+        self.cells = side * side
+        self.full = levels // tiles
+        self.spare = levels - self.full * tiles
+        self.fits = (
+            tiles == SUBLANES
+            and tracers == LANES
+            and self.cells * 2 == LANES
+            and side % layers == 0
+            and self.spare > 0
+            and self.full > 0
+            and tiles % self.spare == 0
+        )
+        if not self.fits:
+            return
+        self.groups = tiles // self.spare
+        self.width = tracers // self.groups
+        self.part_rows = self.cells // self.groups
+        self.kinds = self.full + 1
+        self.tail_at = self.full * self.cells
+        self.courant_at = self.tail_at + self.part_rows
+        self.flip_at = self.courant_at + self.kinds
+        self.rows = -(-(self.flip_at + 1) // SUBLANES) * SUBLANES
+        self.own_cells = self.cells // layers
+        self.back_tail = self.full * self.own_cells
+        self.back_part = self.own_cells // self.groups
+        self.back_rows = -(-(self.back_tail + self.back_part) // SUBLANES) * SUBLANES
+        self.all_levels = levels * layers
+        self.fits = (
+            self.cells % self.groups == 0
+            and self.own_cells % self.groups == 0
+            and self.part_rows % SUBLANES == 0
+        )
+
+
+def lane_group(shape, width):
+    return lax.broadcasted_iota(jnp.int32, shape, 1) // width
+
+
+def pack_kernel(p, x_ref, first_ref, second_ref, flip_ref, out_ref, spare_ref, faces_ref, sems):
+    copies = []
+    for d in range(p.tiles):
+        for f in range(p.full):
+            copies.append(
+                pltpu.make_async_copy(
+                    x_ref.at[:, p.full * d + f, :],
+                    out_ref.at[d, pl.ds(f * p.cells, p.cells), :],
+                    sems.at[len(copies)],
+                )
+            )
+    spares = []
+    for h in range(p.spare):
+        spares.append(
+            pltpu.make_async_copy(
+                x_ref.at[:, p.full * p.tiles + h, :],
+                spare_ref.at[h],
+                sems.at[len(copies) + h],
+            )
+        )
+    for copy in spares + copies:
+        copy.start()
+    faces_ref[...] = jnp.zeros_like(faces_ref)
+    faces_ref[: p.cells, : p.levels] = first_ref[...]
+    faces_ref[p.cells :, : p.levels] = second_ref[...]
+    faces = faces_ref[...].T
+    lane = lax.broadcasted_iota(jnp.int32, (1, LANES), 1)
+    first_flip = jnp.full((1, LANES), flip_ref[0, 0]).astype(jnp.float32)
+    second_flip = jnp.full((1, LANES), flip_ref[0, 1]).astype(jnp.float32)
+    flips = jnp.where(lane < p.cells, first_flip, second_flip)
+    filler = jnp.zeros((p.rows - p.flip_at - 1, LANES), jnp.float32)
+    for d in range(p.tiles):
+        level = p.full * d
+        out_ref[d, p.courant_at : p.courant_at + p.full, :] = faces[level : level + p.full]
+        rest = p.full * p.tiles + d // p.groups
+        out_ref[d, p.courant_at + p.full : p.flip_at, :] = faces[rest : rest + 1]
+        out_ref[d, p.flip_at : p.flip_at + 1, :] = flips
+        if p.rows > p.flip_at + 1:
+            out_ref[d, p.flip_at + 1 :, :] = filler
+    for copy in spares:
+        copy.wait()
+    group = lane_group((p.part_rows, LANES), p.width)
+    for h in range(p.spare):
+        parts = [spare_ref[h, m * p.part_rows : (m + 1) * p.part_rows, :] for m in range(p.groups)]
+        for g in range(p.groups):
+            rows = None
+            for m in range(p.groups):
+                shift = (m - g) * p.width % LANES
+                moved = pltpu.roll(parts[m], shift, 1) if shift else parts[m]
+                rows = moved if rows is None else jnp.where(group == m, moved, rows)
+            out_ref[h * p.groups + g, p.tail_at : p.tail_at + p.part_rows, :] = rows
+    for copy in copies:
+        copy.wait()
+
+
+def advect_kernel(p, stride, in_ref, out_ref, q_ref, near_ref, far_ref, mid_ref):
+    tiles, side, cells = p.tiles, p.side, p.cells
+    shape = (tiles, LANES)
+
+    def row(at):
+        return in_ref[pl.ds(at, tiles, stride=p.rows), :]
+
+    flips = row(p.flip_at)
+    first_flip = jnp.broadcast_to(flips[:, 0:1], shape) > 0.5
+    second_flip = jnp.broadcast_to(flips[:, cells : cells + 1], shape) > 0.5
+
+    def turned(get):
+        for i in range(side // 2):
+            for j in range(side // 2):
+                i2, j2 = side - 1 - i, side - 1 - j
+                ll, hl, lh, hh = get(i, j), get(i2, j), get(i, j2), get(i2, j2)
+                a, b = jnp.where(first_flip, hl, ll), jnp.where(first_flip, ll, hl)
+                c, d = jnp.where(first_flip, hh, lh), jnp.where(first_flip, lh, hh)
+                yield i * side + j, jnp.where(second_flip, c, a)
+                yield i2 * side + j, jnp.where(second_flip, d, b)
+                yield i * side + j2, jnp.where(second_flip, a, c)
+                yield i2 * side + j2, jnp.where(second_flip, b, d)
+
+    for kind in range(p.kinds):
+        if kind < p.full:
+            get = lambda i, j: row(kind * cells + i * side + j)
+        else:
+
+            def get(i, j):
+                m, r = divmod(i * side + j, p.part_rows)
+                value = row(p.tail_at + r)
+                return pltpu.roll(value, LANES - m * p.width, 1) if m else value
+
+        for cell, value in turned(get):
+            q_ref[kind * cells + cell] = value
+        courant = row(p.courant_at + kind)
+        for at in range(2 * cells):
+            c = jnp.broadcast_to(courant[:, at : at + 1], shape)
+            e = jnp.abs(c)
+            u = 1.0 - e
+            cu = c * u
+            near_ref[kind * 2 * cells + at] = (cu * u) * (1.0 / 12.0)
+            far_ref[kind * 2 * cells + at] = (cu * e) * (-1.0 / 12.0)
+            mid_ref[kind * 2 * cells + at] = (c * e) * (3.0 - 2.0 * e)
+
+    def sweep(at, faces_at, step, shift):
+        cell = [at + step * i for i in range(side)]
+        face = [faces_at + step * i for i in range(side)]
+        q = [q_ref[cell[i]] for i in range(side)]
+        up = lambda v: pltpu.roll(v, shift, 0)
+        down = lambda v: pltpu.roll(v, tiles - shift, 0)
+        ext = [up(q[side - 1])] + q + [down(q[0]), down(q[1])]
+        edge = [
+            7.0 * (ext[i + 1] + ext[i + 2]) - (ext[i] + ext[i + 3]) for i in range(side)
+        ]
+        edges = [up(edge[side - 1])] + edge + [down(edge[0])]
+        flux = []
+        for i in range(side):
+            near = near_ref[face[i]]
+            upwind = near >= 0.0
+            far = jnp.where(upwind, edges[i], edges[i + 2])
+            mid = jnp.where(upwind, ext[i + 1], ext[i + 2])
+            flux.append(near * edge[i] + far_ref[face[i]] * far + mid_ref[face[i]] * mid)
+        fluxes = [up(flux[side - 1])] + flux
+        for i in range(side):
+            q_ref[cell[i]] = q[i] - (fluxes[i + 1] - fluxes[i])
+
+    def step(count, carry):
+        kind = count // SUBSTEPS
+        at = kind * cells
+        faces_at = kind * 2 * cells
+        for j in range(side):
+            sweep(at + j, faces_at + j, side, stride)
+        for i in range(side):
+            sweep(at + i * side, faces_at + cells + i * side, 1, 1)
+        return carry
+
+    lax.fori_loop(0, p.kinds * SUBSTEPS, step, 0)
+
+    pitch = p.layers * p.back_rows
+
+    def send(cell_layer, at, value):
+        out_ref[pl.ds(cell_layer * p.back_rows + at, tiles, stride=pitch), :] = value
+
+    for kind in range(p.kinds):
+        back = turned(lambda i, j: q_ref[kind * cells + i * side + j])
+        if kind < p.full:
+            for cell, value in back:
+                layer, own = divmod(cell, p.own_cells)
+                send(layer, kind * p.own_cells + own, value)
+        else:
+            for cell, value in back:
+                q_ref[kind * cells + cell] = value
+    group = lane_group(shape, p.width)
+    for layer in range(p.layers):
+        for r in range(p.back_part):
+            rows = None
+            for m in range(p.groups):
+                value = q_ref[p.full * cells + layer * p.own_cells + m * p.back_part + r]
+                moved = pltpu.roll(value, m * p.width, 1) if m else value
+                rows = moved if rows is None else jnp.where(group == m, moved, rows)
+            send(layer, p.back_tail + r, rows)
+
+
+def mix_kernel(p, in_ref, weights_ref, *refs):
+    out_refs, (x_ref, all_ref) = refs[: p.layers], refs[p.layers :]
+    tiles = p.tiles
+    shape = (tiles, LANES)
+    pitch = p.layers * p.back_rows
+    group = lane_group(shape, p.width)
+    part = lax.broadcasted_iota(jnp.int32, shape, 0) % p.groups
+    places = [(group == g) & (part == g) for g in range(p.groups)]
+
+    def row(layer, at):
+        return in_ref[pl.ds(layer * p.back_rows + at, tiles, stride=pitch), :]
+
+    for r in range(p.back_part):
+        turned = []
+        for layer in range(p.layers):
+            value = row(layer, p.back_tail + r)
+            turned.append([value] + [pltpu.roll(value, s * p.width, 1) for s in range(1, p.groups)])
+        for m in range(p.groups):
+            own = m * p.back_part + r
+            for layer in range(p.layers):
+                base = layer * p.levels
+                for f in range(p.full):
+                    x_ref[own, pl.ds(base + f, tiles, stride=p.full), :] = row(
+                        layer, f * p.own_cells + own
+                    )
+                tail = jnp.zeros(shape, jnp.float32)
+                for g in range(p.groups):
+                    tail = jnp.where(places[g], turned[layer][(g - m) % p.groups], tail)
+                reach = 1
+                while reach < p.groups:
+                    tail = tail + pltpu.roll(tail, tiles - reach, 0)
+                    reach *= 2
+                for h in range(p.spare):
+                    at = base + p.full * tiles + h
+                    x_ref[own, at : at + 1, :] = tail[h * p.groups : h * p.groups + 1]
+    for own in range(p.own_cells):
+        x = x_ref[own]
+        weights = weights_ref[own]
+        scale = 0.4 / jnp.sum(weights, axis=-1, keepdims=True)
+        x_high = x.astype(jnp.bfloat16)
+        x_low = (x - x_high.astype(jnp.float32)).astype(jnp.bfloat16)
+        w_high = weights.astype(jnp.bfloat16)
+        w_low = (weights - w_high.astype(jnp.float32)).astype(jnp.bfloat16)
+        dot = functools.partial(jnp.dot, preferred_element_type=jnp.float32)
+        total = dot(w_high, x_high) + (dot(w_high, x_low) + dot(w_low, x_high))
+        all_ref[pl.ds(own, p.all_levels, stride=p.own_cells), :] = 0.6 * x + scale * total
+    me = lax.axis_index("lev")
+    size = p.levels * p.own_cells
+    for s in range(p.layers):
+        layer = lax.rem(me + s, p.layers)
+        out_refs[s][...] = all_ref[pl.ds(pl.multiple_of(layer * size, SUBLANES), size), :]
+
+
+def place_kernel(p, *refs):
+    in_refs, out_ref = refs[: p.layers], refs[p.layers]
+    me = lax.axis_index("lev")
+    for s in range(p.layers):
+        layer = lax.rem(me - s + p.layers, p.layers)
+        for own in range(p.own_cells):
+            out_ref[layer * p.own_cells + own] = in_refs[s][
+                pl.ds(own, p.levels, stride=p.own_cells), :
+            ]
+
+
+def in_vmem(count):
+    return [pl.BlockSpec(memory_space=pltpu.VMEM)] * count
+
+
+def params():
+    return pltpu.CompilerParams(vmem_limit_bytes=VMEM_LIMIT)
+
+
+def by_levels(p, tracers, courant_first, courant_second, weights, frame_flip):
+    f32 = jnp.float32
+    copies = p.tiles * p.full + p.spare
+    packed = pl.pallas_call(
+        functools.partial(pack_kernel, p),
+        out_shape=jax.ShapeDtypeStruct((p.tiles, p.rows, LANES), f32),
+        in_specs=[pl.BlockSpec(memory_space=pl.ANY)]
+        + in_vmem(2)
+        + [pl.BlockSpec(memory_space=pltpu.SMEM)],
+        out_specs=pl.BlockSpec(memory_space=pltpu.VMEM),
+        scratch_shapes=[
+            pltpu.VMEM((p.spare, p.cells, LANES), f32),
+            pltpu.VMEM((LANES, LANES), f32),
+            pltpu.SemaphoreType.DMA((copies,)),
+        ],
+        compiler_params=params(),
+        name="pack",
+    )(
+        tracers.reshape(p.cells, p.levels, p.tracers),
+        courant_first.reshape(p.cells, p.levels),
+        courant_second.reshape(p.cells, p.levels),
+        frame_flip,
+    )
+    dealt = lax.all_to_all(packed, "tile", split_axis=0, concat_axis=0, tiled=True)
+    moved = pl.pallas_call(
+        functools.partial(advect_kernel, p, tile_stride(p.tiles)),
+        out_shape=jax.ShapeDtypeStruct((p.tiles * p.layers * p.back_rows, LANES), f32),
+        in_specs=in_vmem(1),
+        out_specs=pl.BlockSpec(memory_space=pltpu.VMEM),
+        scratch_shapes=[pltpu.VMEM((p.kinds * p.cells, p.tiles, LANES), f32)]
+        + [pltpu.VMEM((p.kinds * 2 * p.cells, p.tiles, LANES), f32)] * 3,
+        compiler_params=params(),
+        name="advect",
+    )(dealt.reshape(p.tiles * p.rows, LANES))
+    columns = lax.all_to_all(
+        moved.reshape(p.tiles * p.layers, p.back_rows, LANES),
+        ("tile", "lev"),
+        split_axis=0,
+        concat_axis=0,
+        tiled=True,
+    )
+    size = p.levels * p.own_cells
+    mixed = pl.pallas_call(
+        functools.partial(mix_kernel, p),
+        out_shape=[jax.ShapeDtypeStruct((size, LANES), f32)] * p.layers,
+        in_specs=in_vmem(2),
+        out_specs=in_vmem(p.layers),
+        scratch_shapes=[
+            pltpu.VMEM((p.own_cells, p.all_levels, LANES), f32),
+            pltpu.VMEM((p.all_levels * p.own_cells, LANES), f32),
+        ],
+        compiler_params=params(),
+        name="mix",
+    )(
+        columns.reshape(p.tiles * p.layers * p.back_rows, LANES),
+        weights.reshape(p.own_cells, p.all_levels, p.all_levels),
+    )
+    pieces = [mixed[0]] + [passed_along(mixed[s], "lev", s) for s in range(1, p.layers)]
+    placed = pl.pallas_call(
+        functools.partial(place_kernel, p),
+        out_shape=jax.ShapeDtypeStruct((p.cells, p.levels, LANES), f32),
+        in_specs=in_vmem(p.layers),
+        out_specs=pl.BlockSpec(memory_space=pltpu.VMEM),
+        compiler_params=params(),
+        name="place",
+    )(*pieces)
+    return placed.reshape(tracers.shape)
+
+
+def on_device(tracers, courant_first, courant_second, weights, frame_flip):
+    plan = Plan(
+        tracers.shape[1],
+        tracers.shape[3],
+        tracers.shape[4],
+        lax.axis_size("tile"),
+        lax.axis_size("lev"),
+    )
+    if tracers.shape[1] == tracers.shape[2] and tracers.shape[0] == 1 and plan.fits:
+        return by_levels(plan, tracers, courant_first, courant_second, weights, frame_flip)
+    return by_halos(tracers, courant_first, courant_second, weights, frame_flip)
 
 
 def solution(mesh):

time: 133 us -> 61.1 us (0.46)
  waiting for transfers between devices: 64.3 us -> 9.8 us
  starting transfers between devices: 24.7 us -> 5.3 us
  blocking collectives: 17.8 us -> 36.5 us
  other arithmetic: 17.4 us -> 0 us
  Pallas kernels: 0 us -> 6.32 us
  local copies, waits for them, and re-layouts: 5.39 us -> 2.76 us
  between operations: 1.74 us -> 0.07 us
    ppermute x14 -> x3, waiting for transfers between devices: 48.6 us -> 9.8 us  [passed_along(): return lax.ppermute(value, axis, pairs)]
    all_to_all x1 -> x2, blocking collectives: 17.8 us -> 36.5 us  [the longest x1 20.7 us: by_levels(): lax.all_to_all(moved.reshape(p.tiles * p.layers, p.back_rows, LANES), ('t...]
    all_to_all x1 -> x0, waiting for transfers between devices: 15.7 us -> none  [on_device(): lax.all_to_all(advected, 'lev', split_axis=1, concat_axis=3, tiled=True)]
    ppermute x14 -> x3, starting transfers between devices: 20 us -> 5.3 us  [passed_along(): return lax.ppermute(value, axis, pairs)]
    select_n x10 -> x0, other arithmetic: 12.2 us -> none  [the longest x6 9.72 us: ppm_update(): fluxes = jnp.where(courant >= 0.0, upward, downward)]
    pallas_call x0 -> x4, Pallas kernels: none -> 6.32 us  [the longest x1 3.76 us: by_levels(): pl.pallas_call(functools.partial(advect_kernel, p, tile_stride(p.tiles)),...]
    all_to_all x1 -> x0, starting transfers between devices: 4.7 us -> none  [on_device(): lax.all_to_all(advected, 'lev', split_axis=1, concat_axis=3, tiled=True)]
    slice x9 -> x0, local copies, waits for them, and re-layouts: 2.37 us -> none  [the longest x1 1.31 us: to_frame(): second_flag = (flip_flags[:, 1] == 1)[:, None, None, None, None]]
  transfers between devices with their start and end apart: 15 -> 3, of which waited for: 10 -> 2; matrix products, arithmetic and copies ran while one was open for 4% -> 0% of each run, Pallas kernels for 0% -> 0%
where the time goes in v1:
time: 61.1 us; the launch traced here: 60.7 us
  blocking collectives  36.5 us (60%)
  waiting for transfers between devices  9.8 us (16%)
  Pallas kernels  6.32 us (10%)
  starting transfers between devices  5.3 us (9%)
  local copies, waits for them, and re-layouts  2.76 us (5%)
    all_to_all x1, blocking collectives, by_levels(): lax.all_to_all(moved.reshape(p.tiles * p.layers, p.back_rows, LANES), ('t...  20.7 us
    all_to_all x1, blocking collectives, by_levels(): lax.all_to_all(packed, 'tile', split_axis=0, concat_axis=0, tiled=True)  15.8 us
    ppermute x3, waiting for transfers between devices, passed_along(): return lax.ppermute(value, axis, pairs)  9.8 us
    ppermute x3, starting transfers between devices, passed_along(): return lax.ppermute(value, axis, pairs)  5.3 us
    pallas_call x1, Pallas kernels, by_levels(): pl.pallas_call(functools.partial(advect_kernel, p, tile_stride(p.tiles)),...  3.76 us
    unnamed x9, local copies, waits for them, and re-layouts  1.84 us
    pallas_call x1, Pallas kernels, by_levels(): pl.pallas_call(functools.partial(pack_kernel, p), out_shape=jax.ShapeDtyp...  1.35 us
  transfers between devices with their start and end apart: 3, of which 2 were waited for; matrix products, arithmetic and copies ran while one was open for 0% of the time, Pallas kernels for 0%

profile of v1, /device:TPU:0, one launch (start us, length us, event | category | flops | bytes accessed | tf_op | source)
XLA Modules:
  0.0 60.7 jit_solution(10631121433561790808)
XLA Ops:
  0.0 0.0 copy-start.2
  0.0 0.0 copy-start.1
  0.0 1.2 %copy.6 = f32[1,8,8,18,128]{4,3,2,1,0:T(8,128)S(1)} copy(f32[1,8,8,18,128]{4,2,3,1,0:T(8,128)} %param.5) | data formatting | bytes 1179648 | tf_op args[0]
  1.2 0.0 copy-start.3
  1.2 0.0 copy-done.2
  1.2 0.0 copy-done.1
  1.2 0.6 %copy-done.3 = s32[1,2]{1,0:T(1,128)S(1)} copy-done((s32[1,2]{1,0:T(1,128)S(1)}, s32[1,2]{1,0:T(1,128)}, u32[]{:S(2)}) %copy-start.3) | copy-done | bytes 32
  1.9 1.3 %pack.1 = f32[8,152,128]{2,1,0:T(8,128)S(1)} custom-call(f32[64,18,128]{2,1,0:T(8,128)S(1)} %bitcast.9, f32[64,18]{1,0:T(8,128)S(1)} %bitcast.14, f32[64,18]{1,0:T(8,128)S(1)} %bitcast.15, s32[1,2]{1,0:T(1,128)S(1)} %copy-done.3), custom_call_target="tpu_custom_call" | custom-call | tf_op jit(solution)/shard_map/pack/pallas_call | solution.py:378
  3.2 15.8 %all_to_all.10 = f32[8,152,128]{2,1,0:T(8,128)S(1)} all-to-all(f32[8,152,128]{2,1,0:T(8,128)S(1)} %pack.1), channel_id=1, replica_groups=mesh['tile'=8,'lev'=4] {'tile'}, dimensions={0} | all-to-all | bytes 1245184 | tf_op jit(solution)/shard_map/all_to_all | solution.py:398
  19.0 3.8 %advect.1 = f32[1280,128]{1,0:T(8,128)S(1)} custom-call(f32[1216,128]{1,0:T(8,128)S(1)} %bitcast.12), custom_call_target="tpu_custom_call" | custom-call | tf_op jit(solution)/shard_map/advect/pallas_call | solution.py:399
  22.8 0.0 copy-start
  22.8 20.7 %all_to_all.11 = f32[32,40,128]{2,1,0:T(8,128)S(1)} all-to-all(f32[32,40,128]{2,1,0:T(8,128)S(1)} %bitcast.11), channel_id=1, replica_groups=mesh['tile'=8,'lev'=4] {'tile','lev'}, dimensions={0} | all-to-all | bytes 1310720 | tf_op jit(solution)/shard_map/all_to_all | solution.py:409
  43.5 0.0 copy-done
  43.5 1.0 %mix.1 = (f32[288,128]{1,0:T(8,128)S(1)}, f32[288,128]{1,0:T(8,128)S(1)}, f32[288,128]{1,0:T(8,128)S(1)}, f32[288,128]{1,0:T(8,128)S(1)}) custom-call(f32[1280,128]{1,0:T(8,128)S(1)} %bitcast.10, f32[16,72,72]{2,1,0:T(8,128)S(1)} %bitcast.13), custom_call_target="tpu_custom_call" | custom-call | tf_op jit(solution)/shard_map/mix/pallas_call | solution.py:417
  44.5 2.9 %collective-permute-start = (f32[288,128]{1,0:T(8,128)S(1)}, f32[288,128]{1,0:T(8,128)S(1)}, u32[]{:S(2)}, u32[]{:S(2)}) collective-permute-start(f32[288,128]{1,0:T(8,128)S(1)} %get-tuple-element.10), channel_id=1, source_target_pairs={{0,1},{1,2},{2,3},{3,0},{4,5},{5,6},{6,7},{7,4},{8,9},{9,10},{10,1... | collective-permute-start | bytes 442376 | tf_op jit(solution)/shard_map/ppermute | solution.py:19
  47.3 0.8 %collective-permute-start.1 = (f32[288,128]{1,0:T(8,128)S(1)}, f32[288,128]{1,0:T(8,128)S(1)}, u32[]{:S(2)}, u32[]{:S(2)}) collective-permute-start(f32[288,128]{1,0:T(8,128)S(1)} %get-tuple-element.11), channel_id=1, source_target_pairs={{0,2},{1,3},{2,0},{3,1},{4,6},{5,7},{6,4},{7,5},{8,10},{9,11},{10,... | collective-permute-start | bytes 442376 | tf_op jit(solution)/shard_map/ppermute | solution.py:19
  48.1 1.6 %collective-permute-start.2 = (f32[288,128]{1,0:T(8,128)S(1)}, f32[288,128]{1,0:T(8,128)S(1)}, u32[]{:S(2)}, u32[]{:S(2)}) collective-permute-start(f32[288,128]{1,0:T(8,128)S(1)} %get-tuple-element.12), channel_id=1, source_target_pairs={{0,3},{1,0},{2,1},{3,2},{4,7},{5,4},{6,5},{7,6},{8,11},{9,8},{10,9... | collective-permute-start | bytes 442376 | tf_op jit(solution)/shard_map/ppermute | solution.py:19
  49.8 3.1 %collective-permute-done.refs_1_ = f32[288,128]{1,0:T(8,128)S(1)} collective-permute-done((f32[288,128]{1,0:T(8,128)S(1)}, f32[288,128]{1,0:T(8,128)S(1)}, u32[]{:S(2)}, u32[]{:S(2)}) %collective-permute-start) | collective-permute-done | bytes 147488 | tf_op jit(solution)/shard_map/ppermute | solution.py:19
  52.9 6.7 %collective-permute-done.1.refs_2_ = f32[288,128]{1,0:T(8,128)S(1)} collective-permute-done((f32[288,128]{1,0:T(8,128)S(1)}, f32[288,128]{1,0:T(8,128)S(1)}, u32[]{:S(2)}, u32[]{:S(2)}) %collective-permute-start.1) | collective-permute-done | bytes 147488 | tf_op jit(solution)/shard_map/ppermute | solution.py:19
  59.6 0.0 collective-permute-done.2.refs_3_
  59.6 0.2 place.1
  59.8 0.9 %copy.7 = f32[1,8,8,18,128]{4,2,3,1,0:T(8,128)} copy(f32[1,8,8,18,128]{4,3,2,1,0:T(8,128)S(1)} %bitcast.8) | data formatting | bytes 1179648 | tf_op jit(solution)/shard_map/reshape | solution.py:441
Async XLA Ops:
  0.0 1.2 %copy-start.2 = (f32[1,8,8,18]{3,2,1,0:T(8,128)S(1)}, f32[1,8,8,18]{3,2,1,0:T(8,128)}, u32[]{:S(2)}) copy-start(f32[1,8,8,18]{3,2,1,0:T(8,128)} %param.7) | copy-start | bytes 13828
  0.0 1.2 %copy-start.1 = (f32[1,8,8,18]{3,2,1,0:T(8,128)S(1)}, f32[1,8,8,18]{3,2,1,0:T(8,128)}, u32[]{:S(2)}) copy-start(f32[1,8,8,18]{3,2,1,0:T(8,128)} %param.6) | copy-start | bytes 13828
  1.2 0.7 %copy-start.3 = (s32[1,2]{1,0:T(1,128)S(1)}, s32[1,2]{1,0:T(1,128)}, u32[]{:S(2)}) copy-start(s32[1,2]{1,0:T(1,128)} %flip_ref.1) | copy-start | bytes 28
  22.8 20.7 %copy-start = (f32[1,2,8,72,72]{4,3,2,1,0:T(8,128)S(1)}, f32[1,2,8,72,72]{4,3,2,1,0:T(8,128)}, u32[]{:S(2)}) copy-start(f32[1,2,8,72,72]{4,3,2,1,0:T(8,128)} %param.8) | copy-start | bytes 995332
  44.5 8.4 %collective-permute-start = (f32[288,128]{1,0:T(8,128)S(1)}, f32[288,128]{1,0:T(8,128)S(1)}, u32[]{:S(2)}, u32[]{:S(2)}) collective-permute-start(f32[288,128]{1,0:T(8,128)S(1)} %get-tuple-element.10), channel_id=1, source_target_pairs={{0,1},{1,2},{2,3},{3,0},{4,5},{5,6},{6,7},{7,4},{8,9},{9,10},{10,1... | collective-permute-start | bytes 442376 | tf_op jit(solution)/shard_map/ppermute | solution.py:19
  47.3 12.2 %collective-permute-start.1 = (f32[288,128]{1,0:T(8,128)S(1)}, f32[288,128]{1,0:T(8,128)S(1)}, u32[]{:S(2)}, u32[]{:S(2)}) collective-permute-start(f32[288,128]{1,0:T(8,128)S(1)} %get-tuple-element.11), channel_id=1, source_target_pairs={{0,2},{1,3},{2,0},{3,1},{4,6},{5,7},{6,4},{7,5},{8,10},{9,11},{10,... | collective-permute-start | bytes 442376 | tf_op jit(solution)/shard_map/ppermute | solution.py:19
  48.1 11.5 %collective-permute-start.2 = (f32[288,128]{1,0:T(8,128)S(1)}, f32[288,128]{1,0:T(8,128)S(1)}, u32[]{:S(2)}, u32[]{:S(2)}) collective-permute-start(f32[288,128]{1,0:T(8,128)S(1)} %get-tuple-element.12), channel_id=1, source_target_pairs={{0,3},{1,0},{2,1},{3,2},{4,7},{5,4},{6,5},{7,6},{8,11},{9,8},{10,9... | collective-permute-start | bytes 442376 | tf_op jit(solution)/shard_map/ppermute | solution.py:19

commit v2 on v1

--- a/solution.py
+++ b/solution.py
@@ -134,6 +134,9 @@
             self.cells % self.groups == 0
             and self.own_cells % self.groups == 0
             and self.part_rows % SUBLANES == 0
+            and self.side == SUBLANES
+            and self.own_cells % side == 0
+            and self.kinds < SUBLANES
         )
 
 
@@ -141,58 +144,67 @@
     return lax.broadcasted_iota(jnp.int32, shape, 1) // width
 
 
-def pack_kernel(p, x_ref, first_ref, second_ref, flip_ref, out_ref, spare_ref, faces_ref, sems):
+def pack_kernel(
+    p, x_ref, first_ref, second_ref, flip_ref, out_ref, spare_ref, courant_ref, flags_ref, faces_ref, sems
+):
     copies = []
+
+    def fetch(source, target):
+        copy = pltpu.make_async_copy(source, target, sems.at[len(copies)])
+        copy.start()
+        copies.append(copy)
+
+    for source, target in ((first_ref, courant_ref.at[0]), (second_ref, courant_ref.at[1])):
+        fetch(source, target)
+    fetch(flip_ref, flags_ref)
+    for h in range(p.spare):
+        fetch(x_ref.at[:, p.full * p.tiles + h], spare_ref.at[h])
+    small = 3
     for d in range(p.tiles):
         for f in range(p.full):
-            copies.append(
-                pltpu.make_async_copy(
-                    x_ref.at[:, p.full * d + f, :],
-                    out_ref.at[d, pl.ds(f * p.cells, p.cells), :],
-                    sems.at[len(copies)],
-                )
+            fetch(
+                x_ref.at[:, p.full * d + f],
+                out_ref.at[d, pl.ds(f * p.side, p.side)],
             )
-    spares = []
+    filler = jnp.zeros((p.side, LANES), jnp.float32)
+    group = lane_group((p.side, LANES), p.width)
+    for copy in copies[small : small + p.spare]:
+        copy.wait()
+    tall = p.part_rows // p.side
     for h in range(p.spare):
-        spares.append(
-            pltpu.make_async_copy(
-                x_ref.at[:, p.full * p.tiles + h, :],
-                spare_ref.at[h],
-                sems.at[len(copies) + h],
-            )
-        )
-    for copy in spares + copies:
-        copy.start()
-    faces_ref[...] = jnp.zeros_like(faces_ref)
-    faces_ref[: p.cells, : p.levels] = first_ref[...]
-    faces_ref[p.cells :, : p.levels] = second_ref[...]
+        for g in range(p.groups):
+            for r in range(tall):
+                rows = None
+                for m in range(p.groups):
+                    part = spare_ref[h, m * tall + r]
+                    shift = (m - g) * p.width % LANES
+                    moved = pltpu.roll(part, shift, 1) if shift else part
+                    rows = moved if rows is None else jnp.where(group == m, moved, rows)
+                out_ref[h * p.groups + g, p.full * p.side + r] = rows
+    for copy in copies[:small]:
+        copy.wait()
+    for way in range(2):
+        for i in range(p.side):
+            at = way * p.cells + i * p.side
+            faces_ref[at : at + p.side, :] = filler
+            faces_ref[at : at + p.side, : p.levels] = courant_ref[way, i]
     faces = faces_ref[...].T
     lane = lax.broadcasted_iota(jnp.int32, (1, LANES), 1)
-    first_flip = jnp.full((1, LANES), flip_ref[0, 0]).astype(jnp.float32)
-    second_flip = jnp.full((1, LANES), flip_ref[0, 1]).astype(jnp.float32)
-    flips = jnp.where(lane < p.cells, first_flip, second_flip)
-    filler = jnp.zeros((p.rows - p.flip_at - 1, LANES), jnp.float32)
+    flags = flags_ref[...].astype(jnp.float32)
+    flips = jnp.where(
+        lane < p.cells,
+        jnp.broadcast_to(flags[:, 0:1], (1, LANES)),
+        jnp.broadcast_to(flags[:, 1:2], (1, LANES)),
+    )
+    last = p.courant_at // SUBLANES
     for d in range(p.tiles):
         level = p.full * d
-        out_ref[d, p.courant_at : p.courant_at + p.full, :] = faces[level : level + p.full]
         rest = p.full * p.tiles + d // p.groups
-        out_ref[d, p.courant_at + p.full : p.flip_at, :] = faces[rest : rest + 1]
-        out_ref[d, p.flip_at : p.flip_at + 1, :] = flips
-        if p.rows > p.flip_at + 1:
-            out_ref[d, p.flip_at + 1 :, :] = filler
-    for copy in spares:
-        copy.wait()
-    group = lane_group((p.part_rows, LANES), p.width)
-    for h in range(p.spare):
-        parts = [spare_ref[h, m * p.part_rows : (m + 1) * p.part_rows, :] for m in range(p.groups)]
-        for g in range(p.groups):
-            rows = None
-            for m in range(p.groups):
-                shift = (m - g) * p.width % LANES
-                moved = pltpu.roll(parts[m], shift, 1) if shift else parts[m]
-                rows = moved if rows is None else jnp.where(group == m, moved, rows)
-            out_ref[h * p.groups + g, p.tail_at : p.tail_at + p.part_rows, :] = rows
-    for copy in copies:
+        out_ref[d, last] = filler
+        out_ref[d, last, : p.full, :] = faces[level : level + p.full]
+        out_ref[d, last, p.full : p.kinds, :] = faces[rest : rest + 1]
+        out_ref[d, last, p.kinds : p.kinds + 1, :] = flips
+    for copy in copies[small + p.spare :]:
         copy.wait()
 
 
@@ -356,12 +368,13 @@
 def place_kernel(p, *refs):
     in_refs, out_ref = refs[: p.layers], refs[p.layers]
     me = lax.axis_index("lev")
+    tall = p.own_cells // p.side
     for s in range(p.layers):
         layer = lax.rem(me - s + p.layers, p.layers)
-        for own in range(p.own_cells):
-            out_ref[layer * p.own_cells + own] = in_refs[s][
-                pl.ds(own, p.levels, stride=p.own_cells), :
-            ]
+        for level in range(p.levels):
+            for r in range(tall):
+                at = level * p.own_cells + r * p.side
+                out_ref[layer * tall + r, level] = in_refs[s][at : at + p.side, :]
 
 
 def in_vmem(count):
@@ -374,26 +387,31 @@
 
 def by_levels(p, tracers, courant_first, courant_second, weights, frame_flip):
     f32 = jnp.float32
-    copies = p.tiles * p.full + p.spare
+    across = (p.side, p.levels, p.side, p.tracers)
     packed = pl.pallas_call(
         functools.partial(pack_kernel, p),
-        out_shape=jax.ShapeDtypeStruct((p.tiles, p.rows, LANES), f32),
-        in_specs=[pl.BlockSpec(memory_space=pl.ANY)]
-        + in_vmem(2)
-        + [pl.BlockSpec(memory_space=pltpu.SMEM)],
+        out_shape=jax.ShapeDtypeStruct((p.tiles, p.rows // p.side, p.side, LANES), f32),
+        in_specs=[pl.BlockSpec(memory_space=pltpu.HBM)] * 4,
         out_specs=pl.BlockSpec(memory_space=pltpu.VMEM),
         scratch_shapes=[
-            pltpu.VMEM((p.spare, p.cells, LANES), f32),
+            pltpu.VMEM((p.spare, p.side, p.side, LANES), f32),
+            pltpu.VMEM((2, p.side, p.side, p.levels), f32),
+            pltpu.VMEM((1, 2), jnp.int32),
             pltpu.VMEM((LANES, LANES), f32),
-            pltpu.SemaphoreType.DMA((copies,)),
+            pltpu.SemaphoreType.DMA((3 + p.tiles * p.full + p.spare,)),
         ],
         compiler_params=params(),
         name="pack",
     )(
-        tracers.reshape(p.cells, p.levels, p.tracers),
-        courant_first.reshape(p.cells, p.levels),
-        courant_second.reshape(p.cells, p.levels),
-        frame_flip,
+        *(
+            pltpu.with_memory_space_constraint(value, pltpu.HBM)
+            for value in (
+                tracers[0].transpose(0, 2, 1, 3),
+                courant_first[0],
+                courant_second[0],
+                frame_flip,
+            )
+        )
     )
     dealt = lax.all_to_all(packed, "tile", split_axis=0, concat_axis=0, tiled=True)
     moved = pl.pallas_call(
@@ -432,13 +450,13 @@
     pieces = [mixed[0]] + [passed_along(mixed[s], "lev", s) for s in range(1, p.layers)]
     placed = pl.pallas_call(
         functools.partial(place_kernel, p),
-        out_shape=jax.ShapeDtypeStruct((p.cells, p.levels, LANES), f32),
+        out_shape=jax.ShapeDtypeStruct(across, f32),
         in_specs=in_vmem(p.layers),
         out_specs=pl.BlockSpec(memory_space=pltpu.VMEM),
         compiler_params=params(),
         name="place",
     )(*pieces)
-    return placed.reshape(tracers.shape)
+    return placed.transpose(0, 2, 1, 3)[None]
 
 
 def on_device(tracers, courant_first, courant_second, weights, frame_flip):

time: 61.1 us -> 58.9 us (0.964)
  local copies, waits for them, and re-layouts: 2.76 us -> 0.01 us
    unnamed x9 -> x2, local copies, waits for them, and re-layouts: 1.84 us -> 0.01 us
    reshape x1 -> x0, local copies, waits for them, and re-layouts: 0.92 us -> none  [by_levels(): return placed.reshape(tracers.shape)]
    pallas_call x1, Pallas kernels: 0.19 us -> 0.87 us  [by_levels(): pl.pallas_call(functools.partial(place_kernel, p), out_shape=jax.ShapeDty...]
where the time goes in v2:
time: 58.9 us; the launch traced here: 58.5 us
  blocking collectives  36.5 us (62%)
  waiting for transfers between devices  9.79 us (17%)
  Pallas kernels  6.88 us (12%)
  starting transfers between devices  5.31 us (9%)
    all_to_all x1, blocking collectives, by_levels(): lax.all_to_all(moved.reshape(p.tiles * p.layers, p.back_rows, LANES), ('t...  20.7 us
    all_to_all x1, blocking collectives, by_levels(): lax.all_to_all(packed, 'tile', split_axis=0, concat_axis=0, tiled=True)  15.8 us
    ppermute x3, waiting for transfers between devices, passed_along(): return lax.ppermute(value, axis, pairs)  9.79 us
    ppermute x3, starting transfers between devices, passed_along(): return lax.ppermute(value, axis, pairs)  5.31 us
    pallas_call x1, Pallas kernels, by_levels(): pl.pallas_call(functools.partial(advect_kernel, p, tile_stride(p.tiles)),...  3.76 us
    pallas_call x1, Pallas kernels, by_levels(): pl.pallas_call(functools.partial(pack_kernel, p), out_shape=jax.ShapeDtyp...  1.25 us
  transfers between devices with their start and end apart: 3, of which 2 were waited for; matrix products, arithmetic and copies ran while one was open for 0% of the time, Pallas kernels for 0%

profile of v2, /device:TPU:0, one launch (start us, length us, event | category | flops | bytes accessed | tf_op | source)
XLA Modules:
  0.0 58.5 jit_solution(7497349134482936385)
XLA Ops:
  0.0 1.2 %pack.1 = f32[8,19,8,128]{3,2,1,0:T(8,128)S(1)} custom-call(f32[8,18,8,128]{3,2,1,0:T(8,128)} %bitcast.16, f32[8,8,18]{2,1,0:T(8,128)} %bitcast.17, f32[8,8,18]{2,1,0:T(8,128)} %bitcast.18, s32[1,2]{1,0:T(1,128)} %flip_ref.1), custom_call_target="tpu_custom_call" | custom-call | tf_op jit(solution)/shard_map/pack/pallas_call | solution.py:391
  1.3 15.8 %all_to_all.10 = f32[8,19,8,128]{3,2,1,0:T(8,128)S(1)} all-to-all(f32[8,19,8,128]{3,2,1,0:T(8,128)S(1)} %pack.1), channel_id=1, replica_groups=mesh['tile'=8,'lev'=4] {'tile'}, dimensions={0} | all-to-all | bytes 1245184 | tf_op jit(solution)/shard_map/all_to_all | solution.py:416
  17.0 3.8 %advect.1 = f32[1280,128]{1,0:T(8,128)S(1)} custom-call(f32[1216,128]{1,0:T(8,128)S(1)} %bitcast.14), custom_call_target="tpu_custom_call" | custom-call | tf_op jit(solution)/shard_map/advect/pallas_call | solution.py:417
  20.8 0.0 copy-start
  20.8 20.7 %all_to_all.11 = f32[32,40,128]{2,1,0:T(8,128)S(1)} all-to-all(f32[32,40,128]{2,1,0:T(8,128)S(1)} %bitcast.13), channel_id=1, replica_groups=mesh['tile'=8,'lev'=4] {'tile','lev'}, dimensions={0} | all-to-all | bytes 1310720 | tf_op jit(solution)/shard_map/all_to_all | solution.py:427
  41.5 0.0 copy-done
  41.5 1.0 %mix.1 = (f32[288,128]{1,0:T(8,128)S(1)}, f32[288,128]{1,0:T(8,128)S(1)}, f32[288,128]{1,0:T(8,128)S(1)}, f32[288,128]{1,0:T(8,128)S(1)}) custom-call(f32[1280,128]{1,0:T(8,128)S(1)} %bitcast.12, f32[16,72,72]{2,1,0:T(8,128)S(1)} %bitcast.15), custom_call_target="tpu_custom_call" | custom-call | tf_op jit(solution)/shard_map/mix/pallas_call | solution.py:435
  42.5 2.9 %collective-permute-start = (f32[288,128]{1,0:T(8,128)S(1)}, f32[288,128]{1,0:T(8,128)S(1)}, u32[]{:S(2)}, u32[]{:S(2)}) collective-permute-start(f32[288,128]{1,0:T(8,128)S(1)} %get-tuple-element.10), channel_id=1, source_target_pairs={{0,1},{1,2},{2,3},{3,0},{4,5},{5,6},{6,7},{7,4},{8,9},{9,10},{10,1... | collective-permute-start | bytes 442376 | tf_op jit(solution)/shard_map/ppermute | solution.py:19
  45.4 0.8 %collective-permute-start.1 = (f32[288,128]{1,0:T(8,128)S(1)}, f32[288,128]{1,0:T(8,128)S(1)}, u32[]{:S(2)}, u32[]{:S(2)}) collective-permute-start(f32[288,128]{1,0:T(8,128)S(1)} %get-tuple-element.11), channel_id=1, source_target_pairs={{0,2},{1,3},{2,0},{3,1},{4,6},{5,7},{6,4},{7,5},{8,10},{9,11},{10,... | collective-permute-start | bytes 442376 | tf_op jit(solution)/shard_map/ppermute | solution.py:19
  46.2 1.7 %collective-permute-start.2 = (f32[288,128]{1,0:T(8,128)S(1)}, f32[288,128]{1,0:T(8,128)S(1)}, u32[]{:S(2)}, u32[]{:S(2)}) collective-permute-start(f32[288,128]{1,0:T(8,128)S(1)} %get-tuple-element.12), channel_id=1, source_target_pairs={{0,3},{1,0},{2,1},{3,2},{4,7},{5,4},{6,5},{7,6},{8,11},{9,8},{10,9... | collective-permute-start | bytes 442376 | tf_op jit(solution)/shard_map/ppermute | solution.py:19
  47.8 3.1 %collective-permute-done.refs_1_ = f32[288,128]{1,0:T(8,128)S(1)} collective-permute-done((f32[288,128]{1,0:T(8,128)S(1)}, f32[288,128]{1,0:T(8,128)S(1)}, u32[]{:S(2)}, u32[]{:S(2)}) %collective-permute-start) | collective-permute-done | bytes 147488 | tf_op jit(solution)/shard_map/ppermute | solution.py:19
  50.9 6.7 %collective-permute-done.1.refs_2_ = f32[288,128]{1,0:T(8,128)S(1)} collective-permute-done((f32[288,128]{1,0:T(8,128)S(1)}, f32[288,128]{1,0:T(8,128)S(1)}, u32[]{:S(2)}, u32[]{:S(2)}) %collective-permute-start.1) | collective-permute-done | bytes 147488 | tf_op jit(solution)/shard_map/ppermute | solution.py:19
  57.6 0.0 collective-permute-done.2.refs_3_
  57.6 0.9 %place.1 = f32[8,18,8,128]{3,2,1,0:T(8,128)} custom-call(f32[288,128]{1,0:T(8,128)S(1)} %get-tuple-element.9.refs_0_, f32[288,128]{1,0:T(8,128)S(1)} %collective-permute-done.refs_1_, f32[288,128]{1,0:T(8,128)S(1)} %collective-permute-done.1.refs_2_, f32[288,128]{1,0:T(8,128)S(1)} %collective-permute-done.2.refs_3_), custom_call_target="tpu_custom_call" | custom-call | tf_op jit(solution)/shard_map/place/pallas_call | solution.py:451
Async XLA Ops:
  20.8 20.7 %copy-start = (f32[1,2,8,72,72]{4,3,2,1,0:T(8,128)S(1)}, f32[1,2,8,72,72]{4,3,2,1,0:T(8,128)}, u32[]{:S(2)}) copy-start(f32[1,2,8,72,72]{4,3,2,1,0:T(8,128)} %param.8) | copy-start | bytes 995332
  42.5 8.4 %collective-permute-start = (f32[288,128]{1,0:T(8,128)S(1)}, f32[288,128]{1,0:T(8,128)S(1)}, u32[]{:S(2)}, u32[]{:S(2)}) collective-permute-start(f32[288,128]{1,0:T(8,128)S(1)} %get-tuple-element.10), channel_id=1, source_target_pairs={{0,1},{1,2},{2,3},{3,0},{4,5},{5,6},{6,7},{7,4},{8,9},{9,10},{10,1... | collective-permute-start | bytes 442376 | tf_op jit(solution)/shard_map/ppermute | solution.py:19
  45.4 12.2 %collective-permute-start.1 = (f32[288,128]{1,0:T(8,128)S(1)}, f32[288,128]{1,0:T(8,128)S(1)}, u32[]{:S(2)}, u32[]{:S(2)}) collective-permute-start(f32[288,128]{1,0:T(8,128)S(1)} %get-tuple-element.11), channel_id=1, source_target_pairs={{0,2},{1,3},{2,0},{3,1},{4,6},{5,7},{6,4},{7,5},{8,10},{9,11},{10,... | collective-permute-start | bytes 442376 | tf_op jit(solution)/shard_map/ppermute | solution.py:19
  46.2 11.5 %collective-permute-start.2 = (f32[288,128]{1,0:T(8,128)S(1)}, f32[288,128]{1,0:T(8,128)S(1)}, u32[]{:S(2)}, u32[]{:S(2)}) collective-permute-start(f32[288,128]{1,0:T(8,128)S(1)} %get-tuple-element.12), channel_id=1, source_target_pairs={{0,3},{1,0},{2,1},{3,2},{4,7},{5,4},{6,5},{7,6},{8,11},{9,8},{10,9... | collective-permute-start | bytes 442376 | tf_op jit(solution)/shard_map/ppermute | solution.py:19

commit v3 on v2

--- a/solution.py
+++ b/solution.py
@@ -67,6 +67,11 @@
     totals = jnp.sum(weights, axis=-1, keepdims=True)
     identity = jnp.eye(weights.shape[-1], dtype=jnp.float32)
     return 0.6 * identity + 0.4 * (weights / totals)
+
+
+def swapped(value, axis, mask):
+    pairs = [(source, source ^ mask) for source in range(lax.axis_size(axis))]
+    return lax.ppermute(value, axis, pairs)
 
 
 def tile_stride(tiles):
@@ -144,9 +149,15 @@
     return lax.broadcasted_iota(jnp.int32, shape, 1) // width
 
 
-def pack_kernel(
-    p, x_ref, first_ref, second_ref, flip_ref, out_ref, spare_ref, courant_ref, flags_ref, faces_ref, sems
-):
+def pack_kernel(p, x_ref, first_ref, second_ref, flip_ref, *refs):
+    chips = p.tiles // 2
+    own_refs, other_ref = refs[:chips], refs[chips]
+    spare_ref, courant_ref, flags_ref, faces_ref, rest_ref, sems = refs[chips + 1 :]
+    me = lax.axis_index("tile")
+    slots = []
+    for s in range(chips):
+        slots.append((lax.bitwise_xor(me, 2 * s), own_refs[s]))
+        slots.append((lax.bitwise_xor(me, 2 * s + 1), other_ref.at[s]))
     copies = []
 
     def fetch(source, target):
@@ -160,12 +171,9 @@
     for h in range(p.spare):
         fetch(x_ref.at[:, p.full * p.tiles + h], spare_ref.at[h])
     small = 3
-    for d in range(p.tiles):
+    for d, slot in slots:
         for f in range(p.full):
-            fetch(
-                x_ref.at[:, p.full * d + f],
-                out_ref.at[d, pl.ds(f * p.side, p.side)],
-            )
+            fetch(x_ref.at[:, p.full * d + f], slot.at[pl.ds(f * p.side, p.side)])
     filler = jnp.zeros((p.side, LANES), jnp.float32)
     group = lane_group((p.side, LANES), p.width)
     for copy in copies[small : small + p.spare]:
@@ -180,7 +188,7 @@
                     shift = (m - g) * p.width % LANES
                     moved = pltpu.roll(part, shift, 1) if shift else part
                     rows = moved if rows is None else jnp.where(group == m, moved, rows)
-                out_ref[h * p.groups + g, p.full * p.side + r] = rows
+                rest_ref[h * p.groups + g, r] = rows
     for copy in copies[:small]:
         copy.wait()
     for way in range(2):
@@ -196,21 +204,33 @@
         jnp.broadcast_to(flags[:, 0:1], (1, LANES)),
         jnp.broadcast_to(flags[:, 1:2], (1, LANES)),
     )
-    last = p.courant_at // SUBLANES
     for d in range(p.tiles):
         level = p.full * d
         rest = p.full * p.tiles + d // p.groups
-        out_ref[d, last] = filler
-        out_ref[d, last, : p.full, :] = faces[level : level + p.full]
-        out_ref[d, last, p.full : p.kinds, :] = faces[rest : rest + 1]
-        out_ref[d, last, p.kinds : p.kinds + 1, :] = flips
+        rest_ref[d, tall] = filler
+        rest_ref[d, tall, : p.full, :] = faces[level : level + p.full]
+        rest_ref[d, tall, p.full : p.kinds, :] = faces[rest : rest + 1]
+        rest_ref[d, tall, p.kinds : p.kinds + 1, :] = flips
+    for d, slot in slots:
+        for r in range(tall + 1):
+            slot[p.full * p.side + r] = rest_ref[d, r]
     for copy in copies[small + p.spare :]:
         copy.wait()
 
 
-def advect_kernel(p, stride, in_ref, out_ref, q_ref, near_ref, far_ref, mid_ref):
+def advect_kernel(p, stride, *refs):
     tiles, side, cells = p.tiles, p.side, p.cells
     shape = (tiles, LANES)
+    parts = refs[: -6]
+    out_ref, in_ref, q_ref, near_ref, far_ref, mid_ref = refs[-6:]
+    me = lax.axis_index("tile")
+    each = tiles // len(parts)
+    for s, part in enumerate(parts):
+        for e in range(each):
+            tile = lax.bitwise_xor(me, s * each + e)
+            in_ref[pl.ds(pl.multiple_of(tile * p.rows, SUBLANES), p.rows), :] = part[
+                e * p.rows : (e + 1) * p.rows, :
+            ]
 
     def row(at):
         return in_ref[pl.ds(at, tiles, stride=p.rows), :]
@@ -388,16 +408,20 @@
 def by_levels(p, tracers, courant_first, courant_second, weights, frame_flip):
     f32 = jnp.float32
     across = (p.side, p.levels, p.side, p.tracers)
-    packed = pl.pallas_call(
+    chips = p.tiles // 2
+    blocks = (p.rows // p.side, p.side, LANES)
+    *own, other = pl.pallas_call(
         functools.partial(pack_kernel, p),
-        out_shape=jax.ShapeDtypeStruct((p.tiles, p.rows // p.side, p.side, LANES), f32),
+        out_shape=[jax.ShapeDtypeStruct(blocks, f32)] * chips
+        + [jax.ShapeDtypeStruct((chips,) + blocks, f32)],
         in_specs=[pl.BlockSpec(memory_space=pltpu.HBM)] * 4,
-        out_specs=pl.BlockSpec(memory_space=pltpu.VMEM),
+        out_specs=in_vmem(chips + 1),
         scratch_shapes=[
             pltpu.VMEM((p.spare, p.side, p.side, LANES), f32),
             pltpu.VMEM((2, p.side, p.side, p.levels), f32),
             pltpu.VMEM((1, 2), jnp.int32),
             pltpu.VMEM((LANES, LANES), f32),
+            pltpu.VMEM((p.tiles, p.part_rows // p.side + 1, p.side, LANES), f32),
             pltpu.SemaphoreType.DMA((3 + p.tiles * p.full + p.spare,)),
         ],
         compiler_params=params(),
@@ -413,17 +437,25 @@
             )
         )
     )
-    dealt = lax.all_to_all(packed, "tile", split_axis=0, concat_axis=0, tiled=True)
+    got = swapped(other, "tile", 1)
+    pieces = [None] * p.tiles
+    for s in range(chips - 1, -1, -1):
+        for e, block in ((0, own[s]), (1, got[s])):
+            block = block.reshape(p.rows, LANES)
+            pieces[2 * s + e] = swapped(block, "tile", 2 * s) if s else block
     moved = pl.pallas_call(
         functools.partial(advect_kernel, p, tile_stride(p.tiles)),
         out_shape=jax.ShapeDtypeStruct((p.tiles * p.layers * p.back_rows, LANES), f32),
-        in_specs=in_vmem(1),
+        in_specs=in_vmem(len(pieces)),
         out_specs=pl.BlockSpec(memory_space=pltpu.VMEM),
-        scratch_shapes=[pltpu.VMEM((p.kinds * p.cells, p.tiles, LANES), f32)]
+        scratch_shapes=[
+            pltpu.VMEM((p.tiles * p.rows, LANES), f32),
+            pltpu.VMEM((p.kinds * p.cells, p.tiles, LANES), f32),
+        ]
         + [pltpu.VMEM((p.kinds * 2 * p.cells, p.tiles, LANES), f32)] * 3,
         compiler_params=params(),
         name="advect",
-    )(dealt.reshape(p.tiles * p.rows, LANES))
+    )(*pieces)
     columns = lax.all_to_all(
         moved.reshape(p.tiles * p.layers, p.back_rows, LANES),
         ("tile", "lev"),

time: 58.9 us -> 56.7 us (0.963)
  blocking collectives: 36.5 us -> 21.2 us
  starting transfers between devices: 5.31 us -> 13.5 us
  waiting for transfers between devices: 9.79 us -> 14.5 us
    all_to_all x1 -> x0, blocking collectives: 15.8 us -> none  [by_levels(): lax.all_to_all(packed, 'tile', split_axis=0, concat_axis=0, tiled=True)]
    ppermute x0 -> x7, starting transfers between devices: none -> 8.24 us  [swapped(): return lax.ppermute(value, axis, pairs)]
    ppermute x0 -> x7, waiting for transfers between devices: none -> 4.72 us  [swapped(): return lax.ppermute(value, axis, pairs)]
  transfers between devices with their start and end apart: 3 -> 10, of which waited for: 2 -> 6; matrix products, arithmetic and copies ran while one was open for 0% -> 0% of each run, Pallas kernels for 0% -> 0%
where the time goes in v3:
time: 56.7 us; the launch traced here: 56.3 us
  blocking collectives  21.2 us (37%)
  waiting for transfers between devices  14.5 us (26%)
  starting transfers between devices  13.5 us (24%)
  Pallas kernels  6.96 us (12%)
    all_to_all x1, blocking collectives, by_levels(): lax.all_to_all(moved.reshape(p.tiles * p.layers, p.back_rows, LANES), ('t...  21.2 us
    ppermute x3, waiting for transfers between devices, passed_along(): return lax.ppermute(value, axis, pairs)  9.8 us
    ppermute x7, starting transfers between devices, swapped(): return lax.ppermute(value, axis, pairs)  8.24 us
    ppermute x3, starting transfers between devices, passed_along(): return lax.ppermute(value, axis, pairs)  5.3 us
    ppermute x7, waiting for transfers between devices, swapped(): return lax.ppermute(value, axis, pairs)  4.72 us
    pallas_call x1, Pallas kernels, by_levels(): pl.pallas_call(functools.partial(advect_kernel, p, tile_stride(p.tiles)),...  3.82 us
    pallas_call x1, Pallas kernels, by_levels(): pl.pallas_call(functools.partial(pack_kernel, p), out_shape=[jax.ShapeDty...  1.25 us
  transfers between devices with their start and end apart: 10, of which 6 were waited for; matrix products, arithmetic and copies ran while one was open for 0% of the time, Pallas kernels for 0%

profile of v3, /device:TPU:0, one launch (start us, length us, event | category | flops | bytes accessed | tf_op | source)
XLA Modules:
  0.0 56.3 jit_solution(4980874916424062132)
XLA Ops:
  0.0 1.3 %pack.1 = (f32[19,8,128]{2,1,0:T(8,128)S(1)}, f32[19,8,128]{2,1,0:T(8,128)S(1)}, f32[19,8,128]{2,1,0:T(8,128)S(1)}, f32[19,8,128]{2,1,0:T(8,128)S(1)}, f32[4,19,8,128]{3,2,1,0:T(8,128)S(1)}) custom-call(f32[8,18,8,128]{3,2,1,0:T(8,128)} %bitcast.30, f32[8,8,18]{2,1,0:T(8,128)} %bitcast.31, f32[8,8,18]{2,1,0:T(8,128)} %bitcast.32, s32[1,2]{1,0:T(1,128)} %flip_ref.1), custom_call_target="tpu_custom_call" | custom-call | tf_op jit(solution)/shard_map/pack/pallas_call | solution.py:413
  1.3 0.5 collective-permute-start
  1.8 2.6 %collective-permute-start.1 = (f32[152,128]{1,0:T(8,128)S(1)}, f32[152,128]{1,0:T(8,128)S(1)}, u32[]{:S(2)}, u32[]{:S(2)}) collective-permute-start(f32[152,128]{1,0:T(8,128)S(1)} %bitcast.29), channel_id=1, source_target_pairs={{0,8},{4,12},{8,0},{12,4},{16,24},{20,28},{24,16},{28,20},{1,9},{5... | collective-permute-start | bytes 233480 | tf_op jit(solution)/shard_map/ppermute | solution.py:74
  4.3 1.5 %collective-permute-start.3 = (f32[152,128]{1,0:T(8,128)S(1)}, f32[152,128]{1,0:T(8,128)S(1)}, u32[]{:S(2)}, u32[]{:S(2)}) collective-permute-start(f32[152,128]{1,0:T(8,128)S(1)} %bitcast.28), channel_id=1, source_target_pairs={{0,16},{4,20},{8,24},{12,28},{16,0},{20,4},{24,8},{28,12},{1,17},{... | collective-permute-start | bytes 233480 | tf_op jit(solution)/shard_map/ppermute | solution.py:74
  5.9 0.0 collective-permute-start.5
  5.9 0.0 collective-permute-done
  5.9 3.0 %collective-permute-start.6 = (f32[152,128]{1,0:T(8,128)S(1)}, f32[152,128]{1,0:T(8,128)S(1)}, u32[]{:S(2)}, u32[]{:S(2)}) collective-permute-start(f32[152,128]{1,0:T(8,128)S(1)} %get-tuple-element.23), channel_id=1, source_target_pairs={{0,24},{4,28},{8,16},{12,20},{16,8},{20,12},{24,0},{28,4},{1,25},{... | collective-permute-start | bytes 233480 | tf_op jit(solution)/shard_map/ppermute | solution.py:74
  8.9 0.5 collective-permute-start.4
  9.4 0.0 collective-permute-done.1.refs_2_
  9.4 0.1 collective-permute-start.2
  9.5 1.0 %collective-permute-done.3.refs_4_ = f32[152,128]{1,0:T(8,128)S(1)} collective-permute-done((f32[152,128]{1,0:T(8,128)S(1)}, f32[152,128]{1,0:T(8,128)S(1)}, u32[]{:S(2)}, u32[]{:S(2)}) %collective-permute-start.3) | collective-permute-done | bytes 77856 | tf_op jit(solution)/shard_map/ppermute | solution.py:74
  10.5 1.3 %collective-permute-done.5.refs_6_ = f32[152,128]{1,0:T(8,128)S(1)} collective-permute-done((f32[152,128]{1,0:T(8,128)S(1)}, f32[152,128]{1,0:T(8,128)S(1)}, u32[]{:S(2)}, u32[]{:S(2)}) %collective-permute-start.5) | collective-permute-done | bytes 77856 | tf_op jit(solution)/shard_map/ppermute | solution.py:74
  11.8 1.3 %collective-permute-done.6.refs_7_ = f32[152,128]{1,0:T(8,128)S(1)} collective-permute-done((f32[152,128]{1,0:T(8,128)S(1)}, f32[152,128]{1,0:T(8,128)S(1)}, u32[]{:S(2)}, u32[]{:S(2)}) %collective-permute-start.6) | collective-permute-done | bytes 77856 | tf_op jit(solution)/shard_map/ppermute | solution.py:74
  13.1 1.1 %collective-permute-done.4.refs_5_ = f32[152,128]{1,0:T(8,128)S(1)} collective-permute-done((f32[152,128]{1,0:T(8,128)S(1)}, f32[152,128]{1,0:T(8,128)S(1)}, u32[]{:S(2)}, u32[]{:S(2)}) %collective-permute-start.4) | collective-permute-done | bytes 77856 | tf_op jit(solution)/shard_map/ppermute | solution.py:74
  14.2 0.0 collective-permute-done.2.refs_3_
  14.3 3.8 %advect.1 = f32[1280,128]{1,0:T(8,128)S(1)} custom-call(f32[152,128]{1,0:T(8,128)S(1)} %bitcast.26, f32[152,128]{1,0:T(8,128)S(1)} %get-tuple-element.26.refs_1_, f32[152,128]{1,0:T(8,128)S(1)} %collective-permute-done.1.refs_2_, f32[152,128]{1,0:T(8,128)S(1)} %collective-permute-done.2.refs_3_, f32[152,128]{1,0:T(8,128)S(1)} %collective-permute-done.3.refs_4_, ...), custom_call_target="tpu_custom_call" | custom-call | tf_op jit(solution)/shard_map/advect/pallas_call | solution.py:446
  18.1 0.0 copy-start
  18.1 21.2 %all_to_all.5 = f32[32,40,128]{2,1,0:T(8,128)S(1)} all-to-all(f32[32,40,128]{2,1,0:T(8,128)S(1)} %bitcast.23), channel_id=1, replica_groups=mesh['tile'=8,'lev'=4] {'tile','lev'}, dimensions={0} | all-to-all | bytes 1310720 | tf_op jit(solution)/shard_map/all_to_all | solution.py:459
  39.3 0.0 copy-done
  39.3 1.0 %mix.1 = (f32[288,128]{1,0:T(8,128)S(1)}, f32[288,128]{1,0:T(8,128)S(1)}, f32[288,128]{1,0:T(8,128)S(1)}, f32[288,128]{1,0:T(8,128)S(1)}) custom-call(f32[1280,128]{1,0:T(8,128)S(1)} %bitcast.24, f32[16,72,72]{2,1,0:T(8,128)S(1)} %bitcast.25), custom_call_target="tpu_custom_call" | custom-call | tf_op jit(solution)/shard_map/mix/pallas_call | solution.py:467
  40.3 2.9 %collective-permute-start.7 = (f32[288,128]{1,0:T(8,128)S(1)}, f32[288,128]{1,0:T(8,128)S(1)}, u32[]{:S(2)}, u32[]{:S(2)}) collective-permute-start(f32[288,128]{1,0:T(8,128)S(1)} %get-tuple-element.20), channel_id=1, source_target_pairs={{0,1},{1,2},{2,3},{3,0},{4,5},{5,6},{6,7},{7,4},{8,9},{9,10},{10,1... | collective-permute-start | bytes 442376 | tf_op jit(solution)/shard_map/ppermute | solution.py:19
  43.2 0.8 %collective-permute-start.8 = (f32[288,128]{1,0:T(8,128)S(1)}, f32[288,128]{1,0:T(8,128)S(1)}, u32[]{:S(2)}, u32[]{:S(2)}) collective-permute-start(f32[288,128]{1,0:T(8,128)S(1)} %get-tuple-element.21), channel_id=1, source_target_pairs={{0,2},{1,3},{2,0},{3,1},{4,6},{5,7},{6,4},{7,5},{8,10},{9,11},{10,... | collective-permute-start | bytes 442376 | tf_op jit(solution)/shard_map/ppermute | solution.py:19
  44.0 1.6 %collective-permute-start.9 = (f32[288,128]{1,0:T(8,128)S(1)}, f32[288,128]{1,0:T(8,128)S(1)}, u32[]{:S(2)}, u32[]{:S(2)}) collective-permute-start(f32[288,128]{1,0:T(8,128)S(1)} %get-tuple-element.22), channel_id=1, source_target_pairs={{0,3},{1,0},{2,1},{3,2},{4,7},{5,4},{6,5},{7,6},{8,11},{9,8},{10,9... | collective-permute-start | bytes 442376 | tf_op jit(solution)/shard_map/ppermute | solution.py:19
  45.6 3.1 %collective-permute-done.7.refs_1_ = f32[288,128]{1,0:T(8,128)S(1)} collective-permute-done((f32[288,128]{1,0:T(8,128)S(1)}, f32[288,128]{1,0:T(8,128)S(1)}, u32[]{:S(2)}, u32[]{:S(2)}) %collective-permute-start.7) | collective-permute-done | bytes 147488 | tf_op jit(solution)/shard_map/ppermute | solution.py:19
  48.7 6.7 %collective-permute-done.8.refs_2_ = f32[288,128]{1,0:T(8,128)S(1)} collective-permute-done((f32[288,128]{1,0:T(8,128)S(1)}, f32[288,128]{1,0:T(8,128)S(1)}, u32[]{:S(2)}, u32[]{:S(2)}) %collective-permute-start.8) | collective-permute-done | bytes 147488 | tf_op jit(solution)/shard_map/ppermute | solution.py:19
  55.4 0.0 collective-permute-done.9.refs_3_
  55.4 0.9 %place.1 = f32[8,18,8,128]{3,2,1,0:T(8,128)} custom-call(f32[288,128]{1,0:T(8,128)S(1)} %get-tuple-element.19.refs_0_, f32[288,128]{1,0:T(8,128)S(1)} %collective-permute-done.7.refs_1_, f32[288,128]{1,0:T(8,128)S(1)} %collective-permute-done.8.refs_2_, f32[288,128]{1,0:T(8,128)S(1)} %collective-permute-done.9.refs_3_), custom_call_target="tpu_custom_call" | custom-call | tf_op jit(solution)/shard_map/place/pallas_call | solution.py:483
  (1 shorter events, 0.0 us)
Async XLA Ops:
  1.3 4.6 %collective-permute-start = (f32[4,19,8,128]{3,2,1,0:T(8,128)S(1)}, f32[4,19,8,128]{3,2,1,0:T(8,128)S(1)}, u32[]{:S(2)}, u32[]{:S(2)}) collective-permute-start(f32[4,19,8,128]{3,2,1,0:T(8,128)S(1)} %get-tuple-element.15), channel_id=1, source_target_pairs={{0,4},{4,0},{8,12},{12,8},{16,20},{20,16},{24,28},{28,24},{1,5},{5... | collective-permute-start | bytes 933896 | tf_op jit(solution)/shard_map/ppermute | solution.py:74
  1.8 7.6 %collective-permute-start.1 = (f32[152,128]{1,0:T(8,128)S(1)}, f32[152,128]{1,0:T(8,128)S(1)}, u32[]{:S(2)}, u32[]{:S(2)}) collective-permute-start(f32[152,128]{1,0:T(8,128)S(1)} %bitcast.29), channel_id=1, source_target_pairs={{0,8},{4,12},{8,0},{12,4},{16,24},{20,28},{24,16},{28,20},{1,9},{5... | collective-permute-start | bytes 233480 | tf_op jit(solution)/shard_map/ppermute | solution.py:74
  4.3 6.2 %collective-permute-start.3 = (f32[152,128]{1,0:T(8,128)S(1)}, f32[152,128]{1,0:T(8,128)S(1)}, u32[]{:S(2)}, u32[]{:S(2)}) collective-permute-start(f32[152,128]{1,0:T(8,128)S(1)} %bitcast.28), channel_id=1, source_target_pairs={{0,16},{4,20},{8,24},{12,28},{16,0},{20,4},{24,8},{28,12},{1,17},{... | collective-permute-start | bytes 233480 | tf_op jit(solution)/shard_map/ppermute | solution.py:74
  5.9 6.0 %collective-permute-start.5 = (f32[152,128]{1,0:T(8,128)S(1)}, f32[152,128]{1,0:T(8,128)S(1)}, u32[]{:S(2)}, u32[]{:S(2)}) collective-permute-start(f32[152,128]{1,0:T(8,128)S(1)} %bitcast.27), channel_id=1, source_target_pairs={{0,24},{4,28},{8,16},{12,20},{16,8},{20,12},{24,0},{28,4},{1,25},{... | collective-permute-start | bytes 233480 | tf_op jit(solution)/shard_map/ppermute | solution.py:74
  5.9 7.2 %collective-permute-start.6 = (f32[152,128]{1,0:T(8,128)S(1)}, f32[152,128]{1,0:T(8,128)S(1)}, u32[]{:S(2)}, u32[]{:S(2)}) collective-permute-start(f32[152,128]{1,0:T(8,128)S(1)} %get-tuple-element.23), channel_id=1, source_target_pairs={{0,24},{4,28},{8,16},{12,20},{16,8},{20,12},{24,0},{28,4},{1,25},{... | collective-permute-start | bytes 233480 | tf_op jit(solution)/shard_map/ppermute | solution.py:74
  8.9 5.4 %collective-permute-start.4 = (f32[152,128]{1,0:T(8,128)S(1)}, f32[152,128]{1,0:T(8,128)S(1)}, u32[]{:S(2)}, u32[]{:S(2)}) collective-permute-start(f32[152,128]{1,0:T(8,128)S(1)} %get-tuple-element.24), channel_id=1, source_target_pairs={{0,16},{4,20},{8,24},{12,28},{16,0},{20,4},{24,8},{28,12},{1,17},{... | collective-permute-start | bytes 233480 | tf_op jit(solution)/shard_map/ppermute | solution.py:74
  9.4 4.9 %collective-permute-start.2 = (f32[152,128]{1,0:T(8,128)S(1)}, f32[152,128]{1,0:T(8,128)S(1)}, u32[]{:S(2)}, u32[]{:S(2)}) collective-permute-start(f32[152,128]{1,0:T(8,128)S(1)} %get-tuple-element.25), channel_id=1, source_target_pairs={{0,8},{4,12},{8,0},{12,4},{16,24},{20,28},{24,16},{28,20},{1,9},{5... | collective-permute-start | bytes 233480 | tf_op jit(solution)/shard_map/ppermute | solution.py:74
  18.1 21.2 %copy-start = (f32[1,2,8,72,72]{4,3,2,1,0:T(8,128)S(1)}, f32[1,2,8,72,72]{4,3,2,1,0:T(8,128)}, u32[]{:S(2)}) copy-start(f32[1,2,8,72,72]{4,3,2,1,0:T(8,128)} %param.8) | copy-start | bytes 995332
  40.3 8.4 %collective-permute-start.7 = (f32[288,128]{1,0:T(8,128)S(1)}, f32[288,128]{1,0:T(8,128)S(1)}, u32[]{:S(2)}, u32[]{:S(2)}) collective-permute-start(f32[288,128]{1,0:T(8,128)S(1)} %get-tuple-element.20), channel_id=1, source_target_pairs={{0,1},{1,2},{2,3},{3,0},{4,5},{5,6},{6,7},{7,4},{8,9},{9,10},{10,1... | collective-permute-start | bytes 442376 | tf_op jit(solution)/shard_map/ppermute | solution.py:19
  43.2 12.2 %collective-permute-start.8 = (f32[288,128]{1,0:T(8,128)S(1)}, f32[288,128]{1,0:T(8,128)S(1)}, u32[]{:S(2)}, u32[]{:S(2)}) collective-permute-start(f32[288,128]{1,0:T(8,128)S(1)} %get-tuple-element.21), channel_id=1, source_target_pairs={{0,2},{1,3},{2,0},{3,1},{4,6},{5,7},{6,4},{7,5},{8,10},{9,11},{10,... | collective-permute-start | bytes 442376 | tf_op jit(solution)/shard_map/ppermute | solution.py:19
  44.0 11.5 %collective-permute-start.9 = (f32[288,128]{1,0:T(8,128)S(1)}, f32[288,128]{1,0:T(8,128)S(1)}, u32[]{:S(2)}, u32[]{:S(2)}) collective-permute-start(f32[288,128]{1,0:T(8,128)S(1)} %get-tuple-element.22), channel_id=1, source_target_pairs={{0,3},{1,0},{2,1},{3,2},{4,7},{5,4},{6,5},{7,6},{8,11},{9,8},{10,9... | collective-permute-start | bytes 442376 | tf_op jit(solution)/shard_map/ppermute | solution.py:19

commit v4 on v3

--- a/solution.py
+++ b/solution.py
@@ -10,6 +10,7 @@
 SUBSTEPS = 3
 SUBLANES = 8
 LANES = 128
+FEW = 4
 VMEM_LIMIT = 40 * 1024 * 1024
 
 
@@ -133,7 +134,7 @@
         self.own_cells = self.cells // layers
         self.back_tail = self.full * self.own_cells
         self.back_part = self.own_cells // self.groups
-        self.back_rows = -(-(self.back_tail + self.back_part) // SUBLANES) * SUBLANES
+        self.back_rows = self.back_tail + self.back_part
         self.all_levels = levels * layers
         self.fits = (
             self.cells % self.groups == 0
@@ -142,6 +143,7 @@
             and self.side == SUBLANES
             and self.own_cells % side == 0
             and self.kinds < SUBLANES
+            and self.back_rows % FEW == 0
         )
 
 
@@ -223,6 +225,7 @@
     shape = (tiles, LANES)
     parts = refs[: -6]
     out_ref, in_ref, q_ref, near_ref, far_ref, mid_ref = refs[-6:]
+    out_ref = out_ref.reshape(tiles * p.layers * p.back_rows, LANES)
     me = lax.axis_index("tile")
     each = tiles // len(parts)
     for s, part in enumerate(parts):
@@ -335,6 +338,7 @@
 def mix_kernel(p, in_ref, weights_ref, *refs):
     out_refs, (x_ref, all_ref) = refs[: p.layers], refs[p.layers :]
     tiles = p.tiles
+    in_ref = in_ref.reshape(tiles * p.layers * p.back_rows, LANES)
     shape = (tiles, LANES)
     pitch = p.layers * p.back_rows
     group = lane_group(shape, p.width)
@@ -445,7 +449,9 @@
             pieces[2 * s + e] = swapped(block, "tile", 2 * s) if s else block
     moved = pl.pallas_call(
         functools.partial(advect_kernel, p, tile_stride(p.tiles)),
-        out_shape=jax.ShapeDtypeStruct((p.tiles * p.layers * p.back_rows, LANES), f32),
+        out_shape=jax.ShapeDtypeStruct(
+            (p.tiles * p.layers, p.back_rows // FEW, FEW, LANES), f32
+        ),
         in_specs=in_vmem(len(pieces)),
         out_specs=pl.BlockSpec(memory_space=pltpu.VMEM),
         scratch_shapes=[
@@ -457,7 +463,7 @@
         name="advect",
     )(*pieces)
     columns = lax.all_to_all(
-        moved.reshape(p.tiles * p.layers, p.back_rows, LANES),
+        moved,
         ("tile", "lev"),
         split_axis=0,
         concat_axis=0,
@@ -476,7 +482,7 @@
         compiler_params=params(),
         name="mix",
     )(
-        columns.reshape(p.tiles * p.layers * p.back_rows, LANES),
+        columns,
         weights.reshape(p.own_cells, p.all_levels, p.all_levels),
     )
     pieces = [mixed[0]] + [passed_along(mixed[s], "lev", s) for s in range(1, p.layers)]

time: 56.7 us -> 54.9 us (0.968)
  blocking collectives: 21.2 us -> 19.9 us
    all_to_all x1, blocking collectives: 21.2 us -> 19.9 us  [by_levels(): lax.all_to_all(moved, ('tile', 'lev'), split_axis=0, concat_axis=0, tiled...]
where the time goes in v4:
time: 54.9 us; the launch traced here: 54.7 us
  blocking collectives  19.9 us (36%)
  waiting for transfers between devices  14.7 us (27%)
  starting transfers between devices  13.4 us (24%)
  Pallas kernels  6.61 us (12%)
    all_to_all x1, blocking collectives, by_levels(): lax.all_to_all(moved, ('tile', 'lev'), split_axis=0, concat_axis=0, tiled...  19.9 us
    ppermute x3, waiting for transfers between devices, passed_along(): return lax.ppermute(value, axis, pairs)  9.94 us
    ppermute x7, starting transfers between devices, swapped(): return lax.ppermute(value, axis, pairs)  8.24 us
    ppermute x3, starting transfers between devices, passed_along(): return lax.ppermute(value, axis, pairs)  5.16 us
    ppermute x7, waiting for transfers between devices, swapped(): return lax.ppermute(value, axis, pairs)  4.72 us
    pallas_call x1, Pallas kernels, by_levels(): pl.pallas_call(functools.partial(advect_kernel, p, tile_stride(p.tiles)),...  3.59 us
    pallas_call x1, Pallas kernels, by_levels(): pl.pallas_call(functools.partial(pack_kernel, p), out_shape=[jax.ShapeDty...  1.25 us
  transfers between devices with their start and end apart: 10, of which 6 were waited for; matrix products, arithmetic and copies ran while one was open for 0% of the time, Pallas kernels for 0%

profile of v4, /device:TPU:0, one launch (start us, length us, event | category | flops | bytes accessed | tf_op | source)
XLA Modules:
  0.0 54.7 jit_solution(12730877820153641221)
XLA Ops:
  0.0 1.3 %pack.1 = (f32[19,8,128]{2,1,0:T(8,128)S(1)}, f32[19,8,128]{2,1,0:T(8,128)S(1)}, f32[19,8,128]{2,1,0:T(8,128)S(1)}, f32[19,8,128]{2,1,0:T(8,128)S(1)}, f32[4,19,8,128]{3,2,1,0:T(8,128)S(1)}) custom-call(f32[8,18,8,128]{3,2,1,0:T(8,128)} %bitcast.26, f32[8,8,18]{2,1,0:T(8,128)} %bitcast.27, f32[8,8,18]{2,1,0:T(8,128)} %bitcast.28, s32[1,2]{1,0:T(1,128)} %flip_ref.1), custom_call_target="tpu_custom_call" | custom-call | tf_op jit(solution)/shard_map/pack/pallas_call | solution.py:417
  1.3 0.5 collective-permute-start
  1.8 2.6 %collective-permute-start.1 = (f32[152,128]{1,0:T(8,128)S(1)}, f32[152,128]{1,0:T(8,128)S(1)}, u32[]{:S(2)}, u32[]{:S(2)}) collective-permute-start(f32[152,128]{1,0:T(8,128)S(1)} %bitcast.25), channel_id=1, source_target_pairs={{0,8},{4,12},{8,0},{12,4},{16,24},{20,28},{24,16},{28,20},{1,9},{5... | collective-permute-start | bytes 233480 | tf_op jit(solution)/shard_map/ppermute | solution.py:75
  4.3 1.5 %collective-permute-start.3 = (f32[152,128]{1,0:T(8,128)S(1)}, f32[152,128]{1,0:T(8,128)S(1)}, u32[]{:S(2)}, u32[]{:S(2)}) collective-permute-start(f32[152,128]{1,0:T(8,128)S(1)} %bitcast.24), channel_id=1, source_target_pairs={{0,16},{4,20},{8,24},{12,28},{16,0},{20,4},{24,8},{28,12},{1,17},{... | collective-permute-start | bytes 233480 | tf_op jit(solution)/shard_map/ppermute | solution.py:75
  5.9 0.0 collective-permute-start.5
  5.9 0.0 collective-permute-done
  5.9 3.0 %collective-permute-start.6 = (f32[152,128]{1,0:T(8,128)S(1)}, f32[152,128]{1,0:T(8,128)S(1)}, u32[]{:S(2)}, u32[]{:S(2)}) collective-permute-start(f32[152,128]{1,0:T(8,128)S(1)} %get-tuple-element.23), channel_id=1, source_target_pairs={{0,24},{4,28},{8,16},{12,20},{16,8},{20,12},{24,0},{28,4},{1,25},{... | collective-permute-start | bytes 233480 | tf_op jit(solution)/shard_map/ppermute | solution.py:75
  8.9 0.5 collective-permute-start.4
  9.4 0.0 collective-permute-done.1.refs_2_
  9.4 0.1 collective-permute-start.2
  9.5 1.0 %collective-permute-done.3.refs_4_ = f32[152,128]{1,0:T(8,128)S(1)} collective-permute-done((f32[152,128]{1,0:T(8,128)S(1)}, f32[152,128]{1,0:T(8,128)S(1)}, u32[]{:S(2)}, u32[]{:S(2)}) %collective-permute-start.3) | collective-permute-done | bytes 77856 | tf_op jit(solution)/shard_map/ppermute | solution.py:75
  10.5 1.3 %collective-permute-done.5.refs_6_ = f32[152,128]{1,0:T(8,128)S(1)} collective-permute-done((f32[152,128]{1,0:T(8,128)S(1)}, f32[152,128]{1,0:T(8,128)S(1)}, u32[]{:S(2)}, u32[]{:S(2)}) %collective-permute-start.5) | collective-permute-done | bytes 77856 | tf_op jit(solution)/shard_map/ppermute | solution.py:75
  11.8 1.3 %collective-permute-done.6.refs_7_ = f32[152,128]{1,0:T(8,128)S(1)} collective-permute-done((f32[152,128]{1,0:T(8,128)S(1)}, f32[152,128]{1,0:T(8,128)S(1)}, u32[]{:S(2)}, u32[]{:S(2)}) %collective-permute-start.6) | collective-permute-done | bytes 77856 | tf_op jit(solution)/shard_map/ppermute | solution.py:75
  13.1 1.1 %collective-permute-done.4.refs_5_ = f32[152,128]{1,0:T(8,128)S(1)} collective-permute-done((f32[152,128]{1,0:T(8,128)S(1)}, f32[152,128]{1,0:T(8,128)S(1)}, u32[]{:S(2)}, u32[]{:S(2)}) %collective-permute-start.4) | collective-permute-done | bytes 77856 | tf_op jit(solution)/shard_map/ppermute | solution.py:75
  14.2 0.0 collective-permute-done.2.refs_3_
  14.3 3.6 %advect.1 = f32[32,9,4,128]{3,2,1,0:T(4,128)S(1)} custom-call(f32[152,128]{1,0:T(8,128)S(1)} %bitcast.22, f32[152,128]{1,0:T(8,128)S(1)} %get-tuple-element.26.refs_1_, f32[152,128]{1,0:T(8,128)S(1)} %collective-permute-done.1.refs_2_, f32[152,128]{1,0:T(8,128)S(1)} %collective-permute-done.2.refs_3_, f32[152,128]{1,0:T(8,128)S(1)} %collective-permute-done.3.refs_4_, ...), custom_call_target="tpu_custom_call" | custom-call | tf_op jit(solution)/shard_map/advect/pallas_call | solution.py:450
  17.8 0.0 copy-start
  17.9 19.9 %all_to_all.5.in_ref = f32[32,9,4,128]{3,2,1,0:T(4,128)S(1)} all-to-all(f32[32,9,4,128]{3,2,1,0:T(4,128)S(1)} %advect.1), channel_id=1, replica_groups=mesh['tile'=8,'lev'=4] {'tile','lev'}, dimensions={0} | all-to-all | bytes 1179648 | tf_op jit(solution)/shard_map/all_to_all | solution.py:465
  37.8 0.0 copy-done
  37.8 0.9 %mix.1 = (f32[288,128]{1,0:T(8,128)S(1)}, f32[288,128]{1,0:T(8,128)S(1)}, f32[288,128]{1,0:T(8,128)S(1)}, f32[288,128]{1,0:T(8,128)S(1)}) custom-call(f32[32,9,4,128]{3,2,1,0:T(4,128)S(1)} %all_to_all.5.in_ref, f32[16,72,72]{2,1,0:T(8,128)S(1)} %bitcast.21), custom_call_target="tpu_custom_call" | custom-call | tf_op jit(solution)/shard_map/mix/pallas_call | solution.py:473
  38.7 2.7 %collective-permute-start.7 = (f32[288,128]{1,0:T(8,128)S(1)}, f32[288,128]{1,0:T(8,128)S(1)}, u32[]{:S(2)}, u32[]{:S(2)}) collective-permute-start(f32[288,128]{1,0:T(8,128)S(1)} %get-tuple-element.20), channel_id=1, source_target_pairs={{0,1},{1,2},{2,3},{3,0},{4,5},{5,6},{6,7},{7,4},{8,9},{9,10},{10,1... | collective-permute-start | bytes 442376 | tf_op jit(solution)/shard_map/ppermute | solution.py:20
  41.4 0.8 %collective-permute-start.8 = (f32[288,128]{1,0:T(8,128)S(1)}, f32[288,128]{1,0:T(8,128)S(1)}, u32[]{:S(2)}, u32[]{:S(2)}) collective-permute-start(f32[288,128]{1,0:T(8,128)S(1)} %get-tuple-element.21), channel_id=1, source_target_pairs={{0,2},{1,3},{2,0},{3,1},{4,6},{5,7},{6,4},{7,5},{8,10},{9,11},{10,... | collective-permute-start | bytes 442376 | tf_op jit(solution)/shard_map/ppermute | solution.py:20
  42.2 1.6 %collective-permute-start.9 = (f32[288,128]{1,0:T(8,128)S(1)}, f32[288,128]{1,0:T(8,128)S(1)}, u32[]{:S(2)}, u32[]{:S(2)}) collective-permute-start(f32[288,128]{1,0:T(8,128)S(1)} %get-tuple-element.22), channel_id=1, source_target_pairs={{0,3},{1,0},{2,1},{3,2},{4,7},{5,4},{6,5},{7,6},{8,11},{9,8},{10,9... | collective-permute-start | bytes 442376 | tf_op jit(solution)/shard_map/ppermute | solution.py:20
  43.8 3.3 %collective-permute-done.7.refs_1_ = f32[288,128]{1,0:T(8,128)S(1)} collective-permute-done((f32[288,128]{1,0:T(8,128)S(1)}, f32[288,128]{1,0:T(8,128)S(1)}, u32[]{:S(2)}, u32[]{:S(2)}) %collective-permute-start.7) | collective-permute-done | bytes 147488 | tf_op jit(solution)/shard_map/ppermute | solution.py:20
  47.1 6.6 %collective-permute-done.8.refs_2_ = f32[288,128]{1,0:T(8,128)S(1)} collective-permute-done((f32[288,128]{1,0:T(8,128)S(1)}, f32[288,128]{1,0:T(8,128)S(1)}, u32[]{:S(2)}, u32[]{:S(2)}) %collective-permute-start.8) | collective-permute-done | bytes 147488 | tf_op jit(solution)/shard_map/ppermute | solution.py:20
  53.8 0.0 collective-permute-done.9.refs_3_
  53.8 0.9 %place.1 = f32[8,18,8,128]{3,2,1,0:T(8,128)} custom-call(f32[288,128]{1,0:T(8,128)S(1)} %get-tuple-element.19.refs_0_, f32[288,128]{1,0:T(8,128)S(1)} %collective-permute-done.7.refs_1_, f32[288,128]{1,0:T(8,128)S(1)} %collective-permute-done.8.refs_2_, f32[288,128]{1,0:T(8,128)S(1)} %collective-permute-done.9.refs_3_), custom_call_target="tpu_custom_call" | custom-call | tf_op jit(solution)/shard_map/place/pallas_call | solution.py:489
  (1 shorter events, 0.0 us)
Async XLA Ops:
  1.3 4.6 %collective-permute-start = (f32[4,19,8,128]{3,2,1,0:T(8,128)S(1)}, f32[4,19,8,128]{3,2,1,0:T(8,128)S(1)}, u32[]{:S(2)}, u32[]{:S(2)}) collective-permute-start(f32[4,19,8,128]{3,2,1,0:T(8,128)S(1)} %get-tuple-element.15), channel_id=1, source_target_pairs={{0,4},{4,0},{8,12},{12,8},{16,20},{20,16},{24,28},{28,24},{1,5},{5... | collective-permute-start | bytes 933896 | tf_op jit(solution)/shard_map/ppermute | solution.py:75
  1.8 7.6 %collective-permute-start.1 = (f32[152,128]{1,0:T(8,128)S(1)}, f32[152,128]{1,0:T(8,128)S(1)}, u32[]{:S(2)}, u32[]{:S(2)}) collective-permute-start(f32[152,128]{1,0:T(8,128)S(1)} %bitcast.25), channel_id=1, source_target_pairs={{0,8},{4,12},{8,0},{12,4},{16,24},{20,28},{24,16},{28,20},{1,9},{5... | collective-permute-start | bytes 233480 | tf_op jit(solution)/shard_map/ppermute | solution.py:75
  4.3 6.2 %collective-permute-start.3 = (f32[152,128]{1,0:T(8,128)S(1)}, f32[152,128]{1,0:T(8,128)S(1)}, u32[]{:S(2)}, u32[]{:S(2)}) collective-permute-start(f32[152,128]{1,0:T(8,128)S(1)} %bitcast.24), channel_id=1, source_target_pairs={{0,16},{4,20},{8,24},{12,28},{16,0},{20,4},{24,8},{28,12},{1,17},{... | collective-permute-start | bytes 233480 | tf_op jit(solution)/shard_map/ppermute | solution.py:75
  5.9 6.0 %collective-permute-start.5 = (f32[152,128]{1,0:T(8,128)S(1)}, f32[152,128]{1,0:T(8,128)S(1)}, u32[]{:S(2)}, u32[]{:S(2)}) collective-permute-start(f32[152,128]{1,0:T(8,128)S(1)} %bitcast.23), channel_id=1, source_target_pairs={{0,24},{4,28},{8,16},{12,20},{16,8},{20,12},{24,0},{28,4},{1,25},{... | collective-permute-start | bytes 233480 | tf_op jit(solution)/shard_map/ppermute | solution.py:75
  5.9 7.2 %collective-permute-start.6 = (f32[152,128]{1,0:T(8,128)S(1)}, f32[152,128]{1,0:T(8,128)S(1)}, u32[]{:S(2)}, u32[]{:S(2)}) collective-permute-start(f32[152,128]{1,0:T(8,128)S(1)} %get-tuple-element.23), channel_id=1, source_target_pairs={{0,24},{4,28},{8,16},{12,20},{16,8},{20,12},{24,0},{28,4},{1,25},{... | collective-permute-start | bytes 233480 | tf_op jit(solution)/shard_map/ppermute | solution.py:75
  8.9 5.4 %collective-permute-start.4 = (f32[152,128]{1,0:T(8,128)S(1)}, f32[152,128]{1,0:T(8,128)S(1)}, u32[]{:S(2)}, u32[]{:S(2)}) collective-permute-start(f32[152,128]{1,0:T(8,128)S(1)} %get-tuple-element.24), channel_id=1, source_target_pairs={{0,16},{4,20},{8,24},{12,28},{16,0},{20,4},{24,8},{28,12},{1,17},{... | collective-permute-start | bytes 233480 | tf_op jit(solution)/shard_map/ppermute | solution.py:75
  9.4 4.9 %collective-permute-start.2 = (f32[152,128]{1,0:T(8,128)S(1)}, f32[152,128]{1,0:T(8,128)S(1)}, u32[]{:S(2)}, u32[]{:S(2)}) collective-permute-start(f32[152,128]{1,0:T(8,128)S(1)} %get-tuple-element.25), channel_id=1, source_target_pairs={{0,8},{4,12},{8,0},{12,4},{16,24},{20,28},{24,16},{28,20},{1,9},{5... | collective-permute-start | bytes 233480 | tf_op jit(solution)/shard_map/ppermute | solution.py:75
  17.8 19.9 %copy-start = (f32[1,2,8,72,72]{4,3,2,1,0:T(8,128)S(1)}, f32[1,2,8,72,72]{4,3,2,1,0:T(8,128)}, u32[]{:S(2)}) copy-start(f32[1,2,8,72,72]{4,3,2,1,0:T(8,128)} %param.8) | copy-start | bytes 995332
  38.7 8.5 %collective-permute-start.7 = (f32[288,128]{1,0:T(8,128)S(1)}, f32[288,128]{1,0:T(8,128)S(1)}, u32[]{:S(2)}, u32[]{:S(2)}) collective-permute-start(f32[288,128]{1,0:T(8,128)S(1)} %get-tuple-element.20), channel_id=1, source_target_pairs={{0,1},{1,2},{2,3},{3,0},{4,5},{5,6},{6,7},{7,4},{8,9},{9,10},{10,1... | collective-permute-start | bytes 442376 | tf_op jit(solution)/shard_map/ppermute | solution.py:20
  41.4 12.4 %collective-permute-start.8 = (f32[288,128]{1,0:T(8,128)S(1)}, f32[288,128]{1,0:T(8,128)S(1)}, u32[]{:S(2)}, u32[]{:S(2)}) collective-permute-start(f32[288,128]{1,0:T(8,128)S(1)} %get-tuple-element.21), channel_id=1, source_target_pairs={{0,2},{1,3},{2,0},{3,1},{4,6},{5,7},{6,4},{7,5},{8,10},{9,11},{10,... | collective-permute-start | bytes 442376 | tf_op jit(solution)/shard_map/ppermute | solution.py:20
  42.2 11.6 %collective-permute-start.9 = (f32[288,128]{1,0:T(8,128)S(1)}, f32[288,128]{1,0:T(8,128)S(1)}, u32[]{:S(2)}, u32[]{:S(2)}) collective-permute-start(f32[288,128]{1,0:T(8,128)S(1)} %get-tuple-element.22), channel_id=1, source_target_pairs={{0,3},{1,0},{2,1},{3,2},{4,7},{5,4},{6,5},{7,6},{8,11},{9,8},{10,9... | collective-permute-start | bytes 442376 | tf_op jit(solution)/shard_map/ppermute | solution.py:20

commit v5 on v4

--- a/solution.py
+++ b/solution.py
@@ -139,7 +139,7 @@
         self.fits = (
             self.cells % self.groups == 0
             and self.own_cells % self.groups == 0
-            and self.part_rows % SUBLANES == 0
+            and self.part_rows % (2 * side) == 0
             and self.side == SUBLANES
             and self.own_cells % side == 0
             and self.kinds < SUBLANES
@@ -170,23 +170,23 @@
     for source, target in ((first_ref, courant_ref.at[0]), (second_ref, courant_ref.at[1])):
         fetch(source, target)
     fetch(flip_ref, flags_ref)
-    for h in range(p.spare):
-        fetch(x_ref.at[:, p.full * p.tiles + h], spare_ref.at[h])
+    fetch(x_ref.at[:, pl.ds(p.full * p.tiles, p.spare)], spare_ref)
     small = 3
     for d, slot in slots:
-        for f in range(p.full):
-            fetch(x_ref.at[:, p.full * d + f], slot.at[pl.ds(f * p.side, p.side)])
+        fetch(
+            x_ref.at[:, pl.ds(p.full * d, p.full)],
+            slot.at[pl.ds(0, p.full * p.side)].reshape(p.side, p.full, p.side, LANES),
+        )
     filler = jnp.zeros((p.side, LANES), jnp.float32)
     group = lane_group((p.side, LANES), p.width)
-    for copy in copies[small : small + p.spare]:
-        copy.wait()
+    copies[small].wait()
     tall = p.part_rows // p.side
     for h in range(p.spare):
         for g in range(p.groups):
             for r in range(tall):
                 rows = None
                 for m in range(p.groups):
-                    part = spare_ref[h, m * tall + r]
+                    part = spare_ref[m * tall + r, h]
                     shift = (m - g) * p.width % LANES
                     moved = pltpu.roll(part, shift, 1) if shift else part
                     rows = moved if rows is None else jnp.where(group == m, moved, rows)
@@ -216,7 +216,7 @@
     for d, slot in slots:
         for r in range(tall + 1):
             slot[p.full * p.side + r] = rest_ref[d, r]
-    for copy in copies[small + p.spare :]:
+    for copy in copies[small + 1 :]:
         copy.wait()
 
 
@@ -241,96 +241,138 @@
     flips = row(p.flip_at)
     first_flip = jnp.broadcast_to(flips[:, 0:1], shape) > 0.5
     second_flip = jnp.broadcast_to(flips[:, cells : cells + 1], shape) > 0.5
-
-    def turned(get):
-        for i in range(side // 2):
+    group = lane_group(shape, p.width)
+    tall = p.part_rows // side
+
+    def reversed_groups(value):
+        turned = {}
+        result = None
+        for g in range(p.groups):
+            by = (2 * g + 1) % p.groups
+            if by not in turned:
+                turned[by] = pltpu.roll(value, by * p.width, 1) if by else value
+            result = turned[by] if result is None else jnp.where(group == g, turned[by], result)
+        return result
+
+    def mirrored(get, height, back):
+        for i in range(height // 2):
             for j in range(side // 2):
-                i2, j2 = side - 1 - i, side - 1 - j
+                i2, j2 = height - 1 - i, side - 1 - j
                 ll, hl, lh, hh = get(i, j), get(i2, j), get(i, j2), get(i2, j2)
-                a, b = jnp.where(first_flip, hl, ll), jnp.where(first_flip, ll, hl)
-                c, d = jnp.where(first_flip, hh, lh), jnp.where(first_flip, lh, hh)
+                a, b = jnp.where(first_flip, back(hl), ll), jnp.where(first_flip, back(ll), hl)
+                c, d = jnp.where(first_flip, back(hh), lh), jnp.where(first_flip, back(lh), hh)
                 yield i * side + j, jnp.where(second_flip, c, a)
                 yield i2 * side + j, jnp.where(second_flip, d, b)
                 yield i * side + j2, jnp.where(second_flip, a, c)
                 yield i2 * side + j2, jnp.where(second_flip, b, d)
 
-    for kind in range(p.kinds):
-        if kind < p.full:
-            get = lambda i, j: row(kind * cells + i * side + j)
-        else:
-
-            def get(i, j):
-                m, r = divmod(i * side + j, p.part_rows)
-                value = row(p.tail_at + r)
-                return pltpu.roll(value, LANES - m * p.width, 1) if m else value
-
-        for cell, value in turned(get):
+    def plain(value):
+        return value
+
+    def set_faces(at, c):
+        e = jnp.abs(c)
+        u = 1.0 - e
+        cu = c * u
+        near_ref[at] = (cu * u) * (1.0 / 12.0)
+        far_ref[at] = (cu * e) * (-1.0 / 12.0)
+        mid_ref[at] = (c * e) * (3.0 - 2.0 * e)
+
+    tail = p.full * cells
+    tail_faces = p.full * 2 * cells
+    for kind in range(p.full):
+        for cell, value in mirrored(
+            lambda i, j: row((i * p.full + kind) * side + j), side, plain
+        ):
             q_ref[kind * cells + cell] = value
         courant = row(p.courant_at + kind)
         for at in range(2 * cells):
-            c = jnp.broadcast_to(courant[:, at : at + 1], shape)
-            e = jnp.abs(c)
-            u = 1.0 - e
-            cu = c * u
-            near_ref[kind * 2 * cells + at] = (cu * u) * (1.0 / 12.0)
-            far_ref[kind * 2 * cells + at] = (cu * e) * (-1.0 / 12.0)
-            mid_ref[kind * 2 * cells + at] = (c * e) * (3.0 - 2.0 * e)
-
-    def sweep(at, faces_at, step, shift):
-        cell = [at + step * i for i in range(side)]
-        face = [faces_at + step * i for i in range(side)]
-        q = [q_ref[cell[i]] for i in range(side)]
-        up = lambda v: pltpu.roll(v, shift, 0)
-        down = lambda v: pltpu.roll(v, tiles - shift, 0)
-        ext = [up(q[side - 1])] + q + [down(q[0]), down(q[1])]
+            set_faces(kind * 2 * cells + at, jnp.broadcast_to(courant[:, at : at + 1], shape))
+    for cell, value in mirrored(
+        lambda i, j: row(p.tail_at + i * side + j), tall, reversed_groups
+    ):
+        q_ref[tail + cell] = value
+    courant = row(p.courant_at + p.full)
+    for way in range(2):
+        for r in range(p.part_rows):
+            c = None
+            for m in range(p.groups):
+                at = way * cells + m * p.part_rows + r
+                value = jnp.broadcast_to(courant[:, at : at + 1], shape)
+                c = value if c is None else jnp.where(group == m, value, c)
+            set_faces(tail_faces + way * p.part_rows + r, c)
+
+    def sweep(at, faces_at, step, length, up, down):
+        cell = [at + step * i for i in range(length)]
+        face = [faces_at + step * i for i in range(length)]
+        q = [q_ref[cell[i]] for i in range(length)]
+        ext = [up(q[length - 1])] + q + [down(q[0]), down(q[1])]
         edge = [
-            7.0 * (ext[i + 1] + ext[i + 2]) - (ext[i] + ext[i + 3]) for i in range(side)
+            7.0 * (ext[i + 1] + ext[i + 2]) - (ext[i] + ext[i + 3]) for i in range(length)
         ]
-        edges = [up(edge[side - 1])] + edge + [down(edge[0])]
+        edges = [up(edge[length - 1])] + edge + [down(edge[0])]
         flux = []
-        for i in range(side):
+        for i in range(length):
             near = near_ref[face[i]]
             upwind = near >= 0.0
             far = jnp.where(upwind, edges[i], edges[i + 2])
             mid = jnp.where(upwind, ext[i + 1], ext[i + 2])
             flux.append(near * edge[i] + far_ref[face[i]] * far + mid_ref[face[i]] * mid)
-        fluxes = [up(flux[side - 1])] + flux
+        fluxes = [up(flux[length - 1])] + flux
+        for i in range(length):
+            q_ref[cell[i]] = q[i] - (fluxes[i + 1] - fluxes[i])
+
+    def low_tile(shift):
+        return lambda v: pltpu.roll(v, shift, 0)
+
+    def high_tile(shift):
+        return lambda v: pltpu.roll(v, tiles - shift, 0)
+
+    def low_group(v):
+        moved = pltpu.roll(v, p.width, 1)
+        return jnp.where(group == 0, low_tile(stride)(moved), moved)
+
+    def high_group(v):
+        moved = pltpu.roll(v, LANES - p.width, 1)
+        return jnp.where(group == p.groups - 1, high_tile(stride)(moved), moved)
+
+    def step(count, carry):
+        for j in range(side):
+            for kind in range(p.full):
+                at, faces_at = kind * cells + j, kind * 2 * cells + j
+                sweep(at, faces_at, side, side, low_tile(stride), high_tile(stride))
+            sweep(tail + j, tail_faces + j, side, tall, low_group, high_group)
         for i in range(side):
-            q_ref[cell[i]] = q[i] - (fluxes[i + 1] - fluxes[i])
-
-    def step(count, carry):
-        kind = count // SUBSTEPS
-        at = kind * cells
-        faces_at = kind * 2 * cells
-        for j in range(side):
-            sweep(at + j, faces_at + j, side, stride)
-        for i in range(side):
-            sweep(at + i * side, faces_at + cells + i * side, 1, 1)
+            for kind in range(p.full):
+                at, faces_at = kind * cells + i * side, (kind * 2 + 1) * cells + i * side
+                sweep(at, faces_at, 1, side, low_tile(1), high_tile(1))
+            if i < tall:
+                at, faces_at = tail + i * side, tail_faces + p.part_rows + i * side
+                sweep(at, faces_at, 1, side, low_tile(1), high_tile(1))
         return carry
 
-    lax.fori_loop(0, p.kinds * SUBSTEPS, step, 0)
+    lax.fori_loop(0, SUBSTEPS, step, 0)
 
     pitch = p.layers * p.back_rows
 
-    def send(cell_layer, at, value):
-        out_ref[pl.ds(cell_layer * p.back_rows + at, tiles, stride=pitch), :] = value
-
-    for kind in range(p.kinds):
-        back = turned(lambda i, j: q_ref[kind * cells + i * side + j])
-        if kind < p.full:
-            for cell, value in back:
-                layer, own = divmod(cell, p.own_cells)
-                send(layer, kind * p.own_cells + own, value)
-        else:
-            for cell, value in back:
-                q_ref[kind * cells + cell] = value
-    group = lane_group(shape, p.width)
+    def send(layer, at, value):
+        out_ref[pl.ds(layer * p.back_rows + at, tiles, stride=pitch), :] = value
+
+    for kind in range(p.full):
+        for cell, value in mirrored(
+            lambda i, j: q_ref[kind * cells + i * side + j], side, plain
+        ):
+            layer, own = divmod(cell, p.own_cells)
+            send(layer, kind * p.own_cells + own, value)
+    rest = dict(mirrored(lambda i, j: q_ref[tail + i * side + j], tall, reversed_groups))
     for layer in range(p.layers):
         for r in range(p.back_part):
             rows = None
             for m in range(p.groups):
-                value = q_ref[p.full * cells + layer * p.own_cells + m * p.back_part + r]
-                moved = pltpu.roll(value, m * p.width, 1) if m else value
+                at, source = divmod(
+                    layer * p.own_cells + m * p.back_part + r, p.part_rows
+                )[::-1]
+                shift = (m - source) * p.width % LANES
+                moved = pltpu.roll(rest[at], shift, 1) if shift else rest[at]
                 rows = moved if rows is None else jnp.where(group == m, moved, rows)
             send(layer, p.back_tail + r, rows)
 
@@ -389,16 +431,23 @@
         out_refs[s][...] = all_ref[pl.ds(pl.multiple_of(layer * size, SUBLANES), size), :]
 
 
-def place_kernel(p, *refs):
-    in_refs, out_ref = refs[: p.layers], refs[p.layers]
+def place_kernel(p, order, *refs):
+    in_refs, out_ref, sems = refs[: p.layers], refs[p.layers], refs[p.layers + 1]
     me = lax.axis_index("lev")
     tall = p.own_cells // p.side
-    for s in range(p.layers):
+    copies = []
+    for n, s in enumerate(order):
         layer = lax.rem(me - s + p.layers, p.layers)
-        for level in range(p.levels):
-            for r in range(tall):
-                at = level * p.own_cells + r * p.side
-                out_ref[layer * tall + r, level] = in_refs[s][at : at + p.side, :]
+        piece = in_refs[n].reshape(p.levels, tall, p.side, LANES)
+        for r in range(tall):
+            copies.append(
+                pltpu.make_async_copy(
+                    piece.at[:, r], out_ref.at[layer * tall + r], sems.at[len(copies)]
+                )
+            )
+            copies[-1].start()
+    for copy in copies:
+        copy.wait()
 
 
 def in_vmem(count):
@@ -421,12 +470,12 @@
         in_specs=[pl.BlockSpec(memory_space=pltpu.HBM)] * 4,
         out_specs=in_vmem(chips + 1),
         scratch_shapes=[
-            pltpu.VMEM((p.spare, p.side, p.side, LANES), f32),
+            pltpu.VMEM((p.side, p.spare, p.side, LANES), f32),
             pltpu.VMEM((2, p.side, p.side, p.levels), f32),
             pltpu.VMEM((1, 2), jnp.int32),
             pltpu.VMEM((LANES, LANES), f32),
             pltpu.VMEM((p.tiles, p.part_rows // p.side + 1, p.side, LANES), f32),
-            pltpu.SemaphoreType.DMA((3 + p.tiles * p.full + p.spare,)),
+            pltpu.SemaphoreType.DMA((4 + p.tiles,)),
         ],
         compiler_params=params(),
         name="pack",
@@ -456,9 +505,9 @@
         out_specs=pl.BlockSpec(memory_space=pltpu.VMEM),
         scratch_shapes=[
             pltpu.VMEM((p.tiles * p.rows, LANES), f32),
-            pltpu.VMEM((p.kinds * p.cells, p.tiles, LANES), f32),
+            pltpu.VMEM((p.full * p.cells + p.part_rows, p.tiles, LANES), f32),
         ]
-        + [pltpu.VMEM((p.kinds * 2 * p.cells, p.tiles, LANES), f32)] * 3,
+        + [pltpu.VMEM((2 * (p.full * p.cells + p.part_rows), p.tiles, LANES), f32)] * 3,
         compiler_params=params(),
         name="advect",
     )(*pieces)
@@ -486,14 +535,16 @@
         weights.reshape(p.own_cells, p.all_levels, p.all_levels),
     )
     pieces = [mixed[0]] + [passed_along(mixed[s], "lev", s) for s in range(1, p.layers)]
+    order = sorted(range(p.layers), key=lambda s: -min(s, p.layers - s) if s else -p.layers)
     placed = pl.pallas_call(
-        functools.partial(place_kernel, p),
+        functools.partial(place_kernel, p, order),
         out_shape=jax.ShapeDtypeStruct(across, f32),
         in_specs=in_vmem(p.layers),
-        out_specs=pl.BlockSpec(memory_space=pltpu.VMEM),
+        out_specs=pl.BlockSpec(memory_space=pltpu.HBM),
+        scratch_shapes=[pltpu.SemaphoreType.DMA((p.cells // p.side,))],
         compiler_params=params(),
         name="place",
-    )(*pieces)
+    )(*(pieces[s] for s in order))
     return placed.transpose(0, 2, 1, 3)[None]
 
 

time: 54.9 us -> 54.3 us (0.989)
  waiting for transfers between devices: 14.7 us -> 13.5 us
  starting transfers between devices: 13.4 us -> 14.1 us
    ppermute x3, waiting for transfers between devices: 9.94 us -> 8.74 us  [passed_along(): return lax.ppermute(value, axis, pairs)]
    ppermute x3, starting transfers between devices: 5.16 us -> 5.82 us  [passed_along(): return lax.ppermute(value, axis, pairs)]
where the time goes in v5:
time: 54.3 us; the launch traced here: 53.8 us
  blocking collectives  19.9 us (37%)
  starting transfers between devices  14.1 us (26%)
  waiting for transfers between devices  13.5 us (25%)
  Pallas kernels  6.3 us (12%)
    all_to_all x1, blocking collectives, by_levels(): lax.all_to_all(moved, ('tile', 'lev'), split_axis=0, concat_axis=0, tiled...  19.9 us
    ppermute x3, waiting for transfers between devices, passed_along(): return lax.ppermute(value, axis, pairs)  8.74 us
    ppermute x7, starting transfers between devices, swapped(): return lax.ppermute(value, axis, pairs)  8.23 us
    ppermute x3, starting transfers between devices, passed_along(): return lax.ppermute(value, axis, pairs)  5.82 us
    ppermute x7, waiting for transfers between devices, swapped(): return lax.ppermute(value, axis, pairs)  4.72 us
    pallas_call x1, Pallas kernels, by_levels(): pl.pallas_call(functools.partial(advect_kernel, p, tile_stride(p.tiles)),...  3.29 us
    pallas_call x1, Pallas kernels, by_levels(): pl.pallas_call(functools.partial(pack_kernel, p), out_shape=[jax.ShapeDty...  1.24 us
  transfers between devices with their start and end apart: 10, of which 6 were waited for; matrix products, arithmetic and copies ran while one was open for 0% of the time, Pallas kernels for 0%

profile of v5, /device:TPU:0, one launch (start us, length us, event | category | flops | bytes accessed | tf_op | source)
XLA Modules:
  0.0 53.8 jit_solution(9417401327529919325)
XLA Ops:
  0.0 1.2 %pack.1 = (f32[19,8,128]{2,1,0:T(8,128)S(1)}, f32[19,8,128]{2,1,0:T(8,128)S(1)}, f32[19,8,128]{2,1,0:T(8,128)S(1)}, f32[19,8,128]{2,1,0:T(8,128)S(1)}, f32[4,19,8,128]{3,2,1,0:T(8,128)S(1)}) custom-call(f32[8,18,8,128]{3,2,1,0:T(8,128)} %bitcast.26, f32[8,8,18]{2,1,0:T(8,128)} %bitcast.27, f32[8,8,18]{2,1,0:T(8,128)} %bitcast.28, s32[1,2]{1,0:T(1,128)} %flip_ref.1), custom_call_target="tpu_custom_call" | custom-call | tf_op jit(solution)/shard_map/pack/pallas_call | solution.py:466
  1.3 0.5 collective-permute-start
  1.8 2.6 %collective-permute-start.1 = (f32[152,128]{1,0:T(8,128)S(1)}, f32[152,128]{1,0:T(8,128)S(1)}, u32[]{:S(2)}, u32[]{:S(2)}) collective-permute-start(f32[152,128]{1,0:T(8,128)S(1)} %bitcast.25), channel_id=1, source_target_pairs={{0,8},{4,12},{8,0},{12,4},{16,24},{20,28},{24,16},{28,20},{1,9},{5... | collective-permute-start | bytes 233480 | tf_op jit(solution)/shard_map/ppermute | solution.py:75
  4.3 1.5 %collective-permute-start.3 = (f32[152,128]{1,0:T(8,128)S(1)}, f32[152,128]{1,0:T(8,128)S(1)}, u32[]{:S(2)}, u32[]{:S(2)}) collective-permute-start(f32[152,128]{1,0:T(8,128)S(1)} %bitcast.24), channel_id=1, source_target_pairs={{0,16},{4,20},{8,24},{12,28},{16,0},{20,4},{24,8},{28,12},{1,17},{... | collective-permute-start | bytes 233480 | tf_op jit(solution)/shard_map/ppermute | solution.py:75
  5.9 0.0 collective-permute-start.5
  5.9 0.0 collective-permute-done
  5.9 3.0 %collective-permute-start.6 = (f32[152,128]{1,0:T(8,128)S(1)}, f32[152,128]{1,0:T(8,128)S(1)}, u32[]{:S(2)}, u32[]{:S(2)}) collective-permute-start(f32[152,128]{1,0:T(8,128)S(1)} %get-tuple-element.23), channel_id=1, source_target_pairs={{0,24},{4,28},{8,16},{12,20},{16,8},{20,12},{24,0},{28,4},{1,25},{... | collective-permute-start | bytes 233480 | tf_op jit(solution)/shard_map/ppermute | solution.py:75
  8.9 0.5 collective-permute-start.4
  9.4 0.0 collective-permute-done.1.refs_2_
  9.4 0.1 collective-permute-start.2
  9.5 1.0 %collective-permute-done.3.refs_4_ = f32[152,128]{1,0:T(8,128)S(1)} collective-permute-done((f32[152,128]{1,0:T(8,128)S(1)}, f32[152,128]{1,0:T(8,128)S(1)}, u32[]{:S(2)}, u32[]{:S(2)}) %collective-permute-start.3) | collective-permute-done | bytes 77856 | tf_op jit(solution)/shard_map/ppermute | solution.py:75
  10.5 1.3 %collective-permute-done.5.refs_6_ = f32[152,128]{1,0:T(8,128)S(1)} collective-permute-done((f32[152,128]{1,0:T(8,128)S(1)}, f32[152,128]{1,0:T(8,128)S(1)}, u32[]{:S(2)}, u32[]{:S(2)}) %collective-permute-start.5) | collective-permute-done | bytes 77856 | tf_op jit(solution)/shard_map/ppermute | solution.py:75
  11.8 1.3 %collective-permute-done.6.refs_7_ = f32[152,128]{1,0:T(8,128)S(1)} collective-permute-done((f32[152,128]{1,0:T(8,128)S(1)}, f32[152,128]{1,0:T(8,128)S(1)}, u32[]{:S(2)}, u32[]{:S(2)}) %collective-permute-start.6) | collective-permute-done | bytes 77856 | tf_op jit(solution)/shard_map/ppermute | solution.py:75
  13.1 1.1 %collective-permute-done.4.refs_5_ = f32[152,128]{1,0:T(8,128)S(1)} collective-permute-done((f32[152,128]{1,0:T(8,128)S(1)}, f32[152,128]{1,0:T(8,128)S(1)}, u32[]{:S(2)}, u32[]{:S(2)}) %collective-permute-start.4) | collective-permute-done | bytes 77856 | tf_op jit(solution)/shard_map/ppermute | solution.py:75
  14.2 0.0 collective-permute-done.2.refs_3_
  14.2 3.3 %advect.1 = f32[32,9,4,128]{3,2,1,0:T(4,128)S(1)} custom-call(f32[152,128]{1,0:T(8,128)S(1)} %bitcast.22, f32[152,128]{1,0:T(8,128)S(1)} %get-tuple-element.26.refs_1_, f32[152,128]{1,0:T(8,128)S(1)} %collective-permute-done.1.refs_2_, f32[152,128]{1,0:T(8,128)S(1)} %collective-permute-done.2.refs_3_, f32[152,128]{1,0:T(8,128)S(1)} %collective-permute-done.3.refs_4_, ...), custom_call_target="tpu_custom_call" | custom-call | tf_op jit(solution)/shard_map/advect/pallas_call | solution.py:499
  17.5 0.0 copy-start
  17.5 19.9 %all_to_all.5.in_ref = f32[32,9,4,128]{3,2,1,0:T(4,128)S(1)} all-to-all(f32[32,9,4,128]{3,2,1,0:T(4,128)S(1)} %advect.1), channel_id=1, replica_groups=mesh['tile'=8,'lev'=4] {'tile','lev'}, dimensions={0} | all-to-all | bytes 1179648 | tf_op jit(solution)/shard_map/all_to_all | solution.py:514
  37.5 0.0 copy-done
  37.5 0.9 %mix.1 = (f32[288,128]{1,0:T(8,128)S(1)}, f32[288,128]{1,0:T(8,128)S(1)}, f32[288,128]{1,0:T(8,128)S(1)}, f32[288,128]{1,0:T(8,128)S(1)}) custom-call(f32[32,9,4,128]{3,2,1,0:T(4,128)S(1)} %all_to_all.5.in_ref, f32[16,72,72]{2,1,0:T(8,128)S(1)} %bitcast.21), custom_call_target="tpu_custom_call" | custom-call | tf_op jit(solution)/shard_map/mix/pallas_call | solution.py:522
  38.4 2.0 %collective-permute-start.7 = (f32[288,128]{1,0:T(8,128)S(1)}, f32[288,128]{1,0:T(8,128)S(1)}, u32[]{:S(2)}, u32[]{:S(2)}) collective-permute-start(f32[288,128]{1,0:T(8,128)S(1)} %get-tuple-element.20), channel_id=1, source_target_pairs={{0,2},{1,3},{2,0},{3,1},{4,6},{5,7},{6,4},{7,5},{8,10},{9,11},{10,... | collective-permute-start | bytes 442376 | tf_op jit(solution)/shard_map/ppermute | solution.py:20
  40.4 1.5 %collective-permute-start.8 = (f32[288,128]{1,0:T(8,128)S(1)}, f32[288,128]{1,0:T(8,128)S(1)}, u32[]{:S(2)}, u32[]{:S(2)}) collective-permute-start(f32[288,128]{1,0:T(8,128)S(1)} %get-tuple-element.21), channel_id=1, source_target_pairs={{0,1},{1,2},{2,3},{3,0},{4,5},{5,6},{6,7},{7,4},{8,9},{9,10},{10,1... | collective-permute-start | bytes 442376 | tf_op jit(solution)/shard_map/ppermute | solution.py:20
  41.9 2.3 %collective-permute-start.9 = (f32[288,128]{1,0:T(8,128)S(1)}, f32[288,128]{1,0:T(8,128)S(1)}, u32[]{:S(2)}, u32[]{:S(2)}) collective-permute-start(f32[288,128]{1,0:T(8,128)S(1)} %get-tuple-element.22), channel_id=1, source_target_pairs={{0,3},{1,0},{2,1},{3,2},{4,7},{5,4},{6,5},{7,6},{8,11},{9,8},{10,9... | collective-permute-start | bytes 442376 | tf_op jit(solution)/shard_map/ppermute | solution.py:20
  44.2 7.9 %collective-permute-done.7.refs_1_ = f32[288,128]{1,0:T(8,128)S(1)} collective-permute-done((f32[288,128]{1,0:T(8,128)S(1)}, f32[288,128]{1,0:T(8,128)S(1)}, u32[]{:S(2)}, u32[]{:S(2)}) %collective-permute-start.7) | collective-permute-done | bytes 147488 | tf_op jit(solution)/shard_map/ppermute | solution.py:20
  52.1 0.0 collective-permute-done.8.refs_2_
  52.1 0.8 %collective-permute-done.9.refs_3_ = f32[288,128]{1,0:T(8,128)S(1)} collective-permute-done((f32[288,128]{1,0:T(8,128)S(1)}, f32[288,128]{1,0:T(8,128)S(1)}, u32[]{:S(2)}, u32[]{:S(2)}) %collective-permute-start.9) | collective-permute-done | bytes 147488 | tf_op jit(solution)/shard_map/ppermute | solution.py:20
  52.9 0.9 %place.1 = f32[8,18,8,128]{3,2,1,0:T(8,128)} custom-call(f32[288,128]{1,0:T(8,128)S(1)} %get-tuple-element.19.refs_0_, f32[288,128]{1,0:T(8,128)S(1)} %collective-permute-done.7.refs_1_, f32[288,128]{1,0:T(8,128)S(1)} %collective-permute-done.8.refs_2_, f32[288,128]{1,0:T(8,128)S(1)} %collective-permute-done.9.refs_3_), custom_call_target="tpu_custom_call" | custom-call | tf_op jit(solution)/shard_map/place/pallas_call | solution.py:539
  (1 shorter events, 0.0 us)
Async XLA Ops:
  1.3 4.6 %collective-permute-start = (f32[4,19,8,128]{3,2,1,0:T(8,128)S(1)}, f32[4,19,8,128]{3,2,1,0:T(8,128)S(1)}, u32[]{:S(2)}, u32[]{:S(2)}) collective-permute-start(f32[4,19,8,128]{3,2,1,0:T(8,128)S(1)} %get-tuple-element.15), channel_id=1, source_target_pairs={{0,4},{4,0},{8,12},{12,8},{16,20},{20,16},{24,28},{28,24},{1,5},{5... | collective-permute-start | bytes 933896 | tf_op jit(solution)/shard_map/ppermute | solution.py:75
  1.8 7.6 %collective-permute-start.1 = (f32[152,128]{1,0:T(8,128)S(1)}, f32[152,128]{1,0:T(8,128)S(1)}, u32[]{:S(2)}, u32[]{:S(2)}) collective-permute-start(f32[152,128]{1,0:T(8,128)S(1)} %bitcast.25), channel_id=1, source_target_pairs={{0,8},{4,12},{8,0},{12,4},{16,24},{20,28},{24,16},{28,20},{1,9},{5... | collective-permute-start | bytes 233480 | tf_op jit(solution)/shard_map/ppermute | solution.py:75
  4.3 6.2 %collective-permute-start.3 = (f32[152,128]{1,0:T(8,128)S(1)}, f32[152,128]{1,0:T(8,128)S(1)}, u32[]{:S(2)}, u32[]{:S(2)}) collective-permute-start(f32[152,128]{1,0:T(8,128)S(1)} %bitcast.24), channel_id=1, source_target_pairs={{0,16},{4,20},{8,24},{12,28},{16,0},{20,4},{24,8},{28,12},{1,17},{... | collective-permute-start | bytes 233480 | tf_op jit(solution)/shard_map/ppermute | solution.py:75
  5.9 6.0 %collective-permute-start.5 = (f32[152,128]{1,0:T(8,128)S(1)}, f32[152,128]{1,0:T(8,128)S(1)}, u32[]{:S(2)}, u32[]{:S(2)}) collective-permute-start(f32[152,128]{1,0:T(8,128)S(1)} %bitcast.23), channel_id=1, source_target_pairs={{0,24},{4,28},{8,16},{12,20},{16,8},{20,12},{24,0},{28,4},{1,25},{... | collective-permute-start | bytes 233480 | tf_op jit(solution)/shard_map/ppermute | solution.py:75
  5.9 7.2 %collective-permute-start.6 = (f32[152,128]{1,0:T(8,128)S(1)}, f32[152,128]{1,0:T(8,128)S(1)}, u32[]{:S(2)}, u32[]{:S(2)}) collective-permute-start(f32[152,128]{1,0:T(8,128)S(1)} %get-tuple-element.23), channel_id=1, source_target_pairs={{0,24},{4,28},{8,16},{12,20},{16,8},{20,12},{24,0},{28,4},{1,25},{... | collective-permute-start | bytes 233480 | tf_op jit(solution)/shard_map/ppermute | solution.py:75
  8.9 5.4 %collective-permute-start.4 = (f32[152,128]{1,0:T(8,128)S(1)}, f32[152,128]{1,0:T(8,128)S(1)}, u32[]{:S(2)}, u32[]{:S(2)}) collective-permute-start(f32[152,128]{1,0:T(8,128)S(1)} %get-tuple-element.24), channel_id=1, source_target_pairs={{0,16},{4,20},{8,24},{12,28},{16,0},{20,4},{24,8},{28,12},{1,17},{... | collective-permute-start | bytes 233480 | tf_op jit(solution)/shard_map/ppermute | solution.py:75
  9.4 4.9 %collective-permute-start.2 = (f32[152,128]{1,0:T(8,128)S(1)}, f32[152,128]{1,0:T(8,128)S(1)}, u32[]{:S(2)}, u32[]{:S(2)}) collective-permute-start(f32[152,128]{1,0:T(8,128)S(1)} %get-tuple-element.25), channel_id=1, source_target_pairs={{0,8},{4,12},{8,0},{12,4},{16,24},{20,28},{24,16},{28,20},{1,9},{5... | collective-permute-start | bytes 233480 | tf_op jit(solution)/shard_map/ppermute | solution.py:75
  17.5 19.9 %copy-start = (f32[1,2,8,72,72]{4,3,2,1,0:T(8,128)S(1)}, f32[1,2,8,72,72]{4,3,2,1,0:T(8,128)}, u32[]{:S(2)}) copy-start(f32[1,2,8,72,72]{4,3,2,1,0:T(8,128)} %param.8) | copy-start | bytes 995332
  38.4 13.7 %collective-permute-start.7 = (f32[288,128]{1,0:T(8,128)S(1)}, f32[288,128]{1,0:T(8,128)S(1)}, u32[]{:S(2)}, u32[]{:S(2)}) collective-permute-start(f32[288,128]{1,0:T(8,128)S(1)} %get-tuple-element.20), channel_id=1, source_target_pairs={{0,2},{1,3},{2,0},{3,1},{4,6},{5,7},{6,4},{7,5},{8,10},{9,11},{10,... | collective-permute-start | bytes 442376 | tf_op jit(solution)/shard_map/ppermute | solution.py:20
  40.4 11.7 %collective-permute-start.8 = (f32[288,128]{1,0:T(8,128)S(1)}, f32[288,128]{1,0:T(8,128)S(1)}, u32[]{:S(2)}, u32[]{:S(2)}) collective-permute-start(f32[288,128]{1,0:T(8,128)S(1)} %get-tuple-element.21), channel_id=1, source_target_pairs={{0,1},{1,2},{2,3},{3,0},{4,5},{5,6},{6,7},{7,4},{8,9},{9,10},{10,1... | collective-permute-start | bytes 442376 | tf_op jit(solution)/shard_map/ppermute | solution.py:20
  41.9 11.0 %collective-permute-start.9 = (f32[288,128]{1,0:T(8,128)S(1)}, f32[288,128]{1,0:T(8,128)S(1)}, u32[]{:S(2)}, u32[]{:S(2)}) collective-permute-start(f32[288,128]{1,0:T(8,128)S(1)} %get-tuple-element.22), channel_id=1, source_target_pairs={{0,3},{1,0},{2,1},{3,2},{4,7},{5,4},{6,5},{7,6},{8,11},{9,8},{10,9... | collective-permute-start | bytes 442376 | tf_op jit(solution)/shard_map/ppermute | solution.py:20

commit v6 on v5

--- a/solution.py
+++ b/solution.py
@@ -422,7 +422,8 @@
         w_high = weights.astype(jnp.bfloat16)
         w_low = (weights - w_high.astype(jnp.float32)).astype(jnp.bfloat16)
         dot = functools.partial(jnp.dot, preferred_element_type=jnp.float32)
-        total = dot(w_high, x_high) + (dot(w_high, x_low) + dot(w_low, x_high))
+        both = dot(w_high, jnp.concatenate([x_high, x_low], axis=1))
+        total = both[:, :LANES] + (both[:, LANES:] + dot(w_low, x_high))
         all_ref[pl.ds(own, p.all_levels, stride=p.own_cells), :] = 0.6 * x + scale * total
     me = lax.axis_index("lev")
     size = p.levels * p.own_cells
@@ -431,12 +432,12 @@
         out_refs[s][...] = all_ref[pl.ds(pl.multiple_of(layer * size, SUBLANES), size), :]
 
 
-def place_kernel(p, order, *refs):
-    in_refs, out_ref, sems = refs[: p.layers], refs[p.layers], refs[p.layers + 1]
+def place_kernel(p, shifts, *refs):
+    in_refs, out_ref, sems = refs[: len(shifts)], refs[-2], refs[-1]
     me = lax.axis_index("lev")
     tall = p.own_cells // p.side
     copies = []
-    for n, s in enumerate(order):
+    for n, s in enumerate(shifts):
         layer = lax.rem(me - s + p.layers, p.layers)
         piece = in_refs[n].reshape(p.levels, tall, p.side, LANES)
         for r in range(tall):
@@ -536,15 +537,22 @@
     )
     pieces = [mixed[0]] + [passed_along(mixed[s], "lev", s) for s in range(1, p.layers)]
     order = sorted(range(p.layers), key=lambda s: -min(s, p.layers - s) if s else -p.layers)
-    placed = pl.pallas_call(
-        functools.partial(place_kernel, p, order),
-        out_shape=jax.ShapeDtypeStruct(across, f32),
-        in_specs=in_vmem(p.layers),
-        out_specs=pl.BlockSpec(memory_space=pltpu.HBM),
-        scratch_shapes=[pltpu.SemaphoreType.DMA((p.cells // p.side,))],
-        compiler_params=params(),
-        name="place",
-    )(*(pieces[s] for s in order))
+    placed = None
+    for shifts in (order[:2], order[2:]):
+        before = [] if placed is None else [placed]
+        placed = pl.pallas_call(
+            functools.partial(place_kernel, p, shifts),
+            out_shape=jax.ShapeDtypeStruct(across, f32),
+            in_specs=in_vmem(len(shifts))
+            + [pl.BlockSpec(memory_space=pltpu.HBM)] * len(before),
+            out_specs=pl.BlockSpec(memory_space=pltpu.HBM),
+            scratch_shapes=[
+                pltpu.SemaphoreType.DMA((len(shifts) * p.own_cells // p.side,))
+            ],
+            input_output_aliases={len(shifts): 0} if before else {},
+            compiler_params=params(),
+            name="place",
+        )(*(pieces[s] for s in shifts), *before)
     return placed.transpose(0, 2, 1, 3)[None]
 
 

time: 54.3 us -> 54 us (level)
  waiting for transfers between devices: 13.5 us -> 12.7 us
    ppermute x3, waiting for transfers between devices: 8.74 us -> 7.98 us  [passed_along(): return lax.ppermute(value, axis, pairs)]
    pallas_call x1 -> x2, Pallas kernels: 0.87 us -> 1.48 us  [by_levels(): pl.pallas_call(functools.partial(place_kernel, p, shifts), out_shape=jax....]
  transfers between devices with their start and end apart: 10 -> 10, of which waited for: 6 -> 6; matrix products, arithmetic and copies ran while one was open for 0% -> 0% of each run, Pallas kernels for 0% -> 1%
where the time goes in v6:
time: 54 us; the launch traced here: 53.5 us
  blocking collectives  19.9 us (37%)
  starting transfers between devices  14 us (26%)
  waiting for transfers between devices  12.7 us (24%)
  Pallas kernels  6.75 us (12%)
    all_to_all x1, blocking collectives, by_levels(): lax.all_to_all(moved, ('tile', 'lev'), split_axis=0, concat_axis=0, tiled...  19.9 us
    ppermute x7, starting transfers between devices, swapped(): return lax.ppermute(value, axis, pairs)  8.23 us
    ppermute x3, waiting for transfers between devices, passed_along(): return lax.ppermute(value, axis, pairs)  7.98 us
    ppermute x3, starting transfers between devices, passed_along(): return lax.ppermute(value, axis, pairs)  5.82 us
    ppermute x7, waiting for transfers between devices, swapped(): return lax.ppermute(value, axis, pairs)  4.72 us
    pallas_call x1, Pallas kernels, by_levels(): pl.pallas_call(functools.partial(advect_kernel, p, tile_stride(p.tiles)),...  3.29 us
    pallas_call x2, Pallas kernels, by_levels(): pl.pallas_call(functools.partial(place_kernel, p, shifts), out_shape=jax....  1.48 us
    pallas_call x1, Pallas kernels, by_levels(): pl.pallas_call(functools.partial(pack_kernel, p), out_shape=[jax.ShapeDty...  1.24 us
  transfers between devices with their start and end apart: 10, of which 6 were waited for; matrix products, arithmetic and copies ran while one was open for 0% of the time, Pallas kernels for 1%

profile of v6, /device:TPU:0, one launch (start us, length us, event | category | flops | bytes accessed | tf_op | source)
XLA Modules:
  0.0 53.5 jit_solution(15621069131119851205)
XLA Ops:
  0.0 1.2 %pack.1 = (f32[19,8,128]{2,1,0:T(8,128)S(1)}, f32[19,8,128]{2,1,0:T(8,128)S(1)}, f32[19,8,128]{2,1,0:T(8,128)S(1)}, f32[19,8,128]{2,1,0:T(8,128)S(1)}, f32[4,19,8,128]{3,2,1,0:T(8,128)S(1)}) custom-call(f32[8,18,8,128]{3,2,1,0:T(8,128)} %bitcast.26, f32[8,8,18]{2,1,0:T(8,128)} %bitcast.27, f32[8,8,18]{2,1,0:T(8,128)} %bitcast.28, s32[1,2]{1,0:T(1,128)} %flip_ref.1), custom_call_target="tpu_custom_call" | custom-call | tf_op jit(solution)/shard_map/pack/pallas_call | solution.py:467
  1.3 0.5 collective-permute-start
  1.8 2.6 %collective-permute-start.1 = (f32[152,128]{1,0:T(8,128)S(1)}, f32[152,128]{1,0:T(8,128)S(1)}, u32[]{:S(2)}, u32[]{:S(2)}) collective-permute-start(f32[152,128]{1,0:T(8,128)S(1)} %bitcast.25), channel_id=1, source_target_pairs={{0,8},{4,12},{8,0},{12,4},{16,24},{20,28},{24,16},{28,20},{1,9},{5... | collective-permute-start | bytes 233480 | tf_op jit(solution)/shard_map/ppermute | solution.py:75
  4.3 1.5 %collective-permute-start.3 = (f32[152,128]{1,0:T(8,128)S(1)}, f32[152,128]{1,0:T(8,128)S(1)}, u32[]{:S(2)}, u32[]{:S(2)}) collective-permute-start(f32[152,128]{1,0:T(8,128)S(1)} %bitcast.24), channel_id=1, source_target_pairs={{0,16},{4,20},{8,24},{12,28},{16,0},{20,4},{24,8},{28,12},{1,17},{... | collective-permute-start | bytes 233480 | tf_op jit(solution)/shard_map/ppermute | solution.py:75
  5.9 0.0 collective-permute-start.5
  5.9 0.0 collective-permute-done
  5.9 3.0 %collective-permute-start.6 = (f32[152,128]{1,0:T(8,128)S(1)}, f32[152,128]{1,0:T(8,128)S(1)}, u32[]{:S(2)}, u32[]{:S(2)}) collective-permute-start(f32[152,128]{1,0:T(8,128)S(1)} %get-tuple-element.23), channel_id=1, source_target_pairs={{0,24},{4,28},{8,16},{12,20},{16,8},{20,12},{24,0},{28,4},{1,25},{... | collective-permute-start | bytes 233480 | tf_op jit(solution)/shard_map/ppermute | solution.py:75
  8.9 0.5 collective-permute-start.4
  9.4 0.0 collective-permute-done.1.refs_2_
  9.4 0.1 collective-permute-start.2
  9.5 1.0 %collective-permute-done.3.refs_4_ = f32[152,128]{1,0:T(8,128)S(1)} collective-permute-done((f32[152,128]{1,0:T(8,128)S(1)}, f32[152,128]{1,0:T(8,128)S(1)}, u32[]{:S(2)}, u32[]{:S(2)}) %collective-permute-start.3) | collective-permute-done | bytes 77856 | tf_op jit(solution)/shard_map/ppermute | solution.py:75
  10.5 1.3 %collective-permute-done.5.refs_6_ = f32[152,128]{1,0:T(8,128)S(1)} collective-permute-done((f32[152,128]{1,0:T(8,128)S(1)}, f32[152,128]{1,0:T(8,128)S(1)}, u32[]{:S(2)}, u32[]{:S(2)}) %collective-permute-start.5) | collective-permute-done | bytes 77856 | tf_op jit(solution)/shard_map/ppermute | solution.py:75
  11.8 1.3 %collective-permute-done.6.refs_7_ = f32[152,128]{1,0:T(8,128)S(1)} collective-permute-done((f32[152,128]{1,0:T(8,128)S(1)}, f32[152,128]{1,0:T(8,128)S(1)}, u32[]{:S(2)}, u32[]{:S(2)}) %collective-permute-start.6) | collective-permute-done | bytes 77856 | tf_op jit(solution)/shard_map/ppermute | solution.py:75
  13.1 1.1 %collective-permute-done.4.refs_5_ = f32[152,128]{1,0:T(8,128)S(1)} collective-permute-done((f32[152,128]{1,0:T(8,128)S(1)}, f32[152,128]{1,0:T(8,128)S(1)}, u32[]{:S(2)}, u32[]{:S(2)}) %collective-permute-start.4) | collective-permute-done | bytes 77856 | tf_op jit(solution)/shard_map/ppermute | solution.py:75
  14.2 0.0 collective-permute-done.2.refs_3_
  14.2 3.3 %advect.1 = f32[32,9,4,128]{3,2,1,0:T(4,128)S(1)} custom-call(f32[152,128]{1,0:T(8,128)S(1)} %bitcast.22, f32[152,128]{1,0:T(8,128)S(1)} %get-tuple-element.26.refs_1_, f32[152,128]{1,0:T(8,128)S(1)} %collective-permute-done.1.refs_2_, f32[152,128]{1,0:T(8,128)S(1)} %collective-permute-done.2.refs_3_, f32[152,128]{1,0:T(8,128)S(1)} %collective-permute-done.3.refs_4_, ...), custom_call_target="tpu_custom_call" | custom-call | tf_op jit(solution)/shard_map/advect/pallas_call | solution.py:500
  17.5 0.0 copy-start
  17.5 19.9 %all_to_all.5.in_ref = f32[32,9,4,128]{3,2,1,0:T(4,128)S(1)} all-to-all(f32[32,9,4,128]{3,2,1,0:T(4,128)S(1)} %advect.1), channel_id=1, replica_groups=mesh['tile'=8,'lev'=4] {'tile','lev'}, dimensions={0} | all-to-all | bytes 1179648 | tf_op jit(solution)/shard_map/all_to_all | solution.py:515
  37.5 0.0 copy-done
  37.5 0.7 %mix.1 = (f32[288,128]{1,0:T(8,128)S(1)}, f32[288,128]{1,0:T(8,128)S(1)}, f32[288,128]{1,0:T(8,128)S(1)}, f32[288,128]{1,0:T(8,128)S(1)}) custom-call(f32[32,9,4,128]{3,2,1,0:T(4,128)S(1)} %all_to_all.5.in_ref, f32[16,72,72]{2,1,0:T(8,128)S(1)} %bitcast.21), custom_call_target="tpu_custom_call" | custom-call | tf_op jit(solution)/shard_map/mix/pallas_call | solution.py:523
  38.2 2.0 %collective-permute-start.9 = (f32[288,128]{1,0:T(8,128)S(1)}, f32[288,128]{1,0:T(8,128)S(1)}, u32[]{:S(2)}, u32[]{:S(2)}) collective-permute-start(f32[288,128]{1,0:T(8,128)S(1)} %get-tuple-element.22), channel_id=1, source_target_pairs={{0,2},{1,3},{2,0},{3,1},{4,6},{5,7},{6,4},{7,5},{8,10},{9,11},{10,... | collective-permute-start | bytes 442376 | tf_op jit(solution)/shard_map/ppermute | solution.py:20
  40.2 1.6 %collective-permute-start.7 = (f32[288,128]{1,0:T(8,128)S(1)}, f32[288,128]{1,0:T(8,128)S(1)}, u32[]{:S(2)}, u32[]{:S(2)}) collective-permute-start(f32[288,128]{1,0:T(8,128)S(1)} %get-tuple-element.19), channel_id=1, source_target_pairs={{0,1},{1,2},{2,3},{3,0},{4,5},{5,6},{6,7},{7,4},{8,9},{9,10},{10,1... | collective-permute-start | bytes 442376 | tf_op jit(solution)/shard_map/ppermute | solution.py:20
  41.8 2.3 %collective-permute-start.8 = (f32[288,128]{1,0:T(8,128)S(1)}, f32[288,128]{1,0:T(8,128)S(1)}, u32[]{:S(2)}, u32[]{:S(2)}) collective-permute-start(f32[288,128]{1,0:T(8,128)S(1)} %get-tuple-element.20), channel_id=1, source_target_pairs={{0,3},{1,0},{2,1},{3,2},{4,7},{5,4},{6,5},{7,6},{8,11},{9,8},{10,9... | collective-permute-start | bytes 442376 | tf_op jit(solution)/shard_map/ppermute | solution.py:20
  44.0 7.9 %collective-permute-done.9.refs_1_ = f32[288,128]{1,0:T(8,128)S(1)} collective-permute-done((f32[288,128]{1,0:T(8,128)S(1)}, f32[288,128]{1,0:T(8,128)S(1)}, u32[]{:S(2)}, u32[]{:S(2)}) %collective-permute-start.9) | collective-permute-done | bytes 147488 | tf_op jit(solution)/shard_map/ppermute | solution.py:20
  51.9 0.7 %place.2.refs_2_ = f32[8,18,8,128]{3,2,1,0:T(8,128)} custom-call(f32[288,128]{1,0:T(8,128)S(1)} %get-tuple-element.21.refs_0_, f32[288,128]{1,0:T(8,128)S(1)} %collective-permute-done.9.refs_1_), custom_call_target="tpu_custom_call" | custom-call | tf_op jit(solution)/shard_map/place/pallas_call | solution.py:543
  52.7 0.0 collective-permute-done.7.refs_0_
  52.7 0.1 collective-permute-done.8.refs_1_
  52.8 0.7 %place.3 = f32[8,18,8,128]{3,2,1,0:T(8,128)} custom-call(f32[288,128]{1,0:T(8,128)S(1)} %collective-permute-done.7.refs_0_, f32[288,128]{1,0:T(8,128)S(1)} %collective-permute-done.8.refs_1_, f32[8,18,8,128]{3,2,1,0:T(8,128)} %place.2.refs_2_), custom_call_target="tpu_custom_call", output_to_operand_aliasing={{}: (2, {})} | custom-call | tf_op jit(solution)/shard_map/place/pallas_call | solution.py:543
  (1 shorter events, 0.0 us)
Async XLA Ops:
  1.3 4.6 %collective-permute-start = (f32[4,19,8,128]{3,2,1,0:T(8,128)S(1)}, f32[4,19,8,128]{3,2,1,0:T(8,128)S(1)}, u32[]{:S(2)}, u32[]{:S(2)}) collective-permute-start(f32[4,19,8,128]{3,2,1,0:T(8,128)S(1)} %get-tuple-element.15), channel_id=1, source_target_pairs={{0,4},{4,0},{8,12},{12,8},{16,20},{20,16},{24,28},{28,24},{1,5},{5... | collective-permute-start | bytes 933896 | tf_op jit(solution)/shard_map/ppermute | solution.py:75
  1.8 7.6 %collective-permute-start.1 = (f32[152,128]{1,0:T(8,128)S(1)}, f32[152,128]{1,0:T(8,128)S(1)}, u32[]{:S(2)}, u32[]{:S(2)}) collective-permute-start(f32[152,128]{1,0:T(8,128)S(1)} %bitcast.25), channel_id=1, source_target_pairs={{0,8},{4,12},{8,0},{12,4},{16,24},{20,28},{24,16},{28,20},{1,9},{5... | collective-permute-start | bytes 233480 | tf_op jit(solution)/shard_map/ppermute | solution.py:75
  4.3 6.2 %collective-permute-start.3 = (f32[152,128]{1,0:T(8,128)S(1)}, f32[152,128]{1,0:T(8,128)S(1)}, u32[]{:S(2)}, u32[]{:S(2)}) collective-permute-start(f32[152,128]{1,0:T(8,128)S(1)} %bitcast.24), channel_id=1, source_target_pairs={{0,16},{4,20},{8,24},{12,28},{16,0},{20,4},{24,8},{28,12},{1,17},{... | collective-permute-start | bytes 233480 | tf_op jit(solution)/shard_map/ppermute | solution.py:75
  5.9 6.0 %collective-permute-start.5 = (f32[152,128]{1,0:T(8,128)S(1)}, f32[152,128]{1,0:T(8,128)S(1)}, u32[]{:S(2)}, u32[]{:S(2)}) collective-permute-start(f32[152,128]{1,0:T(8,128)S(1)} %bitcast.23), channel_id=1, source_target_pairs={{0,24},{4,28},{8,16},{12,20},{16,8},{20,12},{24,0},{28,4},{1,25},{... | collective-permute-start | bytes 233480 | tf_op jit(solution)/shard_map/ppermute | solution.py:75
  5.9 7.2 %collective-permute-start.6 = (f32[152,128]{1,0:T(8,128)S(1)}, f32[152,128]{1,0:T(8,128)S(1)}, u32[]{:S(2)}, u32[]{:S(2)}) collective-permute-start(f32[152,128]{1,0:T(8,128)S(1)} %get-tuple-element.23), channel_id=1, source_target_pairs={{0,24},{4,28},{8,16},{12,20},{16,8},{20,12},{24,0},{28,4},{1,25},{... | collective-permute-start | bytes 233480 | tf_op jit(solution)/shard_map/ppermute | solution.py:75
  8.9 5.4 %collective-permute-start.4 = (f32[152,128]{1,0:T(8,128)S(1)}, f32[152,128]{1,0:T(8,128)S(1)}, u32[]{:S(2)}, u32[]{:S(2)}) collective-permute-start(f32[152,128]{1,0:T(8,128)S(1)} %get-tuple-element.24), channel_id=1, source_target_pairs={{0,16},{4,20},{8,24},{12,28},{16,0},{20,4},{24,8},{28,12},{1,17},{... | collective-permute-start | bytes 233480 | tf_op jit(solution)/shard_map/ppermute | solution.py:75
  9.4 4.9 %collective-permute-start.2 = (f32[152,128]{1,0:T(8,128)S(1)}, f32[152,128]{1,0:T(8,128)S(1)}, u32[]{:S(2)}, u32[]{:S(2)}) collective-permute-start(f32[152,128]{1,0:T(8,128)S(1)} %get-tuple-element.25), channel_id=1, source_target_pairs={{0,8},{4,12},{8,0},{12,4},{16,24},{20,28},{24,16},{28,20},{1,9},{5... | collective-permute-start | bytes 233480 | tf_op jit(solution)/shard_map/ppermute | solution.py:75
  17.5 19.9 %copy-start = (f32[1,2,8,72,72]{4,3,2,1,0:T(8,128)S(1)}, f32[1,2,8,72,72]{4,3,2,1,0:T(8,128)}, u32[]{:S(2)}) copy-start(f32[1,2,8,72,72]{4,3,2,1,0:T(8,128)} %param.8) | copy-start | bytes 995332
  38.2 13.7 %collective-permute-start.9 = (f32[288,128]{1,0:T(8,128)S(1)}, f32[288,128]{1,0:T(8,128)S(1)}, u32[]{:S(2)}, u32[]{:S(2)}) collective-permute-start(f32[288,128]{1,0:T(8,128)S(1)} %get-tuple-element.22), channel_id=1, source_target_pairs={{0,2},{1,3},{2,0},{3,1},{4,6},{5,7},{6,4},{7,5},{8,10},{9,11},{10,... | collective-permute-start | bytes 442376 | tf_op jit(solution)/shard_map/ppermute | solution.py:20
  40.2 12.5 %collective-permute-start.7 = (f32[288,128]{1,0:T(8,128)S(1)}, f32[288,128]{1,0:T(8,128)S(1)}, u32[]{:S(2)}, u32[]{:S(2)}) collective-permute-start(f32[288,128]{1,0:T(8,128)S(1)} %get-tuple-element.19), channel_id=1, source_target_pairs={{0,1},{1,2},{2,3},{3,0},{4,5},{5,6},{6,7},{7,4},{8,9},{9,10},{10,1... | collective-permute-start | bytes 442376 | tf_op jit(solution)/shard_map/ppermute | solution.py:20
  41.8 11.0 %collective-permute-start.8 = (f32[288,128]{1,0:T(8,128)S(1)}, f32[288,128]{1,0:T(8,128)S(1)}, u32[]{:S(2)}, u32[]{:S(2)}) collective-permute-start(f32[288,128]{1,0:T(8,128)S(1)} %get-tuple-element.20), channel_id=1, source_target_pairs={{0,3},{1,0},{2,1},{3,2},{4,7},{5,4},{6,5},{7,6},{8,11},{9,8},{10,9... | collective-permute-start | bytes 442376 | tf_op jit(solution)/shard_map/ppermute | solution.py:20

commit v7 on v6

--- a/solution.py
+++ b/solution.py
@@ -294,11 +294,8 @@
     courant = row(p.courant_at + p.full)
     for way in range(2):
         for r in range(p.part_rows):
-            c = None
-            for m in range(p.groups):
-                at = way * cells + m * p.part_rows + r
-                value = jnp.broadcast_to(courant[:, at : at + 1], shape)
-                c = value if c is None else jnp.where(group == m, value, c)
+            at = group * p.part_rows + (way * cells + r)
+            c = jnp.take_along_axis(courant, at, axis=1)
             set_faces(tail_faces + way * p.part_rows + r, c)
 
     def sweep(at, faces_at, step, length, up, down):

time: 54 us -> 53.9 us (level)
  no operation moved by 1% of the time
where the time goes in v7:
time: 53.9 us; the launch traced here: 53.4 us
  blocking collectives  19.9 us (37%)
  starting transfers between devices  14 us (26%)
  waiting for transfers between devices  12.7 us (24%)
  Pallas kernels  6.67 us (12%)
    all_to_all x1, blocking collectives, by_levels(): lax.all_to_all(moved, ('tile', 'lev'), split_axis=0, concat_axis=0, tiled...  19.9 us
    ppermute x7, starting transfers between devices, swapped(): return lax.ppermute(value, axis, pairs)  8.23 us
    ppermute x3, waiting for transfers between devices, passed_along(): return lax.ppermute(value, axis, pairs)  7.98 us
    ppermute x3, starting transfers between devices, passed_along(): return lax.ppermute(value, axis, pairs)  5.81 us
    ppermute x7, waiting for transfers between devices, swapped(): return lax.ppermute(value, axis, pairs)  4.72 us
    pallas_call x1, Pallas kernels, by_levels(): pl.pallas_call(functools.partial(advect_kernel, p, tile_stride(p.tiles)),...  3.2 us
    pallas_call x2, Pallas kernels, by_levels(): pl.pallas_call(functools.partial(place_kernel, p, shifts), out_shape=jax....  1.48 us
    pallas_call x1, Pallas kernels, by_levels(): pl.pallas_call(functools.partial(pack_kernel, p), out_shape=[jax.ShapeDty...  1.24 us
  transfers between devices with their start and end apart: 10, of which 6 were waited for; matrix products, arithmetic and copies ran while one was open for 0% of the time, Pallas kernels for 1%

profile of v7, /device:TPU:0, one launch (start us, length us, event | category | flops | bytes accessed | tf_op | source)
XLA Modules:
  0.0 53.4 jit_solution(800488288905151830)
XLA Ops:
  0.0 1.2 %pack.1 = (f32[19,8,128]{2,1,0:T(8,128)S(1)}, f32[19,8,128]{2,1,0:T(8,128)S(1)}, f32[19,8,128]{2,1,0:T(8,128)S(1)}, f32[19,8,128]{2,1,0:T(8,128)S(1)}, f32[4,19,8,128]{3,2,1,0:T(8,128)S(1)}) custom-call(f32[8,18,8,128]{3,2,1,0:T(8,128)} %bitcast.26, f32[8,8,18]{2,1,0:T(8,128)} %bitcast.27, f32[8,8,18]{2,1,0:T(8,128)} %bitcast.28, s32[1,2]{1,0:T(1,128)} %flip_ref.1), custom_call_target="tpu_custom_call" | custom-call | tf_op jit(solution)/shard_map/pack/pallas_call | solution.py:464
  1.3 0.5 collective-permute-start
  1.8 2.6 %collective-permute-start.1 = (f32[152,128]{1,0:T(8,128)S(1)}, f32[152,128]{1,0:T(8,128)S(1)}, u32[]{:S(2)}, u32[]{:S(2)}) collective-permute-start(f32[152,128]{1,0:T(8,128)S(1)} %bitcast.25), channel_id=1, source_target_pairs={{0,8},{4,12},{8,0},{12,4},{16,24},{20,28},{24,16},{28,20},{1,9},{5... | collective-permute-start | bytes 233480 | tf_op jit(solution)/shard_map/ppermute | solution.py:75
  4.3 1.5 %collective-permute-start.3 = (f32[152,128]{1,0:T(8,128)S(1)}, f32[152,128]{1,0:T(8,128)S(1)}, u32[]{:S(2)}, u32[]{:S(2)}) collective-permute-start(f32[152,128]{1,0:T(8,128)S(1)} %bitcast.24), channel_id=1, source_target_pairs={{0,16},{4,20},{8,24},{12,28},{16,0},{20,4},{24,8},{28,12},{1,17},{... | collective-permute-start | bytes 233480 | tf_op jit(solution)/shard_map/ppermute | solution.py:75
  5.9 0.0 collective-permute-start.5
  5.9 0.0 collective-permute-done
  5.9 3.0 %collective-permute-start.6 = (f32[152,128]{1,0:T(8,128)S(1)}, f32[152,128]{1,0:T(8,128)S(1)}, u32[]{:S(2)}, u32[]{:S(2)}) collective-permute-start(f32[152,128]{1,0:T(8,128)S(1)} %get-tuple-element.23), channel_id=1, source_target_pairs={{0,24},{4,28},{8,16},{12,20},{16,8},{20,12},{24,0},{28,4},{1,25},{... | collective-permute-start | bytes 233480 | tf_op jit(solution)/shard_map/ppermute | solution.py:75
  8.9 0.5 collective-permute-start.4
  9.4 0.0 collective-permute-done.1.refs_2_
  9.4 0.1 collective-permute-start.2
  9.5 1.0 %collective-permute-done.3.refs_4_ = f32[152,128]{1,0:T(8,128)S(1)} collective-permute-done((f32[152,128]{1,0:T(8,128)S(1)}, f32[152,128]{1,0:T(8,128)S(1)}, u32[]{:S(2)}, u32[]{:S(2)}) %collective-permute-start.3) | collective-permute-done | bytes 77856 | tf_op jit(solution)/shard_map/ppermute | solution.py:75
  10.5 1.3 %collective-permute-done.5.refs_6_ = f32[152,128]{1,0:T(8,128)S(1)} collective-permute-done((f32[152,128]{1,0:T(8,128)S(1)}, f32[152,128]{1,0:T(8,128)S(1)}, u32[]{:S(2)}, u32[]{:S(2)}) %collective-permute-start.5) | collective-permute-done | bytes 77856 | tf_op jit(solution)/shard_map/ppermute | solution.py:75
  11.8 1.3 %collective-permute-done.6.refs_7_ = f32[152,128]{1,0:T(8,128)S(1)} collective-permute-done((f32[152,128]{1,0:T(8,128)S(1)}, f32[152,128]{1,0:T(8,128)S(1)}, u32[]{:S(2)}, u32[]{:S(2)}) %collective-permute-start.6) | collective-permute-done | bytes 77856 | tf_op jit(solution)/shard_map/ppermute | solution.py:75
  13.1 1.1 %collective-permute-done.4.refs_5_ = f32[152,128]{1,0:T(8,128)S(1)} collective-permute-done((f32[152,128]{1,0:T(8,128)S(1)}, f32[152,128]{1,0:T(8,128)S(1)}, u32[]{:S(2)}, u32[]{:S(2)}) %collective-permute-start.4) | collective-permute-done | bytes 77856 | tf_op jit(solution)/shard_map/ppermute | solution.py:75
  14.2 0.0 collective-permute-done.2.refs_3_
  14.2 3.2 %advect.1 = f32[32,9,4,128]{3,2,1,0:T(4,128)S(1)} custom-call(f32[152,128]{1,0:T(8,128)S(1)} %bitcast.22, f32[152,128]{1,0:T(8,128)S(1)} %get-tuple-element.26.refs_1_, f32[152,128]{1,0:T(8,128)S(1)} %collective-permute-done.1.refs_2_, f32[152,128]{1,0:T(8,128)S(1)} %collective-permute-done.2.refs_3_, f32[152,128]{1,0:T(8,128)S(1)} %collective-permute-done.3.refs_4_, ...), custom_call_target="tpu_custom_call" | custom-call | tf_op jit(solution)/shard_map/advect/pallas_call | solution.py:497
  17.5 0.0 copy-start
  17.5 19.9 %all_to_all.5.in_ref = f32[32,9,4,128]{3,2,1,0:T(4,128)S(1)} all-to-all(f32[32,9,4,128]{3,2,1,0:T(4,128)S(1)} %advect.1), channel_id=1, replica_groups=mesh['tile'=8,'lev'=4] {'tile','lev'}, dimensions={0} | all-to-all | bytes 1179648 | tf_op jit(solution)/shard_map/all_to_all | solution.py:512
  37.4 0.0 copy-done
  37.4 0.7 %mix.1 = (f32[288,128]{1,0:T(8,128)S(1)}, f32[288,128]{1,0:T(8,128)S(1)}, f32[288,128]{1,0:T(8,128)S(1)}, f32[288,128]{1,0:T(8,128)S(1)}) custom-call(f32[32,9,4,128]{3,2,1,0:T(4,128)S(1)} %all_to_all.5.in_ref, f32[16,72,72]{2,1,0:T(8,128)S(1)} %bitcast.21), custom_call_target="tpu_custom_call" | custom-call | tf_op jit(solution)/shard_map/mix/pallas_call | solution.py:520
  38.1 2.0 %collective-permute-start.9 = (f32[288,128]{1,0:T(8,128)S(1)}, f32[288,128]{1,0:T(8,128)S(1)}, u32[]{:S(2)}, u32[]{:S(2)}) collective-permute-start(f32[288,128]{1,0:T(8,128)S(1)} %get-tuple-element.22), channel_id=1, source_target_pairs={{0,2},{1,3},{2,0},{3,1},{4,6},{5,7},{6,4},{7,5},{8,10},{9,11},{10,... | collective-permute-start | bytes 442376 | tf_op jit(solution)/shard_map/ppermute | solution.py:20
  40.1 1.6 %collective-permute-start.7 = (f32[288,128]{1,0:T(8,128)S(1)}, f32[288,128]{1,0:T(8,128)S(1)}, u32[]{:S(2)}, u32[]{:S(2)}) collective-permute-start(f32[288,128]{1,0:T(8,128)S(1)} %get-tuple-element.19), channel_id=1, source_target_pairs={{0,1},{1,2},{2,3},{3,0},{4,5},{5,6},{6,7},{7,4},{8,9},{9,10},{10,1... | collective-permute-start | bytes 442376 | tf_op jit(solution)/shard_map/ppermute | solution.py:20
  41.7 2.3 %collective-permute-start.8 = (f32[288,128]{1,0:T(8,128)S(1)}, f32[288,128]{1,0:T(8,128)S(1)}, u32[]{:S(2)}, u32[]{:S(2)}) collective-permute-start(f32[288,128]{1,0:T(8,128)S(1)} %get-tuple-element.20), channel_id=1, source_target_pairs={{0,3},{1,0},{2,1},{3,2},{4,7},{5,4},{6,5},{7,6},{8,11},{9,8},{10,9... | collective-permute-start | bytes 442376 | tf_op jit(solution)/shard_map/ppermute | solution.py:20
  44.0 7.9 %collective-permute-done.9.refs_1_ = f32[288,128]{1,0:T(8,128)S(1)} collective-permute-done((f32[288,128]{1,0:T(8,128)S(1)}, f32[288,128]{1,0:T(8,128)S(1)}, u32[]{:S(2)}, u32[]{:S(2)}) %collective-permute-start.9) | collective-permute-done | bytes 147488 | tf_op jit(solution)/shard_map/ppermute | solution.py:20
  51.9 0.7 %place.2.refs_2_ = f32[8,18,8,128]{3,2,1,0:T(8,128)} custom-call(f32[288,128]{1,0:T(8,128)S(1)} %get-tuple-element.21.refs_0_, f32[288,128]{1,0:T(8,128)S(1)} %collective-permute-done.9.refs_1_), custom_call_target="tpu_custom_call" | custom-call | tf_op jit(solution)/shard_map/place/pallas_call | solution.py:540
  52.6 0.0 collective-permute-done.7.refs_0_
  52.6 0.1 collective-permute-done.8.refs_1_
  52.7 0.7 %place.3 = f32[8,18,8,128]{3,2,1,0:T(8,128)} custom-call(f32[288,128]{1,0:T(8,128)S(1)} %collective-permute-done.7.refs_0_, f32[288,128]{1,0:T(8,128)S(1)} %collective-permute-done.8.refs_1_, f32[8,18,8,128]{3,2,1,0:T(8,128)} %place.2.refs_2_), custom_call_target="tpu_custom_call", output_to_operand_aliasing={{}: (2, {})} | custom-call | tf_op jit(solution)/shard_map/place/pallas_call | solution.py:540
  (1 shorter events, 0.0 us)
Async XLA Ops:
  1.3 4.6 %collective-permute-start = (f32[4,19,8,128]{3,2,1,0:T(8,128)S(1)}, f32[4,19,8,128]{3,2,1,0:T(8,128)S(1)}, u32[]{:S(2)}, u32[]{:S(2)}) collective-permute-start(f32[4,19,8,128]{3,2,1,0:T(8,128)S(1)} %get-tuple-element.15), channel_id=1, source_target_pairs={{0,4},{4,0},{8,12},{12,8},{16,20},{20,16},{24,28},{28,24},{1,5},{5... | collective-permute-start | bytes 933896 | tf_op jit(solution)/shard_map/ppermute | solution.py:75
  1.8 7.6 %collective-permute-start.1 = (f32[152,128]{1,0:T(8,128)S(1)}, f32[152,128]{1,0:T(8,128)S(1)}, u32[]{:S(2)}, u32[]{:S(2)}) collective-permute-start(f32[152,128]{1,0:T(8,128)S(1)} %bitcast.25), channel_id=1, source_target_pairs={{0,8},{4,12},{8,0},{12,4},{16,24},{20,28},{24,16},{28,20},{1,9},{5... | collective-permute-start | bytes 233480 | tf_op jit(solution)/shard_map/ppermute | solution.py:75
  4.3 6.2 %collective-permute-start.3 = (f32[152,128]{1,0:T(8,128)S(1)}, f32[152,128]{1,0:T(8,128)S(1)}, u32[]{:S(2)}, u32[]{:S(2)}) collective-permute-start(f32[152,128]{1,0:T(8,128)S(1)} %bitcast.24), channel_id=1, source_target_pairs={{0,16},{4,20},{8,24},{12,28},{16,0},{20,4},{24,8},{28,12},{1,17},{... | collective-permute-start | bytes 233480 | tf_op jit(solution)/shard_map/ppermute | solution.py:75
  5.9 6.0 %collective-permute-start.5 = (f32[152,128]{1,0:T(8,128)S(1)}, f32[152,128]{1,0:T(8,128)S(1)}, u32[]{:S(2)}, u32[]{:S(2)}) collective-permute-start(f32[152,128]{1,0:T(8,128)S(1)} %bitcast.23), channel_id=1, source_target_pairs={{0,24},{4,28},{8,16},{12,20},{16,8},{20,12},{24,0},{28,4},{1,25},{... | collective-permute-start | bytes 233480 | tf_op jit(solution)/shard_map/ppermute | solution.py:75
  5.9 7.2 %collective-permute-start.6 = (f32[152,128]{1,0:T(8,128)S(1)}, f32[152,128]{1,0:T(8,128)S(1)}, u32[]{:S(2)}, u32[]{:S(2)}) collective-permute-start(f32[152,128]{1,0:T(8,128)S(1)} %get-tuple-element.23), channel_id=1, source_target_pairs={{0,24},{4,28},{8,16},{12,20},{16,8},{20,12},{24,0},{28,4},{1,25},{... | collective-permute-start | bytes 233480 | tf_op jit(solution)/shard_map/ppermute | solution.py:75
  8.9 5.4 %collective-permute-start.4 = (f32[152,128]{1,0:T(8,128)S(1)}, f32[152,128]{1,0:T(8,128)S(1)}, u32[]{:S(2)}, u32[]{:S(2)}) collective-permute-start(f32[152,128]{1,0:T(8,128)S(1)} %get-tuple-element.24), channel_id=1, source_target_pairs={{0,16},{4,20},{8,24},{12,28},{16,0},{20,4},{24,8},{28,12},{1,17},{... | collective-permute-start | bytes 233480 | tf_op jit(solution)/shard_map/ppermute | solution.py:75
  9.4 4.9 %collective-permute-start.2 = (f32[152,128]{1,0:T(8,128)S(1)}, f32[152,128]{1,0:T(8,128)S(1)}, u32[]{:S(2)}, u32[]{:S(2)}) collective-permute-start(f32[152,128]{1,0:T(8,128)S(1)} %get-tuple-element.25), channel_id=1, source_target_pairs={{0,8},{4,12},{8,0},{12,4},{16,24},{20,28},{24,16},{28,20},{1,9},{5... | collective-permute-start | bytes 233480 | tf_op jit(solution)/shard_map/ppermute | solution.py:75
  17.5 19.9 %copy-start = (f32[1,2,8,72,72]{4,3,2,1,0:T(8,128)S(1)}, f32[1,2,8,72,72]{4,3,2,1,0:T(8,128)}, u32[]{:S(2)}) copy-start(f32[1,2,8,72,72]{4,3,2,1,0:T(8,128)} %param.8) | copy-start | bytes 995332
  38.1 13.7 %collective-permute-start.9 = (f32[288,128]{1,0:T(8,128)S(1)}, f32[288,128]{1,0:T(8,128)S(1)}, u32[]{:S(2)}, u32[]{:S(2)}) collective-permute-start(f32[288,128]{1,0:T(8,128)S(1)} %get-tuple-element.22), channel_id=1, source_target_pairs={{0,2},{1,3},{2,0},{3,1},{4,6},{5,7},{6,4},{7,5},{8,10},{9,11},{10,... | collective-permute-start | bytes 442376 | tf_op jit(solution)/shard_map/ppermute | solution.py:20
  40.1 12.5 %collective-permute-start.7 = (f32[288,128]{1,0:T(8,128)S(1)}, f32[288,128]{1,0:T(8,128)S(1)}, u32[]{:S(2)}, u32[]{:S(2)}) collective-permute-start(f32[288,128]{1,0:T(8,128)S(1)} %get-tuple-element.19), channel_id=1, source_target_pairs={{0,1},{1,2},{2,3},{3,0},{4,5},{5,6},{6,7},{7,4},{8,9},{9,10},{10,1... | collective-permute-start | bytes 442376 | tf_op jit(solution)/shard_map/ppermute | solution.py:20
  41.7 11.0 %collective-permute-start.8 = (f32[288,128]{1,0:T(8,128)S(1)}, f32[288,128]{1,0:T(8,128)S(1)}, u32[]{:S(2)}, u32[]{:S(2)}) collective-permute-start(f32[288,128]{1,0:T(8,128)S(1)} %get-tuple-element.20), channel_id=1, source_target_pairs={{0,3},{1,0},{2,1},{3,2},{4,7},{5,4},{6,5},{7,6},{8,11},{9,8},{10,9... | collective-permute-start | bytes 442376 | tf_op jit(solution)/shard_map/ppermute | solution.py:20

commit v8 on v7

--- a/solution.py
+++ b/solution.py
@@ -387,6 +387,19 @@
     def row(layer, at):
         return in_ref[pl.ds(layer * p.back_rows + at, tiles, stride=pitch), :]
 
+    def mix(own):
+        x = x_ref[own]
+        weights = weights_ref[own]
+        scale = 0.4 / jnp.sum(weights, axis=-1, keepdims=True)
+        x_high = x.astype(jnp.bfloat16)
+        x_low = (x - x_high.astype(jnp.float32)).astype(jnp.bfloat16)
+        w_high = weights.astype(jnp.bfloat16)
+        w_low = (weights - w_high.astype(jnp.float32)).astype(jnp.bfloat16)
+        dot = functools.partial(jnp.dot, preferred_element_type=jnp.float32)
+        both = dot(w_high, jnp.concatenate([x_high, x_low], axis=1))
+        total = both[:, :LANES] + (both[:, LANES:] + dot(w_low, x_high))
+        all_ref[pl.ds(own, p.all_levels, stride=p.own_cells), :] = 0.6 * x + scale * total
+
     for r in range(p.back_part):
         turned = []
         for layer in range(p.layers):
@@ -410,18 +423,7 @@
                 for h in range(p.spare):
                     at = base + p.full * tiles + h
                     x_ref[own, at : at + 1, :] = tail[h * p.groups : h * p.groups + 1]
-    for own in range(p.own_cells):
-        x = x_ref[own]
-        weights = weights_ref[own]
-        scale = 0.4 / jnp.sum(weights, axis=-1, keepdims=True)
-        x_high = x.astype(jnp.bfloat16)
-        x_low = (x - x_high.astype(jnp.float32)).astype(jnp.bfloat16)
-        w_high = weights.astype(jnp.bfloat16)
-        w_low = (weights - w_high.astype(jnp.float32)).astype(jnp.bfloat16)
-        dot = functools.partial(jnp.dot, preferred_element_type=jnp.float32)
-        both = dot(w_high, jnp.concatenate([x_high, x_low], axis=1))
-        total = both[:, :LANES] + (both[:, LANES:] + dot(w_low, x_high))
-        all_ref[pl.ds(own, p.all_levels, stride=p.own_cells), :] = 0.6 * x + scale * total
+            mix(own)
     me = lax.axis_index("lev")
     size = p.levels * p.own_cells
     for s in range(p.layers):

time: 53.9 us -> 53.9 us (level)
  no operation moved by 1% of the time
where the time goes in v8:
time: 53.9 us; the launch traced here: 53.4 us
  blocking collectives  19.9 us (37%)
  starting transfers between devices  14 us (26%)
  waiting for transfers between devices  12.7 us (24%)
  Pallas kernels  6.66 us (12%)
    all_to_all x1, blocking collectives, by_levels(): lax.all_to_all(moved, ('tile', 'lev'), split_axis=0, concat_axis=0, tiled...  19.9 us
    ppermute x7, starting transfers between devices, swapped(): return lax.ppermute(value, axis, pairs)  8.23 us
    ppermute x3, waiting for transfers between devices, passed_along(): return lax.ppermute(value, axis, pairs)  7.98 us
    ppermute x3, starting transfers between devices, passed_along(): return lax.ppermute(value, axis, pairs)  5.81 us
    ppermute x7, waiting for transfers between devices, swapped(): return lax.ppermute(value, axis, pairs)  4.72 us
    pallas_call x1, Pallas kernels, by_levels(): pl.pallas_call(functools.partial(advect_kernel, p, tile_stride(p.tiles)),...  3.2 us
    pallas_call x2, Pallas kernels, by_levels(): pl.pallas_call(functools.partial(place_kernel, p, shifts), out_shape=jax....  1.48 us
    pallas_call x1, Pallas kernels, by_levels(): pl.pallas_call(functools.partial(pack_kernel, p), out_shape=[jax.ShapeDty...  1.24 us
  transfers between devices with their start and end apart: 10, of which 6 were waited for; matrix products, arithmetic and copies ran while one was open for 0% of the time, Pallas kernels for 1%

profile of v8, /device:TPU:0, one launch (start us, length us, event | category | flops | bytes accessed | tf_op | source)
XLA Modules:
  0.0 53.4 jit_solution(5156757593615112856)
XLA Ops:
  0.0 1.2 %pack.1 = (f32[19,8,128]{2,1,0:T(8,128)S(1)}, f32[19,8,128]{2,1,0:T(8,128)S(1)}, f32[19,8,128]{2,1,0:T(8,128)S(1)}, f32[19,8,128]{2,1,0:T(8,128)S(1)}, f32[4,19,8,128]{3,2,1,0:T(8,128)S(1)}) custom-call(f32[8,18,8,128]{3,2,1,0:T(8,128)} %bitcast.26, f32[8,8,18]{2,1,0:T(8,128)} %bitcast.27, f32[8,8,18]{2,1,0:T(8,128)} %bitcast.28, s32[1,2]{1,0:T(1,128)} %flip_ref.1), custom_call_target="tpu_custom_call" | custom-call | tf_op jit(solution)/shard_map/pack/pallas_call | solution.py:466
  1.3 0.5 collective-permute-start
  1.8 2.6 %collective-permute-start.1 = (f32[152,128]{1,0:T(8,128)S(1)}, f32[152,128]{1,0:T(8,128)S(1)}, u32[]{:S(2)}, u32[]{:S(2)}) collective-permute-start(f32[152,128]{1,0:T(8,128)S(1)} %bitcast.25), channel_id=1, source_target_pairs={{0,8},{4,12},{8,0},{12,4},{16,24},{20,28},{24,16},{28,20},{1,9},{5... | collective-permute-start | bytes 233480 | tf_op jit(solution)/shard_map/ppermute | solution.py:75
  4.3 1.5 %collective-permute-start.3 = (f32[152,128]{1,0:T(8,128)S(1)}, f32[152,128]{1,0:T(8,128)S(1)}, u32[]{:S(2)}, u32[]{:S(2)}) collective-permute-start(f32[152,128]{1,0:T(8,128)S(1)} %bitcast.24), channel_id=1, source_target_pairs={{0,16},{4,20},{8,24},{12,28},{16,0},{20,4},{24,8},{28,12},{1,17},{... | collective-permute-start | bytes 233480 | tf_op jit(solution)/shard_map/ppermute | solution.py:75
  5.9 0.0 collective-permute-start.5
  5.9 0.0 collective-permute-done
  5.9 3.0 %collective-permute-start.6 = (f32[152,128]{1,0:T(8,128)S(1)}, f32[152,128]{1,0:T(8,128)S(1)}, u32[]{:S(2)}, u32[]{:S(2)}) collective-permute-start(f32[152,128]{1,0:T(8,128)S(1)} %get-tuple-element.23), channel_id=1, source_target_pairs={{0,24},{4,28},{8,16},{12,20},{16,8},{20,12},{24,0},{28,4},{1,25},{... | collective-permute-start | bytes 233480 | tf_op jit(solution)/shard_map/ppermute | solution.py:75
  8.9 0.5 collective-permute-start.4
  9.4 0.0 collective-permute-done.1.refs_2_
  9.4 0.1 collective-permute-start.2
  9.5 1.0 %collective-permute-done.3.refs_4_ = f32[152,128]{1,0:T(8,128)S(1)} collective-permute-done((f32[152,128]{1,0:T(8,128)S(1)}, f32[152,128]{1,0:T(8,128)S(1)}, u32[]{:S(2)}, u32[]{:S(2)}) %collective-permute-start.3) | collective-permute-done | bytes 77856 | tf_op jit(solution)/shard_map/ppermute | solution.py:75
  10.5 1.3 %collective-permute-done.5.refs_6_ = f32[152,128]{1,0:T(8,128)S(1)} collective-permute-done((f32[152,128]{1,0:T(8,128)S(1)}, f32[152,128]{1,0:T(8,128)S(1)}, u32[]{:S(2)}, u32[]{:S(2)}) %collective-permute-start.5) | collective-permute-done | bytes 77856 | tf_op jit(solution)/shard_map/ppermute | solution.py:75
  11.8 1.3 %collective-permute-done.6.refs_7_ = f32[152,128]{1,0:T(8,128)S(1)} collective-permute-done((f32[152,128]{1,0:T(8,128)S(1)}, f32[152,128]{1,0:T(8,128)S(1)}, u32[]{:S(2)}, u32[]{:S(2)}) %collective-permute-start.6) | collective-permute-done | bytes 77856 | tf_op jit(solution)/shard_map/ppermute | solution.py:75
  13.1 1.1 %collective-permute-done.4.refs_5_ = f32[152,128]{1,0:T(8,128)S(1)} collective-permute-done((f32[152,128]{1,0:T(8,128)S(1)}, f32[152,128]{1,0:T(8,128)S(1)}, u32[]{:S(2)}, u32[]{:S(2)}) %collective-permute-start.4) | collective-permute-done | bytes 77856 | tf_op jit(solution)/shard_map/ppermute | solution.py:75
  14.2 0.0 collective-permute-done.2.refs_3_
  14.2 3.2 %advect.1 = f32[32,9,4,128]{3,2,1,0:T(4,128)S(1)} custom-call(f32[152,128]{1,0:T(8,128)S(1)} %bitcast.22, f32[152,128]{1,0:T(8,128)S(1)} %get-tuple-element.26.refs_1_, f32[152,128]{1,0:T(8,128)S(1)} %collective-permute-done.1.refs_2_, f32[152,128]{1,0:T(8,128)S(1)} %collective-permute-done.2.refs_3_, f32[152,128]{1,0:T(8,128)S(1)} %collective-permute-done.3.refs_4_, ...), custom_call_target="tpu_custom_call" | custom-call | tf_op jit(solution)/shard_map/advect/pallas_call | solution.py:499
  17.5 0.0 copy-start
  17.5 19.9 %all_to_all.5.in_ref = f32[32,9,4,128]{3,2,1,0:T(4,128)S(1)} all-to-all(f32[32,9,4,128]{3,2,1,0:T(4,128)S(1)} %advect.1), channel_id=1, replica_groups=mesh['tile'=8,'lev'=4] {'tile','lev'}, dimensions={0} | all-to-all | bytes 1179648 | tf_op jit(solution)/shard_map/all_to_all | solution.py:514
  37.4 0.0 copy-done
  37.4 0.7 %mix.1 = (f32[288,128]{1,0:T(8,128)S(1)}, f32[288,128]{1,0:T(8,128)S(1)}, f32[288,128]{1,0:T(8,128)S(1)}, f32[288,128]{1,0:T(8,128)S(1)}) custom-call(f32[32,9,4,128]{3,2,1,0:T(4,128)S(1)} %all_to_all.5.in_ref, f32[16,72,72]{2,1,0:T(8,128)S(1)} %bitcast.21), custom_call_target="tpu_custom_call" | custom-call | tf_op jit(solution)/shard_map/mix/pallas_call | solution.py:522
  38.1 2.0 %collective-permute-start.9 = (f32[288,128]{1,0:T(8,128)S(1)}, f32[288,128]{1,0:T(8,128)S(1)}, u32[]{:S(2)}, u32[]{:S(2)}) collective-permute-start(f32[288,128]{1,0:T(8,128)S(1)} %get-tuple-element.22), channel_id=1, source_target_pairs={{0,2},{1,3},{2,0},{3,1},{4,6},{5,7},{6,4},{7,5},{8,10},{9,11},{10,... | collective-permute-start | bytes 442376 | tf_op jit(solution)/shard_map/ppermute | solution.py:20
  40.1 1.6 %collective-permute-start.7 = (f32[288,128]{1,0:T(8,128)S(1)}, f32[288,128]{1,0:T(8,128)S(1)}, u32[]{:S(2)}, u32[]{:S(2)}) collective-permute-start(f32[288,128]{1,0:T(8,128)S(1)} %get-tuple-element.19), channel_id=1, source_target_pairs={{0,1},{1,2},{2,3},{3,0},{4,5},{5,6},{6,7},{7,4},{8,9},{9,10},{10,1... | collective-permute-start | bytes 442376 | tf_op jit(solution)/shard_map/ppermute | solution.py:20
  41.7 2.3 %collective-permute-start.8 = (f32[288,128]{1,0:T(8,128)S(1)}, f32[288,128]{1,0:T(8,128)S(1)}, u32[]{:S(2)}, u32[]{:S(2)}) collective-permute-start(f32[288,128]{1,0:T(8,128)S(1)} %get-tuple-element.20), channel_id=1, source_target_pairs={{0,3},{1,0},{2,1},{3,2},{4,7},{5,4},{6,5},{7,6},{8,11},{9,8},{10,9... | collective-permute-start | bytes 442376 | tf_op jit(solution)/shard_map/ppermute | solution.py:20
  43.9 7.9 %collective-permute-done.9.refs_1_ = f32[288,128]{1,0:T(8,128)S(1)} collective-permute-done((f32[288,128]{1,0:T(8,128)S(1)}, f32[288,128]{1,0:T(8,128)S(1)}, u32[]{:S(2)}, u32[]{:S(2)}) %collective-permute-start.9) | collective-permute-done | bytes 147488 | tf_op jit(solution)/shard_map/ppermute | solution.py:20
  51.8 0.7 %place.2.refs_2_ = f32[8,18,8,128]{3,2,1,0:T(8,128)} custom-call(f32[288,128]{1,0:T(8,128)S(1)} %get-tuple-element.21.refs_0_, f32[288,128]{1,0:T(8,128)S(1)} %collective-permute-done.9.refs_1_), custom_call_target="tpu_custom_call" | custom-call | tf_op jit(solution)/shard_map/place/pallas_call | solution.py:542
  52.6 0.0 collective-permute-done.7.refs_0_
  52.6 0.1 collective-permute-done.8.refs_1_
  52.7 0.7 %place.3 = f32[8,18,8,128]{3,2,1,0:T(8,128)} custom-call(f32[288,128]{1,0:T(8,128)S(1)} %collective-permute-done.7.refs_0_, f32[288,128]{1,0:T(8,128)S(1)} %collective-permute-done.8.refs_1_, f32[8,18,8,128]{3,2,1,0:T(8,128)} %place.2.refs_2_), custom_call_target="tpu_custom_call", output_to_operand_aliasing={{}: (2, {})} | custom-call | tf_op jit(solution)/shard_map/place/pallas_call | solution.py:542
  (1 shorter events, 0.0 us)
Async XLA Ops:
  1.3 4.6 %collective-permute-start = (f32[4,19,8,128]{3,2,1,0:T(8,128)S(1)}, f32[4,19,8,128]{3,2,1,0:T(8,128)S(1)}, u32[]{:S(2)}, u32[]{:S(2)}) collective-permute-start(f32[4,19,8,128]{3,2,1,0:T(8,128)S(1)} %get-tuple-element.15), channel_id=1, source_target_pairs={{0,4},{4,0},{8,12},{12,8},{16,20},{20,16},{24,28},{28,24},{1,5},{5... | collective-permute-start | bytes 933896 | tf_op jit(solution)/shard_map/ppermute | solution.py:75
  1.8 7.6 %collective-permute-start.1 = (f32[152,128]{1,0:T(8,128)S(1)}, f32[152,128]{1,0:T(8,128)S(1)}, u32[]{:S(2)}, u32[]{:S(2)}) collective-permute-start(f32[152,128]{1,0:T(8,128)S(1)} %bitcast.25), channel_id=1, source_target_pairs={{0,8},{4,12},{8,0},{12,4},{16,24},{20,28},{24,16},{28,20},{1,9},{5... | collective-permute-start | bytes 233480 | tf_op jit(solution)/shard_map/ppermute | solution.py:75
  4.3 6.2 %collective-permute-start.3 = (f32[152,128]{1,0:T(8,128)S(1)}, f32[152,128]{1,0:T(8,128)S(1)}, u32[]{:S(2)}, u32[]{:S(2)}) collective-permute-start(f32[152,128]{1,0:T(8,128)S(1)} %bitcast.24), channel_id=1, source_target_pairs={{0,16},{4,20},{8,24},{12,28},{16,0},{20,4},{24,8},{28,12},{1,17},{... | collective-permute-start | bytes 233480 | tf_op jit(solution)/shard_map/ppermute | solution.py:75
  5.9 6.0 %collective-permute-start.5 = (f32[152,128]{1,0:T(8,128)S(1)}, f32[152,128]{1,0:T(8,128)S(1)}, u32[]{:S(2)}, u32[]{:S(2)}) collective-permute-start(f32[152,128]{1,0:T(8,128)S(1)} %bitcast.23), channel_id=1, source_target_pairs={{0,24},{4,28},{8,16},{12,20},{16,8},{20,12},{24,0},{28,4},{1,25},{... | collective-permute-start | bytes 233480 | tf_op jit(solution)/shard_map/ppermute | solution.py:75
  5.9 7.2 %collective-permute-start.6 = (f32[152,128]{1,0:T(8,128)S(1)}, f32[152,128]{1,0:T(8,128)S(1)}, u32[]{:S(2)}, u32[]{:S(2)}) collective-permute-start(f32[152,128]{1,0:T(8,128)S(1)} %get-tuple-element.23), channel_id=1, source_target_pairs={{0,24},{4,28},{8,16},{12,20},{16,8},{20,12},{24,0},{28,4},{1,25},{... | collective-permute-start | bytes 233480 | tf_op jit(solution)/shard_map/ppermute | solution.py:75
  8.9 5.4 %collective-permute-start.4 = (f32[152,128]{1,0:T(8,128)S(1)}, f32[152,128]{1,0:T(8,128)S(1)}, u32[]{:S(2)}, u32[]{:S(2)}) collective-permute-start(f32[152,128]{1,0:T(8,128)S(1)} %get-tuple-element.24), channel_id=1, source_target_pairs={{0,16},{4,20},{8,24},{12,28},{16,0},{20,4},{24,8},{28,12},{1,17},{... | collective-permute-start | bytes 233480 | tf_op jit(solution)/shard_map/ppermute | solution.py:75
  9.4 4.9 %collective-permute-start.2 = (f32[152,128]{1,0:T(8,128)S(1)}, f32[152,128]{1,0:T(8,128)S(1)}, u32[]{:S(2)}, u32[]{:S(2)}) collective-permute-start(f32[152,128]{1,0:T(8,128)S(1)} %get-tuple-element.25), channel_id=1, source_target_pairs={{0,8},{4,12},{8,0},{12,4},{16,24},{20,28},{24,16},{28,20},{1,9},{5... | collective-permute-start | bytes 233480 | tf_op jit(solution)/shard_map/ppermute | solution.py:75
  17.5 19.9 %copy-start = (f32[1,2,8,72,72]{4,3,2,1,0:T(8,128)S(1)}, f32[1,2,8,72,72]{4,3,2,1,0:T(8,128)}, u32[]{:S(2)}) copy-start(f32[1,2,8,72,72]{4,3,2,1,0:T(8,128)} %param.8) | copy-start | bytes 995332
  38.1 13.7 %collective-permute-start.9 = (f32[288,128]{1,0:T(8,128)S(1)}, f32[288,128]{1,0:T(8,128)S(1)}, u32[]{:S(2)}, u32[]{:S(2)}) collective-permute-start(f32[288,128]{1,0:T(8,128)S(1)} %get-tuple-element.22), channel_id=1, source_target_pairs={{0,2},{1,3},{2,0},{3,1},{4,6},{5,7},{6,4},{7,5},{8,10},{9,11},{10,... | collective-permute-start | bytes 442376 | tf_op jit(solution)/shard_map/ppermute | solution.py:20
  40.1 12.5 %collective-permute-start.7 = (f32[288,128]{1,0:T(8,128)S(1)}, f32[288,128]{1,0:T(8,128)S(1)}, u32[]{:S(2)}, u32[]{:S(2)}) collective-permute-start(f32[288,128]{1,0:T(8,128)S(1)} %get-tuple-element.19), channel_id=1, source_target_pairs={{0,1},{1,2},{2,3},{3,0},{4,5},{5,6},{6,7},{7,4},{8,9},{9,10},{10,1... | collective-permute-start | bytes 442376 | tf_op jit(solution)/shard_map/ppermute | solution.py:20
  41.7 11.0 %collective-permute-start.8 = (f32[288,128]{1,0:T(8,128)S(1)}, f32[288,128]{1,0:T(8,128)S(1)}, u32[]{:S(2)}, u32[]{:S(2)}) collective-permute-start(f32[288,128]{1,0:T(8,128)S(1)} %get-tuple-element.20), channel_id=1, source_target_pairs={{0,3},{1,0},{2,1},{3,2},{4,7},{5,4},{6,5},{7,6},{8,11},{9,8},{10,9... | collective-permute-start | bytes 442376 | tf_op jit(solution)/shard_map/ppermute | solution.py:20
